TPU v7x, 32 devices: a whole 2x2x4 slice. The times are simulated.
32 devices in a mesh: sub: 8 (over z, core), tile: 4 (over y, x).
Axes of the slice: x: 2, y: 2, z: 4, core: 2. Of those that a mesh axis runs over, the one named last changes fastest.
Arguments:
- load_current: float32 [8, 2, 256, 4096], P('sub', None, 'tile'), may hold values from -6 to 6
- diagonal: float32 [8, 2, 256, 4096], P('sub', None, 'tile')
- start_field: float32 [8, 2, 256, 4096], P('sub', None, 'tile'), may hold values from -4 to 4
- block_inverse: float32 [8, 16, 2, 256, 2, 256], P('sub')
- multipliers: float32 [8, 2, 256, 128], P('sub', None, 'tile'), may hold values from -6 to 6
- active_rows: int32 [8], replicated, may hold values from 64 to 256, as said below
- contact_peer: int32 [8, 8], replicated, may hold values from 0 to 7, as said below
- contact_len: int32 [8, 8], replicated, may hold values from 1 to 128, 256 in all within a row
- port_row: int32 [8, 16], P('sub'), may hold values from 0 to 255
- port_col: int32 [8, 16], P('sub'), may hold values from 0 to 3968
- port_current: float32 [8, 2, 16], P('sub'), may hold values from -16 to 16
Outputs:
- solution: float32 [8, 2, 256, 4096], P('sub', None, 'tile')
- next_multipliers: float32 [8, 2, 256, 128], P('sub', None, 'tile')
Inputs may be any that keep to these rules, and one draw needn't show every extreme that they name: `active_rows`: at least one subdomain has all 256 lines active. `contact_peer`: a contact never names its own subdomain.
All inputs are finite; a program needn't handle non-finite values.
Results may differ from a plain program's by a relative error of at most 0.0003.
Values sent between devices are 32-bit elements; how exact they have to be, the bound alone decides.
No kernel may reach another device: no remote copies, remote signals or barrier semaphores. Data moves between devices by JAX's collectives and lax.ppermute only.
A program may use at most 128 MiB of HBM per device.

v0:
```python
import functools

import jax
import jax.numpy as jnp
from jax import lax
from jax.experimental import pallas as pl
from jax.experimental.pallas import tpu as pltpu
from jax.sharding import PartitionSpec as P

IB = 128
PB = 128
SWEEPS = 3
LANES = 128
PAD = 8
SLOTS = 4
MIB = 1 << 20

VMEM_SPEC = pl.BlockSpec(memory_space=pltpu.VMEM)
SMEM_SPEC = pl.BlockSpec(memory_space=pltpu.SMEM)
ANY_SPEC = pl.BlockSpec(memory_space=pl.ANY)


def call(kernel, args, specs, outs, limit, scratch=(), flops=0, moved=0):
    return pl.pallas_call(
        kernel,
        out_shape=outs,
        in_specs=specs,
        out_specs=jax.tree.map(lambda _: VMEM_SPEC, outs),
        scratch_shapes=scratch,
        compiler_params=pltpu.CompilerParams(vmem_limit_bytes=limit),
        cost_estimate=pl.CostEstimate(flops=flops, bytes_accessed=moved, transcendentals=0),
    )(*args)


def held(shape, dtype=jnp.float32):
    return pltpu.VMEM(shape, dtype)


def line_peers(peer_ref, len_ref, s, lines):
    found = jnp.zeros(lines.shape, jnp.int32)
    start = jnp.int32(0)
    for c in range(peer_ref.shape[1]):
        end = start + len_ref[s, c]
        found = jnp.where((lines >= start) & (lines < end), peer_ref[s, c], found)
        start = end
    return found


def pick(hit, cells):
    return jnp.where(hit[None], cells, 0.0)


def split_halves(x):
    high = x.astype(jnp.bfloat16)
    return high, (x - high.astype(jnp.float32)).astype(jnp.bfloat16)


def weights_kernel(size, b_ref, hi_ref, lo_ref, buf, sem):
    nb = b_ref.shape[0]
    both = 2 * size
    parts = both // LANES

    def copy(k):
        return pltpu.make_async_copy(b_ref.at[k], buf.at[k % SLOTS], sem.at[k % SLOTS])

    for k in range(min(SLOTS - 1, nb)):
        copy(k).start()
    for k in range(nb):
        if k + SLOTS - 1 < nb:
            copy(k + SLOTS - 1).start()
        copy(k).wait()
        for q in range(parts):
            piece, comp = divmod(q, 2)
            rows = pl.ds(comp * size + piece * LANES, LANES)
            high, low = split_halves(buf[k % SLOTS, pl.ds(q, both, parts), :].T)
            hi_ref[k, rows, :] = high
            lo_ref[k, rows, :] = low


def split_weights(blocks):
    nb, _, size, _, _ = blocks.shape
    both = 2 * size
    parts = both // LANES
    flat = blocks.reshape(nb, 2, size, 2, size // LANES, LANES).transpose(0, 1, 2, 4, 3, 5)
    flat = flat.reshape(nb, both * parts, LANES)
    shape = (nb, both, both)
    return call(
        functools.partial(weights_kernel, size),
        (flat,),
        [ANY_SPEC],
        [held(shape, jnp.bfloat16)] * 2,
        10 * MIB,
        [pltpu.VMEM((SLOTS, both * parts, LANES), jnp.float32), pltpu.SemaphoreType.DMA((SLOTS,))],
        moved=nb * both * both * 8,
    )


def edges_kernel(start_ref, load_ref, diag_ref, one_ref, two_ref):
    rows = start_ref.shape[1]
    even = lax.rem(lax.axis_index("tile"), 2) == 0
    top, bottom = pl.ds(0, PAD), pl.ds(rows - PAD, PAD)
    row = lax.broadcasted_iota(jnp.int32, (PAD, start_ref.shape[2]), 0)
    for c in range(2):
        first = jnp.where(
            row < 3,
            start_ref[c, top, :],
            jnp.where(
                row < 5, pltpu.roll(load_ref[c, top, :], 3, 0), pltpu.roll(diag_ref[c, top, :], 5, 0)
            ),
        )
        last = jnp.where(
            row < 3,
            pltpu.roll(start_ref[c, bottom, :], 3, 0),
            jnp.where(
                row < 5,
                pltpu.roll(load_ref[c, bottom, :], 5, 0),
                pltpu.roll(diag_ref[c, bottom, :], 7, 0),
            ),
        )
        one_ref[c] = jnp.where(even, last, first)
        two_ref[c] = jnp.where(even, first, last)


def swaps(count):
    one = [(i, i ^ 1) for i in range(count)]
    two = [(i, ((i - 1) if i % 2 == 0 else (i + 1)) % count) for i in range(count)]
    return one, two


def swap_edges(one, two):
    first, second = swaps(lax.axis_size("tile"))
    return lax.ppermute(one, "tile", first), lax.ppermute(two, "tile", second)


def to_subs_kernel(tail, far, own_ref, other_ref, peer_ref, len_ref, *outs):
    count = peer_ref.shape[0]
    me = lax.axis_index("sub")
    partner = me + 1 - 2 * lax.rem(me, 2)
    shape = own_ref.shape[1:]
    rows = shape[0] - tail
    at = lax.broadcasted_iota(jnp.int32, shape, 0)
    at = jnp.where(at < rows + tail // 2, at, at - rows - tail)
    lines = at + lax.axis_index("tile") * rows
    own, other = own_ref[...], other_ref[...]
    if far:
        outs[-1][...] = pick(line_peers(peer_ref, len_ref, me, lines) == partner, other)
    else:
        of_own = line_peers(peer_ref, len_ref, me, lines)
        of_other = line_peers(peer_ref, len_ref, partner, lines)
        outs[-1][...] = pick(of_other == me, other)
    for step in range(1, count // 2):
        to = lax.rem(me + 2 * step, count)
        if far:
            wanted = line_peers(peer_ref, len_ref, to, lines)
            sent = pick(wanted == me, own) + pick(wanted == partner, other)
        else:
            sent = pick(of_own == to, own) + pick(of_other == to, other)
        outs[step - 1][...] = sent


def to_subs(cells, contact_peer, contact_len, tail, far):
    count = lax.axis_size("sub")
    other = lax.ppermute(cells, "sub", [(i, i ^ 1) for i in range(count)])
    outs = call(
        functools.partial(to_subs_kernel, tail, far),
        (cells, other, contact_peer, contact_len),
        [VMEM_SPEC, VMEM_SPEC, SMEM_SPEC, SMEM_SPEC],
        [held(cells.shape)] * (count // 2),
        4 * MIB,
    )
    got = [
        lax.ppermute(outs[step - 1], "sub", [(i, (i + 2 * step) % count) for i in range(count)])
        for step in range(1, count // 2)
    ]
    return got + [outs[-1]]


def line_mask(active_ref, shape, rows):
    at = lax.broadcasted_iota(jnp.int32, shape, 0) - PAD + lax.axis_index("tile") * rows
    return (at >= 0) & (at < active_ref[lax.axis_index("sub")])


def tiles_of(parts, c, k, size, last):
    def ref_of(b):
        for first, ref in parts:
            if first <= b < first + ref.shape[2] // size:
                return ref, (b - first) * size

    ref, at = ref_of(k)
    mid = ref[c, :, at : at + size]
    none = jnp.zeros((mid.shape[0], LANES), jnp.float32)
    left, right = none, none
    if k > 0:
        ref, at = ref_of(k - 1)
        left = ref[c, :, at + size - LANES : at + size]
    if k < last:
        ref, at = ref_of(k + 1)
        right = ref[c, :, at : at + LANES]
    return mid, jnp.concatenate([left, mid, right], axis=1)


def relax_block(parts, source, diag_ref, hi_ref, lo_ref, k, mask):
    size = hi_ref.shape[1] // 2
    last = hi_ref.shape[0] - 1
    mids, sums = [], []
    for c in range(2):
        mid, wide = tiles_of(parts, c, k, size, last)
        rows, width = wide.shape
        beside = (
            pltpu.roll(wide, 1, 1)[:, LANES : LANES + size]
            + pltpu.roll(wide, width - 1, 1)[:, LANES : LANES + size]
        )
        beside = beside + (pltpu.roll(mid, 1, 0) + pltpu.roll(mid, rows - 1, 0))
        mids.append(mid)
        sums.append(source(c) + beside)
    cols = slice(k * size, (k + 1) * size)
    d0, d1 = diag_ref[0, :, cols], diag_ref[1, :, cols]
    r0 = sums[0] - (d0 * mids[0] - d1 * mids[1])
    r1 = sums[1] - (d0 * mids[1] + d1 * mids[0])
    high, low = split_halves(jnp.concatenate([r0, r1], axis=1))
    rows = high.shape[0]
    z = jnp.dot(
        jnp.concatenate([high, low], axis=0), hi_ref[k], preferred_element_type=jnp.float32
    )
    z = (z[:rows] + z[rows:]) + jnp.dot(high, lo_ref[k], preferred_element_type=jnp.float32)
    return [
        jnp.where(mask, mids[c] + z[:, c * size : (c + 1) * size], 0.0) for c in range(2)
    ]


def stored_source(source_ref, k, size):
    return lambda c: source_ref[c, :, k * size : (k + 1) * size]


def first_kernel(
    upto, start_ref, load_ref, diag_ref, one_ref, two_ref, mult_ref, hi_ref, lo_ref,
    active_ref, prow_ref, pcol_ref, pcur_ref, src_ref, dg_ref, f1_ref, f0_ref,
):
    _, rows, width = load_ref.shape
    size = hi_ref.shape[1] // 2
    own = slice(PAD, PAD + rows)
    above, below = slice(0, PAD), slice(PAD + rows, 2 * PAD + rows)
    tile = lax.axis_index("tile")
    even = lax.rem(tile, 2) == 0
    active = active_ref[lax.axis_index("sub")]

    def masked(cells, first):
        line = lax.broadcasted_iota(jnp.int32, cells.shape, 0) + (first + tile * rows)
        return jnp.where((line >= 0) & (line < active), cells, 0.0)

    for c in range(2):
        one, two = one_ref[c], two_ref[c]
        up = jnp.where(even, two, one)
        down = jnp.where(even, one, two)
        f0_ref[c, own, :] = masked(start_ref[c], 0)
        f0_ref[c, above, :] = masked(pltpu.roll(up, 5, 0), -PAD)
        f0_ref[c, below, :] = masked(down, rows)
        src_ref[c, own, :] = load_ref[c]
        src_ref[c, above, :] = pltpu.roll(up, 3, 0)
        src_ref[c, below, :] = pltpu.roll(down, 5, 0)
        dg_ref[c, own, :] = diag_ref[c]
        dg_ref[c, above, :] = pltpu.roll(up, 1, 0)
        dg_ref[c, below, :] = pltpu.roll(down, 3, 0)
        src_ref[c, own, 0:IB] -= mult_ref[c, 0:rows, :]
        src_ref[c, above, 0:IB] -= mult_ref[c, rows:, :]
        src_ref[c, below, 0:IB] -= mult_ref[c, rows:, :]
    span = PB + LANES
    at_row = lax.broadcasted_iota(jnp.int32, (PAD, span), 0)
    at_col = lax.broadcasted_iota(jnp.int32, (PAD, span), 1)
    for p in range(prow_ref.shape[1]):
        row = prow_ref[0, p] - tile * rows + PAD
        col = pcol_ref[0, p]
        base = pl.multiple_of(jnp.minimum(col // LANES * LANES, width - span), LANES)

        @pl.when((row >= 0) & (row < rows + 2 * PAD))
        def _(p=p, row=row, col=col, base=base):
            first = pl.multiple_of(row // PAD * PAD, PAD)
            hit = (at_row == row - first) & (at_col >= col - base) & (at_col < col - base + PB)
            for c in range(2):
                where = (c, pl.ds(first, PAD), pl.ds(base, span))
                src_ref[where] = src_ref[where] + jnp.where(hit, pcur_ref[0, c, p], 0.0)

    mask = line_mask(active_ref, (rows + 2 * PAD, size), rows)
    for k in range(upto):
        new = relax_block(
            [(0, f0_ref)], stored_source(src_ref, k, size), dg_ref, hi_ref, lo_ref, k, mask
        )
        for c in range(2):
            f1_ref[c, :, k * size : (k + 1) * size] = new[c]


def far_kernel(
    count, f0_ref, f1_ref, src_ref, dg_ref, hi_ref, lo_ref, active_ref, *refs
):
    pieces, (f1e_ref, f2e_ref, f3e_ref, far_ref) = refs[:count], refs[count:]
    last = hi_ref.shape[0] - 1
    size = hi_ref.shape[1] // 2
    rows = far_ref.shape[1]
    mask = line_mask(active_ref, (rows + 2 * PAD, size), rows)
    into = []
    for c in range(2):
        piece = pieces[0][c]
        for other in pieces[1:]:
            piece = piece + other[c]
        edge = piece[rows:]
        ends = jnp.concatenate([edge, piece[:rows], edge], axis=0)
        into.append(jnp.concatenate([jnp.zeros((rows + 2 * PAD, size - IB), jnp.float32), ends], axis=1))
    end = stored_source(src_ref, last, size)

    def with_incoming(c):
        return end(c) + into[c]

    new = relax_block([(0, f0_ref)], with_incoming, dg_ref, hi_ref, lo_ref, last, mask)
    for c in range(2):
        f1e_ref[c] = new[c]
    f1 = [(last, f1e_ref), (0, f1_ref)]
    for k, source in ((last, with_incoming), (last - 1, stored_source(src_ref, last - 1, size))):
        new = relax_block(f1, source, dg_ref, hi_ref, lo_ref, k, mask)
        for c in range(2):
            f2e_ref[c, :, (k - last + 1) * size : (k - last + 2) * size] = new[c]
    new = relax_block([(last - 1, f2e_ref)], with_incoming, dg_ref, hi_ref, lo_ref, last, mask)
    for c in range(2):
        f3e_ref[c] = new[c][PAD : PAD + rows]
        far_ref[c] = new[c][PAD : PAD + rows, size - IB :]


def middle_kernel(f1_ref, src_ref, dg_ref, hi_ref, lo_ref, active_ref, f2_ref):
    size = hi_ref.shape[1] // 2
    mask = line_mask(active_ref, (f2_ref.shape[1], size), f2_ref.shape[1] - 2 * PAD)
    for k in range(f2_ref.shape[2] // size):
        new = relax_block(
            [(0, f1_ref)], stored_source(src_ref, k, size), dg_ref, hi_ref, lo_ref, k, mask
        )
        for c in range(2):
            f2_ref[c, :, k * size : (k + 1) * size] = new[c]


def last_kernel(f2_ref, f2e_ref, f3e_ref, src_ref, dg_ref, hi_ref, lo_ref, active_ref, out_ref, near_ref):
    size = hi_ref.shape[1] // 2
    last = hi_ref.shape[0] - 1
    rows = out_ref.shape[1]
    mask = line_mask(active_ref, (rows + 2 * PAD, size), rows)
    f2 = [(last - 1, f2e_ref), (0, f2_ref)]
    for k in range(last):
        new = relax_block(f2, stored_source(src_ref, k, size), dg_ref, hi_ref, lo_ref, k, mask)
        for c in range(2):
            out_ref[c, :, k * size : (k + 1) * size] = new[c][PAD : PAD + rows]
            if k == 0:
                near_ref[c] = new[c][PAD : PAD + rows, :IB]
    for c in range(2):
        out_ref[c, :, last * size :] = f3e_ref[c]


def per_device(
    load_current,
    diagonal,
    start_field,
    block_inverse,
    multipliers,
    active_rows,
    contact_peer,
    contact_len,
    port_row,
    port_col,
    port_current,
):
    load, diag, start, mult = load_current[0], diagonal[0], start_field[0], multipliers[0]
    _, rows, width = load.shape
    nb, _, size, _, _ = block_inverse.shape[1:]
    high = rows + 2 * PAD
    step = 6 * high * (2 * size) ** 2
    even = lax.axis_index("tile") % 2 == 0

    top, bottom = mult[:, :PAD], mult[:, rows - PAD :]
    one, two = swap_edges(jnp.where(even, bottom, top), jnp.where(even, top, bottom))
    up, down = jnp.where(even, two, one), jnp.where(even, one, two)
    tail = jnp.concatenate([down[:, : PAD // 2], up[:, PAD // 2 :]], axis=1)
    lines_mult = jnp.concatenate([mult, tail], axis=1)

    edge = jax.ShapeDtypeStruct((2, PAD, width), jnp.float32)
    one, two = swap_edges(
        *call(edges_kernel, (start, load, diag), [VMEM_SPEC] * 3, [edge] * 2, 16 * MIB)
    )
    incoming = to_subs(lines_mult, contact_peer, contact_len, PAD, False)
    hi, lo = split_weights(block_inverse[0])

    whole = held((2, high, width))
    src, dg, f1, f0 = call(
        functools.partial(first_kernel, nb - 1),
        (start, load, diag, one, two, lines_mult, hi, lo, active_rows, port_row, port_col, port_current),
        [VMEM_SPEC] * 8 + [SMEM_SPEC] * 4,
        [whole, whole, held((2, high, (nb - 1) * size)), whole],
        16 * MIB,
        flops=step * (nb - 1),
    )
    f1e, f2e, f3e, far = call(
        functools.partial(far_kernel, len(incoming)),
        (f0, f1, src, dg, hi, lo, active_rows, *incoming),
        [VMEM_SPEC] * 6 + [SMEM_SPEC] + [VMEM_SPEC] * len(incoming),
        [held((2, high, size)), held((2, high, 2 * size)), held((2, rows, size)), held((2, rows, IB))],
        8 * MIB,
        flops=step * 4,
    )
    ends = to_subs(far, contact_peer, contact_len, 0, True)
    f2 = call(
        middle_kernel,
        (f1, src, dg, hi, lo, active_rows),
        [VMEM_SPEC] * 5 + [SMEM_SPEC],
        held((2, high, (nb - 2) * size)),
        8 * MIB,
        flops=step * (nb - 2),
    )
    solved, near = call(
        last_kernel,
        (f2, f2e, f3e, src, dg, hi, lo, active_rows),
        [VMEM_SPEC] * 7 + [SMEM_SPEC],
        [jax.ShapeDtypeStruct((2, rows, width), jnp.float32), held((2, rows, IB))],
        8 * MIB,
        flops=step * (nb - 1),
    )
    updated = mult + (near - sum(ends))
    return (solved[None], updated[None])


def solution(mesh):
    lines = P("sub", None, "tile", None)
    in_specs = (
        lines,
        lines,
        lines,
        P("sub", None, None, None, None, None),
        lines,
        P(),
        P(),
        P(),
        P("sub", None),
        P("sub", None),
        P("sub", None, None),
    )
    return jax.shard_map(
        per_device, mesh=mesh, in_specs=in_specs, out_specs=(lines, lines), check_vma=False
    )
```

profile of v0, /device:TPU:0, one launch (start us, length us, event | category | flops | bytes accessed | tf_op | source)
XLA Modules:
  0.0 58.7 jit_solution(18271447334621989940)
XLA Ops:
  0.6 0.7 %slice_select_fusion = (f32[2,8,128]{2,1,0:T(8,128)S(1)}, f32[2,8,128]{2,1,0:T(8,128)S(1)}) fusion(f32[2,64,128]{2,1,0:T(8,128)} %bitcast.20, pred[]{:T(512)S(6)} %eq.5), kind=kLoop, calls=%fused_computation.2 | loop fusion | flops 4096 | bytes 32769 | tf_op jit(solution)/shard_map/jit(_where)/select_n | solution.py:375
  1.4 3.9 %collective-permute-start.3 = (f32[2,8,128]{2,1,0:T(8,128)S(1)}, f32[2,8,128]{2,1,0:T(8,128)S(1)}, u32[]{:S(2)}, u32[]{:S(2)}) collective-permute-start(f32[2,8,128]{2,1,0:T(8,128)S(1)} %get-tuple-element.44), channel_id=1, source_target_pairs={{0,3},{1,2},{2,1},{3,0},{4,7},{5,6},{6,5},{7,4},{8,11},{9,10},{10,... | collective-permute-start | bytes 24584 | tf_op jit(solution)/shard_map/ppermute | solution.py:132
  5.3 0.5 collective-permute-start.2
  5.8 0.0 copy-start.3
  5.8 1.6 %copy-done.3 = f32[1,2,64,4096]{3,2,1,0:T(8,128)S(1)} copy-done((f32[1,2,64,4096]{3,2,1,0:T(8,128)S(1)}, f32[1,2,64,4096]{3,2,1,0:T(8,128)}, u32[]{:S(2)}) %copy-start.3) | copy-done | bytes 2097176
  7.4 0.0 copy-start.5
  7.4 1.6 %copy-done.5 = f32[1,2,64,4096]{3,2,1,0:T(8,128)S(1)} copy-done((f32[1,2,64,4096]{3,2,1,0:T(8,128)S(1)}, f32[1,2,64,4096]{3,2,1,0:T(8,128)}, u32[]{:S(2)}) %copy-start.5) | copy-done | bytes 2097176
  9.0 0.0 copy-start.7
  9.0 1.6 %copy-done.7 = f32[1,2,64,4096]{3,2,1,0:T(8,128)S(1)} copy-done((f32[1,2,64,4096]{3,2,1,0:T(8,128)S(1)}, f32[1,2,64,4096]{3,2,1,0:T(8,128)}, u32[]{:S(2)}) %copy-start.7) | copy-done | bytes 2097176
  10.6 0.0 copy-start.15
  10.6 0.1 shard_map.122
  10.7 1.6 %collective-permute-start = (f32[2,8,4096]{2,1,0:T(8,128)S(1)}, f32[2,8,4096]{2,1,0:T(8,128)S(1)}, u32[]{:S(2)}, u32[]{:S(2)}) collective-permute-start(f32[2,8,4096]{2,1,0:T(8,128)S(1)} %get-tuple-element.23), channel_id=1, source_target_pairs={{0,1},{1,0},{2,3},{3,2},{4,5},{5,4},{6,7},{7,6},{8,9},{9,8},{10,11... | collective-permute-start | bytes 786440 | tf_op jit(solution)/shard_map/ppermute | solution.py:132
  12.2 0.0 collective-permute-start.1
  12.3 0.0 collective-permute-done.3
  12.3 0.0 collective-permute-done.2
  12.3 0.0 copy-done.15
  12.3 0.1 collective-permute-start.4
  12.4 0.0 copy-start.2
  12.4 5.8 %copy-done.2 = f32[1,16,2,256,2,256]{5,4,3,2,1,0:T(2,128)S(1)} copy-done((f32[1,16,2,256,2,256]{5,4,3,2,1,0:T(2,128)S(1)}, f32[1,16,2,256,2,256]{5,4,3,2,1,0:T(2,128)}, u32[]{:S(2)}) %copy-start.2) | copy-done | bytes 16777240
  18.1 0.0 copy-start.9
  18.2 0.0 copy-start.10
  18.2 0.0 copy-start.8
  18.2 0.0 copy-start.11
  18.2 0.0 copy-start.12
  18.2 0.0 copy-start.13
  18.2 0.0 copy-start.14
  18.2 6.6 %shard_map.123 = (bf16[16,512,512]{2,1,0:T(8,128)(2,1)S(1)}, bf16[16,512,512]{2,1,0:T(8,128)(2,1)S(1)}) custom-call(f32[16,2048,128]{2,1,0:T(8,128)S(1)} %bitcast.13), custom_call_target="tpu_custom_call" | custom-call | bytes 33554432 | tf_op jit(solution)/shard_map/pallas_call | solution.py:24
  24.9 0.0 copy-start
  24.9 0.0 collective-permute-done.4.other_ref
  24.9 0.0 copy-done.9
  24.9 0.0 copy-done.10
  24.9 0.8 %shard_map.126 = (f32[2,72,128]{2,1,0:T(8,128)S(1)}, f32[2,72,128]{2,1,0:T(8,128)S(1)}, f32[2,72,128]{2,1,0:T(8,128)S(1)}, f32[2,72,128]{2,1,0:T(8,128)S(1)}) custom-call(f32[2,72,128]{2,1,0:T(8,128)S(1)} %pad_maximum_fusion.mult_ref.own_ref, f32[2,72,128]{2,1,0:T(8,128)S(1)} %collective-permute-done.4.other_ref, s32[8,8]{1,0:T(8,128)S(1)} %copy-done.9, ...), custom_call_target="tpu_custom_call" | custom-call | tf_op jit(solution)/shard_map/pallas_call | solution.py:24
  25.7 2.1 %collective-permute-start.5 = (f32[2,72,128]{2,1,0:T(8,128)S(1)}, f32[2,72,128]{2,1,0:T(8,128)S(1)}, u32[]{:S(2)}, u32[]{:S(2)}) collective-permute-start(f32[2,72,128]{2,1,0:T(8,128)S(1)} %get-tuple-element.31), channel_id=1, source_target_pairs={{0,8},{4,12},{8,16},{12,20},{16,24},{20,28},{24,0},{28,4},{1,9},{5... | collective-permute-start | bytes 221192 | tf_op jit(solution)/shard_map/ppermute | solution.py:172
  27.8 2.6 %collective-permute-start.6 = (f32[2,72,128]{2,1,0:T(8,128)S(1)}, f32[2,72,128]{2,1,0:T(8,128)S(1)}, u32[]{:S(2)}, u32[]{:S(2)}) collective-permute-start(f32[2,72,128]{2,1,0:T(8,128)S(1)} %get-tuple-element.32), channel_id=1, source_target_pairs={{0,16},{4,20},{8,24},{12,28},{16,0},{20,4},{24,8},{28,12},{1,17},{... | collective-permute-start | bytes 221192 | tf_op jit(solution)/shard_map/ppermute | solution.py:172
  30.4 1.3 %collective-permute-start.7 = (f32[2,72,128]{2,1,0:T(8,128)S(1)}, f32[2,72,128]{2,1,0:T(8,128)S(1)}, u32[]{:S(2)}, u32[]{:S(2)}) collective-permute-start(f32[2,72,128]{2,1,0:T(8,128)S(1)} %get-tuple-element.33), channel_id=1, source_target_pairs={{0,24},{4,28},{8,0},{12,4},{16,8},{20,12},{24,16},{28,20},{1,25},{... | collective-permute-start | bytes 221192 | tf_op jit(solution)/shard_map/ppermute | solution.py:172
  31.7 0.0 collective-permute-done.one_ref
  31.7 0.0 collective-permute-done.1.two_ref
  31.7 0.0 copy-done.4
  31.7 0.0 copy-done.6
  31.8 0.0 copy-done.8
  31.8 0.0 copy-done.11
  31.8 0.0 copy-done.12
  31.8 0.0 copy-done.13
  31.8 0.0 copy-done.14
  31.8 5.5 %shard_map.124 = (f32[2,80,4096]{2,1,0:T(8,128)S(1)}, f32[2,80,4096]{2,1,0:T(8,128)S(1)}, f32[2,80,3840]{2,1,0:T(8,128)S(1)}, f32[2,80,4096]{2,1,0:T(8,128)S(1)}) custom-call(f32[2,64,4096]{2,1,0:T(8,128)S(1)} %bitcast.15, f32[2,64,4096]{2,1,0:T(8,128)S(1)} %bitcast.17, f32[2,64,4096]{2,1,0:T(8,128)S(1)} %bitcast.19, ...), custom_call_target="tpu_custom_call" | custom-call | flops 1887436800 | tf_op jit(solution)/shard_map/pallas_call | solution.py:24
  37.3 0.0 copy-done
  37.3 0.0 collective-permute-done.5.refs_0_
  37.3 0.0 collective-permute-done.6.refs_1_
  37.3 0.0 collective-permute-done.7.refs_2_
  37.3 0.0 copy-start.1
  37.4 3.4 %copy-done.1 = bf16[16,512,512]{2,1,0:T(8,128)(2,1)S(1)} copy-done((bf16[16,512,512]{2,1,0:T(8,128)(2,1)S(1)}, bf16[16,512,512]{2,1,0:T(8,128)(2,1)}, u32[]{:S(2)}) %copy-start.1) | copy-done | bytes 8388632
  40.7 2.5 %shard_map.127 = (f32[2,80,256]{2,1,0:T(8,128)}, f32[2,80,512]{2,1,0:T(8,128)S(1)}, f32[2,64,256]{2,1,0:T(8,128)S(1)}, f32[2,64,128]{2,1,0:T(8,128)S(1)}) custom-call(f32[2,80,4096]{2,1,0:T(8,128)S(1)} %get-tuple-element.30.f0_ref, f32[2,80,3840]{2,1,0:T(8,128)S(1)} %get-tuple-element.27.f1_ref, f32[2,80,4096]{2,1,0:T(8,128)S(1)} %get-tuple-element.28.src_ref, ...), custom_call_target="tpu_custom_call" | custom-call | flops 503316480 | tf_op jit(solution)/shard_map/pallas_call | solution.py:24
  43.2 0.0 collective-permute-start.8
  43.2 4.1 %shard_map.125.f2_ref = f32[2,80,3584]{2,1,0:T(8,128)S(1)} custom-call(f32[2,80,3840]{2,1,0:T(8,128)S(1)} %get-tuple-element.27.f1_ref, f32[2,80,4096]{2,1,0:T(8,128)S(1)} %get-tuple-element.28.src_ref, f32[2,80,4096]{2,1,0:T(8,128)S(1)} %get-tuple-element.29.dg_ref, bf16[16,512,512]{2,1,0:T(8,128)(2,1)S(1)} %get-tuple-element.25.hi_ref, ...), custom_call_target="tpu_custom_call" | custom-call | flops 1761607680 | tf_op jit(solution)/shard_map/pallas_call | solution.py:24
  47.4 0.0 collective-permute-done.8.other_ref
  47.4 0.9 %shard_map.129 = (f32[2,64,128]{2,1,0:T(8,128)S(1)}, f32[2,64,128]{2,1,0:T(8,128)S(1)}, f32[2,64,128]{2,1,0:T(8,128)S(1)}, f32[2,64,128]{2,1,0:T(8,128)S(1)}) custom-call(f32[2,64,128]{2,1,0:T(8,128)S(1)} %get-tuple-element.39.own_ref, f32[2,64,128]{2,1,0:T(8,128)S(1)} %collective-permute-done.8.other_ref, s32[8,8]{1,0:T(8,128)S(1)} %copy-done.9, ...), custom_call_target="tpu_custom_call" | custom-call | tf_op jit(solution)/shard_map/pallas_call | solution.py:24
  48.2 0.8 %collective-permute-start.9 = (f32[2,64,128]{2,1,0:T(8,128)S(1)}, f32[2,64,128]{2,1,0:T(8,128)S(1)}, u32[]{:S(2)}, u32[]{:S(2)}) collective-permute-start(f32[2,64,128]{2,1,0:T(8,128)S(1)} %get-tuple-element.40), channel_id=1, source_target_pairs={{0,8},{4,12},{8,16},{12,20},{16,24},{20,28},{24,0},{28,4},{1,9},{5... | collective-permute-start | bytes 196616 | tf_op jit(solution)/shard_map/ppermute | solution.py:172
  49.0 1.6 %collective-permute-start.10 = (f32[2,64,128]{2,1,0:T(8,128)S(1)}, f32[2,64,128]{2,1,0:T(8,128)S(1)}, u32[]{:S(2)}, u32[]{:S(2)}) collective-permute-start(f32[2,64,128]{2,1,0:T(8,128)S(1)} %get-tuple-element.41), channel_id=1, source_target_pairs={{0,16},{4,20},{8,24},{12,28},{16,0},{20,4},{24,8},{28,12},{1,17},{... | collective-permute-start | bytes 196616 | tf_op jit(solution)/shard_map/ppermute | solution.py:172
  50.6 1.5 %collective-permute-start.11 = (f32[2,64,128]{2,1,0:T(8,128)S(1)}, f32[2,64,128]{2,1,0:T(8,128)S(1)}, u32[]{:S(2)}, u32[]{:S(2)}) collective-permute-start(f32[2,64,128]{2,1,0:T(8,128)S(1)} %get-tuple-element.42), channel_id=1, source_target_pairs={{0,24},{4,28},{8,0},{12,4},{16,8},{20,12},{24,16},{28,20},{1,25},{... | collective-permute-start | bytes 196616 | tf_op jit(solution)/shard_map/ppermute | solution.py:172
  52.1 5.9 %shard_map.128 = (f32[2,64,4096]{2,1,0:T(8,128)}, f32[2,64,128]{2,1,0:T(8,128)S(1)}) custom-call(f32[2,80,3584]{2,1,0:T(8,128)S(1)} %shard_map.125.f2_ref, f32[2,80,512]{2,1,0:T(8,128)S(1)} %get-tuple-element.35.f2e_ref, f32[2,64,256]{2,1,0:T(8,128)S(1)} %get-tuple-element.36.f3e_ref, f32[2,80,4096]{2,1,0:T(8,128)S(1)} %get-tuple-element.28.src_ref, ...), custom_call_target="tpu_custom_call" | custom-call | flops 1887436800 | tf_op jit(solution)/shard_map/pallas_call | solution.py:24
  58.0 0.0 collective-permute-done.9
  58.0 0.0 collective-permute-done.10
  58.0 0.0 collective-permute-done.11
  58.0 0.7 %add_bitcast_fusion = f32[1,2,64,128]{3,2,1,0:T(8,128)} fusion(f32[2,64,128]{2,1,0:T(8,128)S(1)} %get-tuple-element.38, f32[2,64,128]{2,1,0:T(8,128)S(1)} %get-tuple-element.43, f32[2,64,128]{2,1,0:T(8,128)S(1)} %collective-permute-done.11, f32[2,64,128]{2,1,0:T(8,128)S(1)} %collective-permute-done.9, f32[2,64,128]{2,1,0:T(8,128)S(1)} %collective-permute-done.10, ...), kind=kLoop, calls=%fused_computation.1 | loop fusion | flops 81920 | bytes 458752 | tf_op jit(solution)/shard_map/broadcast_in_dim | solution.py:422
  (4 shorter events, 0.0 us)
Async XLA Ops:
  1.4 10.9 %collective-permute-start.3 = (f32[2,8,128]{2,1,0:T(8,128)S(1)}, f32[2,8,128]{2,1,0:T(8,128)S(1)}, u32[]{:S(2)}, u32[]{:S(2)}) collective-permute-start(f32[2,8,128]{2,1,0:T(8,128)S(1)} %get-tuple-element.44), channel_id=1, source_target_pairs={{0,3},{1,2},{2,1},{3,0},{4,7},{5,6},{6,5},{7,4},{8,11},{9,10},{10,... | collective-permute-start | bytes 24584 | tf_op jit(solution)/shard_map/ppermute | solution.py:132
  5.3 7.0 %collective-permute-start.2 = (f32[2,8,128]{2,1,0:T(8,128)S(1)}, f32[2,8,128]{2,1,0:T(8,128)S(1)}, u32[]{:S(2)}, u32[]{:S(2)}) collective-permute-start(f32[2,8,128]{2,1,0:T(8,128)S(1)} %get-tuple-element.45), channel_id=1, source_target_pairs={{0,1},{1,0},{2,3},{3,2},{4,5},{5,4},{6,7},{7,6},{8,9},{9,8},{10,11... | collective-permute-start | bytes 24584 | tf_op jit(solution)/shard_map/ppermute | solution.py:132
  5.8 1.6 %copy-start.3 = (f32[1,2,64,4096]{3,2,1,0:T(8,128)S(1)}, f32[1,2,64,4096]{3,2,1,0:T(8,128)}, u32[]{:S(2)}) copy-start(f32[1,2,64,4096]{3,2,1,0:T(8,128)} %param.13) | copy-start | bytes 6291460
  7.4 1.6 %copy-start.5 = (f32[1,2,64,4096]{3,2,1,0:T(8,128)S(1)}, f32[1,2,64,4096]{3,2,1,0:T(8,128)}, u32[]{:S(2)}) copy-start(f32[1,2,64,4096]{3,2,1,0:T(8,128)} %param.11) | copy-start | bytes 6291460
  9.0 1.6 %copy-start.7 = (f32[1,2,64,4096]{3,2,1,0:T(8,128)S(1)}, f32[1,2,64,4096]{3,2,1,0:T(8,128)}, u32[]{:S(2)}) copy-start(f32[1,2,64,4096]{3,2,1,0:T(8,128)} %param.12) | copy-start | bytes 6291460
  10.6 1.7 %copy-start.15 = (f32[1,2,64,128]{3,2,1,0:T(8,128)S(1)}, f32[1,2,64,128]{3,2,1,0:T(8,128)}, u32[]{:S(2)}) copy-start(f32[1,2,64,128]{3,2,1,0:T(8,128)} %param.15) | copy-start | bytes 196612
  10.7 21.1 %collective-permute-start = (f32[2,8,4096]{2,1,0:T(8,128)S(1)}, f32[2,8,4096]{2,1,0:T(8,128)S(1)}, u32[]{:S(2)}, u32[]{:S(2)}) collective-permute-start(f32[2,8,4096]{2,1,0:T(8,128)S(1)} %get-tuple-element.23), channel_id=1, source_target_pairs={{0,1},{1,0},{2,3},{3,2},{4,5},{5,4},{6,7},{7,6},{8,9},{9,8},{10,11... | collective-permute-start | bytes 786440 | tf_op jit(solution)/shard_map/ppermute | solution.py:132
  12.2 19.5 %collective-permute-start.1 = (f32[2,8,4096]{2,1,0:T(8,128)S(1)}, f32[2,8,4096]{2,1,0:T(8,128)S(1)}, u32[]{:S(2)}, u32[]{:S(2)}) collective-permute-start(f32[2,8,4096]{2,1,0:T(8,128)S(1)} %get-tuple-element.24), channel_id=1, source_target_pairs={{0,3},{1,2},{2,1},{3,0},{4,7},{5,6},{6,5},{7,4},{8,11},{9,10},{10,... | collective-permute-start | bytes 786440 | tf_op jit(solution)/shard_map/ppermute | solution.py:132
  12.3 12.6 %collective-permute-start.4 = (f32[2,72,128]{2,1,0:T(8,128)S(1)}, f32[2,72,128]{2,1,0:T(8,128)S(1)}, u32[]{:S(2)}, u32[]{:S(2)}) collective-permute-start(f32[2,72,128]{2,1,0:T(8,128)S(1)} %pad_maximum_fusion.mult_ref.own_ref), channel_id=1, source_target_pairs={{0,4},{4,0},{8,12},{12,8},{16,20},{20,16},{24,28},{28,24},{1,5},{5... | collective-permute-start | bytes 221192 | tf_op jit(solution)/shard_map/ppermute | solution.py:163
  12.4 5.8 %copy-start.2 = (f32[1,16,2,256,2,256]{5,4,3,2,1,0:T(2,128)S(1)}, f32[1,16,2,256,2,256]{5,4,3,2,1,0:T(2,128)}, u32[]{:S(2)}) copy-start(f32[1,16,2,256,2,256]{5,4,3,2,1,0:T(2,128)} %param.14) | copy-start | bytes 50331652
  18.1 6.7 %copy-start.9 = (s32[8,8]{1,0:T(8,128)S(1)}, s32[8,8]{1,0:T(8,128)}, u32[]{:S(2)}) copy-start(s32[8,8]{1,0:T(8,128)} %peer_ref.3) | copy-start | bytes 772
  18.2 6.8 %copy-start.10 = (s32[8,8]{1,0:T(8,128)S(1)}, s32[8,8]{1,0:T(8,128)}, u32[]{:S(2)}) copy-start(s32[8,8]{1,0:T(8,128)} %len_ref.3) | copy-start | bytes 772
  18.2 13.6 %copy-start.4 = (f32[1,2,64,4096]{3,2,1,0:T(8,128)S(1)}, f32[1,2,64,4096]{3,2,1,0:T(8,128)}, u32[]{:S(2)}) copy-start(f32[1,2,64,4096]{3,2,1,0:T(8,128)} %param.13) | copy-start | bytes 6291460
  18.2 13.6 %copy-start.6 = (f32[1,2,64,4096]{3,2,1,0:T(8,128)S(1)}, f32[1,2,64,4096]{3,2,1,0:T(8,128)}, u32[]{:S(2)}) copy-start(f32[1,2,64,4096]{3,2,1,0:T(8,128)} %param.11) | copy-start | bytes 6291460
  18.2 13.6 %copy-start.8 = (f32[1,2,64,4096]{3,2,1,0:T(8,128)S(1)}, f32[1,2,64,4096]{3,2,1,0:T(8,128)}, u32[]{:S(2)}) copy-start(f32[1,2,64,4096]{3,2,1,0:T(8,128)} %param.12) | copy-start | bytes 6291460
  18.2 13.6 %copy-start.11 = (s32[8]{0:T(128)S(1)}, s32[8]{0:T(128)}, u32[]{:S(2)}) copy-start(s32[8]{0:T(128)} %active_ref.7) | copy-start | bytes 100
  18.2 13.6 %copy-start.12 = (f32[1,2,16]{2,1,0:T(2,128)S(1)}, f32[1,2,16]{2,1,0:T(2,128)}, u32[]{:S(2)}) copy-start(f32[1,2,16]{2,1,0:T(2,128)} %pcur_ref.1) | copy-start | bytes 388
  18.2 13.6 %copy-start.13 = (s32[1,16]{1,0:T(1,128)S(1)}, s32[1,16]{1,0:T(1,128)}, u32[]{:S(2)}) copy-start(s32[1,16]{1,0:T(1,128)} %prow_ref.1) | copy-start | bytes 196
  18.2 13.6 %copy-start.14 = (s32[1,16]{1,0:T(1,128)S(1)}, s32[1,16]{1,0:T(1,128)}, u32[]{:S(2)}) copy-start(s32[1,16]{1,0:T(1,128)} %pcol_ref.1) | copy-start | bytes 196
  24.9 12.4 %copy-start = (bf16[16,512,512]{2,1,0:T(8,128)(2,1)}, bf16[16,512,512]{2,1,0:T(8,128)(2,1)S(1)}, u32[]{:S(2)}) copy-start(bf16[16,512,512]{2,1,0:T(8,128)(2,1)S(1)} %get-tuple-element.26.lo_ref) | copy-start | bytes 25165828
  25.7 11.6 %collective-permute-start.5 = (f32[2,72,128]{2,1,0:T(8,128)S(1)}, f32[2,72,128]{2,1,0:T(8,128)S(1)}, u32[]{:S(2)}, u32[]{:S(2)}) collective-permute-start(f32[2,72,128]{2,1,0:T(8,128)S(1)} %get-tuple-element.31), channel_id=1, source_target_pairs={{0,8},{4,12},{8,16},{12,20},{16,24},{20,28},{24,0},{28,4},{1,9},{5... | collective-permute-start | bytes 221192 | tf_op jit(solution)/shard_map/ppermute | solution.py:172
  27.8 9.5 %collective-permute-start.6 = (f32[2,72,128]{2,1,0:T(8,128)S(1)}, f32[2,72,128]{2,1,0:T(8,128)S(1)}, u32[]{:S(2)}, u32[]{:S(2)}) collective-permute-start(f32[2,72,128]{2,1,0:T(8,128)S(1)} %get-tuple-element.32), channel_id=1, source_target_pairs={{0,16},{4,20},{8,24},{12,28},{16,0},{20,4},{24,8},{28,12},{1,17},{... | collective-permute-start | bytes 221192 | tf_op jit(solution)/shard_map/ppermute | solution.py:172
  30.4 6.9 %collective-permute-start.7 = (f32[2,72,128]{2,1,0:T(8,128)S(1)}, f32[2,72,128]{2,1,0:T(8,128)S(1)}, u32[]{:S(2)}, u32[]{:S(2)}) collective-permute-start(f32[2,72,128]{2,1,0:T(8,128)S(1)} %get-tuple-element.33), channel_id=1, source_target_pairs={{0,24},{4,28},{8,0},{12,4},{16,8},{20,12},{24,16},{28,20},{1,25},{... | collective-permute-start | bytes 221192 | tf_op jit(solution)/shard_map/ppermute | solution.py:172
  37.3 3.4 %copy-start.1 = (bf16[16,512,512]{2,1,0:T(8,128)(2,1)S(1)}, bf16[16,512,512]{2,1,0:T(8,128)(2,1)}, u32[]{:S(2)}) copy-start(bf16[16,512,512]{2,1,0:T(8,128)(2,1)} %copy-done) | copy-start | bytes 25165828
  43.2 4.2 %collective-permute-start.8 = (f32[2,64,128]{2,1,0:T(8,128)S(1)}, f32[2,64,128]{2,1,0:T(8,128)S(1)}, u32[]{:S(2)}, u32[]{:S(2)}) collective-permute-start(f32[2,64,128]{2,1,0:T(8,128)S(1)} %get-tuple-element.39.own_ref), channel_id=1, source_target_pairs={{0,4},{4,0},{8,12},{12,8},{16,20},{20,16},{24,28},{28,24},{1,5},{5... | collective-permute-start | bytes 196616 | tf_op jit(solution)/shard_map/ppermute | solution.py:163
  48.2 9.8 %collective-permute-start.9 = (f32[2,64,128]{2,1,0:T(8,128)S(1)}, f32[2,64,128]{2,1,0:T(8,128)S(1)}, u32[]{:S(2)}, u32[]{:S(2)}) collective-permute-start(f32[2,64,128]{2,1,0:T(8,128)S(1)} %get-tuple-element.40), channel_id=1, source_target_pairs={{0,8},{4,12},{8,16},{12,20},{16,24},{20,28},{24,0},{28,4},{1,9},{5... | collective-permute-start | bytes 196616 | tf_op jit(solution)/shard_map/ppermute | solution.py:172
  49.0 9.0 %collective-permute-start.10 = (f32[2,64,128]{2,1,0:T(8,128)S(1)}, f32[2,64,128]{2,1,0:T(8,128)S(1)}, u32[]{:S(2)}, u32[]{:S(2)}) collective-permute-start(f32[2,64,128]{2,1,0:T(8,128)S(1)} %get-tuple-element.41), channel_id=1, source_target_pairs={{0,16},{4,20},{8,24},{12,28},{16,0},{20,4},{24,8},{28,12},{1,17},{... | collective-permute-start | bytes 196616 | tf_op jit(solution)/shard_map/ppermute | solution.py:172
  50.6 7.4 %collective-permute-start.11 = (f32[2,64,128]{2,1,0:T(8,128)S(1)}, f32[2,64,128]{2,1,0:T(8,128)S(1)}, u32[]{:S(2)}, u32[]{:S(2)}) collective-permute-start(f32[2,64,128]{2,1,0:T(8,128)S(1)} %get-tuple-element.42), channel_id=1, source_target_pairs={{0,24},{4,28},{8,0},{12,4},{16,8},{20,12},{24,16},{28,20},{1,25},{... | collective-permute-start | bytes 196616 | tf_op jit(solution)/shard_map/ppermute | solution.py:172
where the time goes:
time: 59 us; the launch traced here: 58.7 us
  Pallas kernels  26.4 us (45%)
  starting transfers between devices  16 us (27%)
  local copies, waits for them, and re-layouts  14 us (24%)
  other arithmetic  1.39 us (2%)
  between operations  0.91 us (2%)
    pallas_call x8, Pallas kernels, call(): pl.pallas_call(kernel, out_shape=outs, in_specs=specs, out_specs=jax.tree...  26.4 us
    unnamed x32, local copies, waits for them, and re-layouts  14 us
    ppermute x6, starting transfers between devices, to_subs(): lax.ppermute(outs[step - 1], 'sub', [(i, (i + 2 * step) % count) for i in...  9.9 us
    ppermute x4, starting transfers between devices, swap_edges(): return (lax.ppermute(one, 'tile', first), lax.ppermute(two, 'tile', second))  6.01 us
  transfers between devices with their start and end apart: 12, of which 0 were waited for; matrix products, arithmetic and copies ran while one was open for 0% of the time, Pallas kernels for 39%

commit v1 on v0

--- a/solution.py
+++ b/solution.py
@@ -12,7 +12,7 @@
 SWEEPS = 3
 LANES = 128
 PAD = 8
-SLOTS = 4
+FILL = 6
 MIB = 1 << 20
 
 VMEM_SPEC = pl.BlockSpec(memory_space=pltpu.VMEM)
@@ -20,12 +20,12 @@
 ANY_SPEC = pl.BlockSpec(memory_space=pl.ANY)
 
 
-def call(kernel, args, specs, outs, limit, scratch=(), flops=0, moved=0):
+def call(kernel, args, specs, outs, limit, scratch=(), flops=0, moved=0, out_specs=None):
     return pl.pallas_call(
         kernel,
         out_shape=outs,
         in_specs=specs,
-        out_specs=jax.tree.map(lambda _: VMEM_SPEC, outs),
+        out_specs=out_specs or jax.tree.map(lambda _: VMEM_SPEC, outs),
         scratch_shapes=scratch,
         compiler_params=pltpu.CompilerParams(vmem_limit_bytes=limit),
         cost_estimate=pl.CostEstimate(flops=flops, bytes_accessed=moved, transcendentals=0),
@@ -55,24 +55,14 @@
     return high, (x - high.astype(jnp.float32)).astype(jnp.bfloat16)
 
 
-def weights_kernel(size, b_ref, hi_ref, lo_ref, buf, sem):
-    nb = b_ref.shape[0]
+def weights_kernel(size, b_ref, hi_ref, lo_ref):
     both = 2 * size
     parts = both // LANES
-
-    def copy(k):
-        return pltpu.make_async_copy(b_ref.at[k], buf.at[k % SLOTS], sem.at[k % SLOTS])
-
-    for k in range(min(SLOTS - 1, nb)):
-        copy(k).start()
-    for k in range(nb):
-        if k + SLOTS - 1 < nb:
-            copy(k + SLOTS - 1).start()
-        copy(k).wait()
+    for k in range(b_ref.shape[0]):
         for q in range(parts):
             piece, comp = divmod(q, 2)
             rows = pl.ds(comp * size + piece * LANES, LANES)
-            high, low = split_halves(buf[k % SLOTS, pl.ds(q, both, parts), :].T)
+            high, low = split_halves(b_ref[k, pl.ds(q, both, parts), :].T)
             hi_ref[k, rows, :] = high
             lo_ref[k, rows, :] = low
 
@@ -86,39 +76,29 @@
     shape = (nb, both, both)
     return call(
         functools.partial(weights_kernel, size),
-        (flat,),
-        [ANY_SPEC],
+        (pltpu.with_memory_space_constraint(flat, pltpu.VMEM),),
+        [VMEM_SPEC],
         [held(shape, jnp.bfloat16)] * 2,
-        10 * MIB,
-        [pltpu.VMEM((SLOTS, both * parts, LANES), jnp.float32), pltpu.SemaphoreType.DMA((SLOTS,))],
+        2 * MIB,
         moved=nb * both * both * 8,
     )
 
 
-def edges_kernel(start_ref, load_ref, diag_ref, one_ref, two_ref):
-    rows = start_ref.shape[1]
+def edge_lines(start, load, diag, top):
+    rows = load.shape[1]
+    field = slice(0, 3) if top else slice(rows - 3, rows)
+    other = slice(0, 2) if top else slice(rows - 2, rows)
+    parts = [start[:, field], load[:, other], diag[:, other], diag[:, :1]]
+    return jnp.concatenate(parts, axis=1)
+
+
+def lines_kernel(mult_ref, one_ref, two_ref, out_ref):
+    rows = mult_ref.shape[1]
     even = lax.rem(lax.axis_index("tile"), 2) == 0
-    top, bottom = pl.ds(0, PAD), pl.ds(rows - PAD, PAD)
-    row = lax.broadcasted_iota(jnp.int32, (PAD, start_ref.shape[2]), 0)
-    for c in range(2):
-        first = jnp.where(
-            row < 3,
-            start_ref[c, top, :],
-            jnp.where(
-                row < 5, pltpu.roll(load_ref[c, top, :], 3, 0), pltpu.roll(diag_ref[c, top, :], 5, 0)
-            ),
-        )
-        last = jnp.where(
-            row < 3,
-            pltpu.roll(start_ref[c, bottom, :], 3, 0),
-            jnp.where(
-                row < 5,
-                pltpu.roll(load_ref[c, bottom, :], 5, 0),
-                pltpu.roll(diag_ref[c, bottom, :], 7, 0),
-            ),
-        )
-        one_ref[c] = jnp.where(even, last, first)
-        two_ref[c] = jnp.where(even, first, last)
+    low = lax.broadcasted_iota(jnp.int32, (PAD, IB), 0) < PAD // 2
+    for c in range(2):
+        out_ref[c, :rows] = mult_ref[c]
+        out_ref[c, rows:] = jnp.where(low == even, one_ref[c], two_ref[c])
 
 
 def swaps(count):
@@ -292,7 +272,7 @@
 def far_kernel(
     count, f0_ref, f1_ref, src_ref, dg_ref, hi_ref, lo_ref, active_ref, *refs
 ):
-    pieces, (f1e_ref, f2e_ref, f3e_ref, far_ref) = refs[:count], refs[count:]
+    pieces, (f1e_ref, f2s_ref, f2e_ref, f3e_ref, far_ref) = refs[:count], refs[count:]
     last = hi_ref.shape[0] - 1
     size = hi_ref.shape[1] // 2
     rows = far_ref.shape[1]
@@ -314,10 +294,21 @@
     for c in range(2):
         f1e_ref[c] = new[c]
     f1 = [(last, f1e_ref), (0, f1_ref)]
+    fill = f2s_ref.shape[2] // size
+
+    def beside(k):
+        new = relax_block([(0, f1_ref)], stored_source(src_ref, k, size), dg_ref, hi_ref, lo_ref, k, mask)
+        for c in range(2):
+            f2s_ref[c, :, k * size : (k + 1) * size] = new[c]
+
+    for k in range(fill // 2):
+        beside(k)
     for k, source in ((last, with_incoming), (last - 1, stored_source(src_ref, last - 1, size))):
         new = relax_block(f1, source, dg_ref, hi_ref, lo_ref, k, mask)
         for c in range(2):
             f2e_ref[c, :, (k - last + 1) * size : (k - last + 2) * size] = new[c]
+    for k in range(fill // 2, fill):
+        beside(k)
     new = relax_block([(last - 1, f2e_ref)], with_incoming, dg_ref, hi_ref, lo_ref, last, mask)
     for c in range(2):
         f3e_ref[c] = new[c][PAD : PAD + rows]
@@ -327,28 +318,41 @@
 def middle_kernel(f1_ref, src_ref, dg_ref, hi_ref, lo_ref, active_ref, f2_ref):
     size = hi_ref.shape[1] // 2
     mask = line_mask(active_ref, (f2_ref.shape[1], size), f2_ref.shape[1] - 2 * PAD)
-    for k in range(f2_ref.shape[2] // size):
+    for i in range(f2_ref.shape[2] // size):
+        k = i + FILL
         new = relax_block(
             [(0, f1_ref)], stored_source(src_ref, k, size), dg_ref, hi_ref, lo_ref, k, mask
         )
         for c in range(2):
-            f2_ref[c, :, k * size : (k + 1) * size] = new[c]
-
-
-def last_kernel(f2_ref, f2e_ref, f3e_ref, src_ref, dg_ref, hi_ref, lo_ref, active_ref, out_ref, near_ref):
+            f2_ref[c, :, i * size : (i + 1) * size] = new[c]
+
+
+def last_kernel(
+    f2s_ref, f2_ref, f2e_ref, f3e_ref, src_ref, dg_ref, hi_ref, lo_ref, active_ref, out_ref, near_ref,
+    held_ref, sem,
+):
     size = hi_ref.shape[1] // 2
+
+    def copy(k):
+        cols = pl.ds(k * size, size)
+        return pltpu.make_async_copy(held_ref.at[:, :, cols], out_ref.at[:, :, cols], sem.at[k])
+
     last = hi_ref.shape[0] - 1
     rows = out_ref.shape[1]
     mask = line_mask(active_ref, (rows + 2 * PAD, size), rows)
-    f2 = [(last - 1, f2e_ref), (0, f2_ref)]
+    f2 = [(last - 1, f2e_ref), (FILL, f2_ref), (0, f2s_ref)]
+    for c in range(2):
+        held_ref[c, :, last * size :] = f3e_ref[c]
+    copy(last).start()
     for k in range(last):
         new = relax_block(f2, stored_source(src_ref, k, size), dg_ref, hi_ref, lo_ref, k, mask)
         for c in range(2):
-            out_ref[c, :, k * size : (k + 1) * size] = new[c][PAD : PAD + rows]
+            held_ref[c, :, k * size : (k + 1) * size] = new[c][PAD : PAD + rows]
             if k == 0:
                 near_ref[c] = new[c][PAD : PAD + rows, :IB]
-    for c in range(2):
-        out_ref[c, :, last * size :] = f3e_ref[c]
+        copy(k).start()
+    for k in range(last + 1):
+        copy(k).wait()
 
 
 def per_device(
@@ -372,14 +376,18 @@
     even = lax.axis_index("tile") % 2 == 0
 
     top, bottom = mult[:, :PAD], mult[:, rows - PAD :]
-    one, two = swap_edges(jnp.where(even, bottom, top), jnp.where(even, top, bottom))
-    up, down = jnp.where(even, two, one), jnp.where(even, one, two)
-    tail = jnp.concatenate([down[:, : PAD // 2], up[:, PAD // 2 :]], axis=1)
-    lines_mult = jnp.concatenate([mult, tail], axis=1)
-
-    edge = jax.ShapeDtypeStruct((2, PAD, width), jnp.float32)
-    one, two = swap_edges(
-        *call(edges_kernel, (start, load, diag), [VMEM_SPEC] * 3, [edge] * 2, 16 * MIB)
+    ends = swap_edges(jnp.where(even, bottom, top), jnp.where(even, top, bottom))
+    first = edge_lines(start, load, diag, True)
+    last = edge_lines(start, load, diag, False)
+    one, two = swap_edges(jnp.where(even, last, first), jnp.where(even, first, last))
+    lines_mult = call(
+        lines_kernel,
+        (mult, *ends),
+        [VMEM_SPEC] * 3,
+        held((2, rows + PAD, IB)),
+        2 * MIB,
+        flops=4 * 10**10,
+        moved=10**8,
     )
     incoming = to_subs(lines_mult, contact_peer, contact_len, PAD, False)
     hi, lo = split_weights(block_inverse[0])
@@ -390,33 +398,35 @@
         (start, load, diag, one, two, lines_mult, hi, lo, active_rows, port_row, port_col, port_current),
         [VMEM_SPEC] * 8 + [SMEM_SPEC] * 4,
         [whole, whole, held((2, high, (nb - 1) * size)), whole],
-        16 * MIB,
+        4 * MIB,
         flops=step * (nb - 1),
     )
-    f1e, f2e, f3e, far = call(
+    f1e, f2s, f2e, f3e, far = call(
         functools.partial(far_kernel, len(incoming)),
         (f0, f1, src, dg, hi, lo, active_rows, *incoming),
         [VMEM_SPEC] * 6 + [SMEM_SPEC] + [VMEM_SPEC] * len(incoming),
-        [held((2, high, size)), held((2, high, 2 * size)), held((2, rows, size)), held((2, rows, IB))],
-        8 * MIB,
-        flops=step * 4,
+        [held((2, high, size)), held((2, high, FILL * size)), held((2, high, 2 * size)), held((2, rows, size)), held((2, rows, IB))],
+        4 * MIB,
+        flops=step * (4 + FILL),
     )
     ends = to_subs(far, contact_peer, contact_len, 0, True)
     f2 = call(
         middle_kernel,
         (f1, src, dg, hi, lo, active_rows),
         [VMEM_SPEC] * 5 + [SMEM_SPEC],
-        held((2, high, (nb - 2) * size)),
-        8 * MIB,
-        flops=step * (nb - 2),
+        held((2, high, (nb - 2 - FILL) * size)),
+        4 * MIB,
+        flops=step * (nb - 2 - FILL),
     )
     solved, near = call(
         last_kernel,
-        (f2, f2e, f3e, src, dg, hi, lo, active_rows),
-        [VMEM_SPEC] * 7 + [SMEM_SPEC],
+        (f2s, f2, f2e, f3e, src, dg, hi, lo, active_rows),
+        [VMEM_SPEC] * 8 + [SMEM_SPEC],
         [jax.ShapeDtypeStruct((2, rows, width), jnp.float32), held((2, rows, IB))],
-        8 * MIB,
+        4 * MIB + 8 * rows * width,
+        [pltpu.VMEM((2, rows, width), jnp.float32), pltpu.SemaphoreType.DMA((nb,))],
         flops=step * (nb - 1),
+        out_specs=[ANY_SPEC, VMEM_SPEC],
     )
     updated = mult + (near - sum(ends))
     return (solved[None], updated[None])

time: 59 us -> 48.5 us (0.82)
  local copies, waits for them, and re-layouts: 14 us -> 7.91 us
  Pallas kernels: 26.4 us -> 22.2 us
    unnamed x32 -> x28, local copies, waits for them, and re-layouts: 14 us -> 4.43 us
    pallas_call x8, Pallas kernels: 26.4 us -> 22.2 us  [call(): pl.pallas_call(kernel, out_shape=outs, in_specs=specs, out_specs=out_spec...]
    slice x0 -> x3, local copies, waits for them, and re-layouts: none -> 3.48 us  [edge_lines(): parts = [start[:, field], load[:, other], diag[:, other], diag[:, :1]]]
  transfers between devices with their start and end apart: 12 -> 12, of which waited for: 0 -> 0; matrix products, arithmetic and copies ran while one was open for 0% -> 8% of each run, Pallas kernels for 39% -> 37%
where the time goes in v1:
time: 48.5 us; the launch traced here: 48.3 us
  Pallas kernels  22.2 us (46%)
  starting transfers between devices  15.6 us (32%)
  local copies, waits for them, and re-layouts  7.91 us (16%)
  other arithmetic  1.63 us (3%)
  between operations  0.92 us (2%)
    pallas_call x8, Pallas kernels, call(): pl.pallas_call(kernel, out_shape=outs, in_specs=specs, out_specs=out_spec...  22.2 us
    ppermute x6, starting transfers between devices, to_subs(): lax.ppermute(outs[step - 1], 'sub', [(i, (i + 2 * step) % count) for i in...  9.45 us
    ppermute x4, starting transfers between devices, swap_edges(): return (lax.ppermute(one, 'tile', first), lax.ppermute(two, 'tile', second))  6.09 us
    unnamed x28, local copies, waits for them, and re-layouts  4.43 us
    slice x3, local copies, waits for them, and re-layouts, edge_lines(): parts = [start[:, field], load[:, other], diag[:, other], diag[:, :1]]  3.48 us
  transfers between devices with their start and end apart: 12, of which 0 were waited for; matrix products, arithmetic and copies ran while one was open for 8% of the time, Pallas kernels for 37%

profile of v1, /device:TPU:0, one launch (start us, length us, event | category | flops | bytes accessed | tf_op | source)
XLA Modules:
  0.0 48.3 jit_solution(12440447638738917094)
XLA Ops:
  0.6 0.0 copy-start.3
  0.7 0.8 %slice_select_fusion = (f32[2,8,128]{2,1,0:T(8,128)S(1)}, f32[2,8,128]{2,1,0:T(8,128)S(1)}) fusion(f32[2,64,128]{2,1,0:T(8,128)} %bitcast.23, pred[]{:T(512)S(6)} %eq.5), kind=kLoop, calls=%fused_computation.5 | loop fusion | flops 4096 | bytes 32769 | tf_op jit(solution)/shard_map/jit(_where)/select_n | solution.py:379
  1.4 3.9 %collective-permute-start.3 = (f32[2,8,128]{2,1,0:T(8,128)S(1)}, f32[2,8,128]{2,1,0:T(8,128)S(1)}, u32[]{:S(2)}, u32[]{:S(2)}) collective-permute-start(f32[2,8,128]{2,1,0:T(8,128)S(1)} %get-tuple-element.50), channel_id=1, source_target_pairs={{0,3},{1,2},{2,1},{3,0},{4,7},{5,6},{6,5},{7,4},{8,11},{9,10},{10,... | collective-permute-start | bytes 24584 | tf_op jit(solution)/shard_map/ppermute | solution.py:112
  5.3 0.5 %collective-permute-start.2 = (f32[2,8,128]{2,1,0:T(8,128)S(1)}, f32[2,8,128]{2,1,0:T(8,128)S(1)}, u32[]{:S(2)}, u32[]{:S(2)}) collective-permute-start(f32[2,8,128]{2,1,0:T(8,128)S(1)} %get-tuple-element.51), channel_id=1, source_target_pairs={{0,1},{1,0},{2,3},{3,2},{4,5},{5,4},{6,7},{7,6},{8,9},{9,8},{10,11... | collective-permute-start | bytes 24584 | tf_op jit(solution)/shard_map/ppermute | solution.py:112
  5.8 1.0 %slice.40 = f32[2,1,4096]{2,1,0:T(1,128)S(1)} slice(f32[2,64,4096]{2,1,0:T(8,128)} %bitcast.18), slice={[0:2], [0:1], [0:4096]} | slice | bytes 65536 | tf_op jit(solution)/shard_map/slice | solution.py:91
  6.8 1.3 %fusion.3 = (f32[2,2,4096]{2,1,0:T(2,128)S(1)}, f32[2,2,4096]{2,1,0:T(2,128)S(1)}, f32[2,2,4096]{2,1,0:T(2,128)S(1)}, f32[2,2,4096]{2,1,0:T(2,128)S(1)}) fusion(f32[2,64,4096]{2,1,0:T(8,128)} %bitcast.21, f32[2,64,4096]{2,1,0:T(8,128)} %bitcast.19), kind=kLoop, calls=%fused_computation.8 | loop fusion | bytes 524288 | tf_op jit(solution)/shard_map/slice | solution.py:91
  8.1 0.0 slice-start
  8.1 1.2 %fusion.2 = (f32[2,3,4096]{2,1,0:T(4,128)S(1)}, f32[2,3,4096]{2,1,0:T(4,128)S(1)}) fusion(f32[2,64,4096]{2,1,0:T(8,128)} %bitcast.16), kind=kLoop, calls=%fused_computation.7 | loop fusion | bytes 393216 | tf_op jit(solution)/shard_map/slice | solution.py:91
  9.3 0.2 fusion
  9.6 1.5 %collective-permute-start.1 = (f32[2,8,4096]{2,1,0:T(8,128)S(1)}, f32[2,8,4096]{2,1,0:T(8,128)S(1)}, u32[]{:S(2)}, u32[]{:S(2)}) collective-permute-start(f32[2,8,4096]{2,1,0:T(8,128)S(1)} %get-tuple-element.48), channel_id=1, source_target_pairs={{0,3},{1,2},{2,1},{3,0},{4,7},{5,6},{6,5},{7,4},{8,11},{9,10},{10,... | collective-permute-start | bytes 786440 | tf_op jit(solution)/shard_map/ppermute | solution.py:112
  11.1 0.0 slice-start.1
  11.1 0.0 slice-start.2
  11.1 0.0 slice-start.3
  11.1 0.2 collective-permute-start
  11.2 0.0 collective-permute-done.3.two_ref
  11.2 0.0 collective-permute-done.2.one_ref
  11.2 0.0 copy-done.3
  11.3 0.1 collective-permute-start.4
  11.3 0.0 slice-done
  11.4 1.9 %slice-done.1 = s8[4194304]{0:T(1024)(128)(4,1)S(1)} async-done(((s8[16777216]{0:T(1024)(128)(4,1)}), s8[4194304]{0:T(1024)(128)(4,1)S(1)}, s32[]{:S(2)}) %slice-start.1) | async-done | bytes 4194328
  13.3 1.3 %slice-done.2 = s8[4194304]{0:T(1024)(128)(4,1)S(1)} async-done(((s8[16777216]{0:T(1024)(128)(4,1)}), s8[4194304]{0:T(1024)(128)(4,1)S(1)}, s32[]{:S(2)}) %slice-start.2) | async-done | bytes 4194328
  14.5 1.2 %slice-done.3 = s8[4194304]{0:T(1024)(128)(4,1)S(1)} async-done(((s8[16777216]{0:T(1024)(128)(4,1)}), s8[4194304]{0:T(1024)(128)(4,1)S(1)}, s32[]{:S(2)}) %slice-start.3) | async-done | bytes 4194328
  15.7 0.0 copy-start.4
  15.7 0.0 copy-start.5
  15.7 0.0 copy-start
  15.7 0.0 copy-start.2
  15.8 0.0 copy-start.6
  15.8 0.0 copy-start.7
  15.8 0.0 copy-start.8
  15.8 0.0 copy-start.9
  15.8 4.4 %shard_map.123 = (bf16[16,512,512]{2,1,0:T(8,128)(2,1)S(1)}, bf16[16,512,512]{2,1,0:T(8,128)(2,1)S(1)}) custom-call(f32[16,2048,128]{2,1,0:T(8,128)S(1)} %bitcast.15), custom_call_target="tpu_custom_call" | custom-call | bytes 33554432 | tf_op jit(solution)/shard_map/pallas_call | solution.py:24
  20.2 0.0 collective-permute-done.4.other_ref
  20.2 0.0 copy-done.4
  20.2 0.0 copy-done.5
  20.2 0.8 %shard_map.125 = (f32[2,72,128]{2,1,0:T(8,128)S(1)}, f32[2,72,128]{2,1,0:T(8,128)S(1)}, f32[2,72,128]{2,1,0:T(8,128)S(1)}, f32[2,72,128]{2,1,0:T(8,128)S(1)}) custom-call(f32[2,72,128]{2,1,0:T(8,128)S(1)} %shard_map.122.mult_ref.own_ref, f32[2,72,128]{2,1,0:T(8,128)S(1)} %collective-permute-done.4.other_ref, s32[8,8]{1,0:T(8,128)S(1)} %copy-done.4, ...), custom_call_target="tpu_custom_call" | custom-call | tf_op jit(solution)/shard_map/pallas_call | solution.py:24
  21.0 1.6 %collective-permute-start.5 = (f32[2,72,128]{2,1,0:T(8,128)S(1)}, f32[2,72,128]{2,1,0:T(8,128)S(1)}, u32[]{:S(2)}, u32[]{:S(2)}) collective-permute-start(f32[2,72,128]{2,1,0:T(8,128)S(1)} %get-tuple-element.28), channel_id=1, source_target_pairs={{0,8},{4,12},{8,16},{12,20},{16,24},{20,28},{24,0},{28,4},{1,9},{5... | collective-permute-start | bytes 221192 | tf_op jit(solution)/shard_map/ppermute | solution.py:152
  22.6 2.6 %collective-permute-start.6 = (f32[2,72,128]{2,1,0:T(8,128)S(1)}, f32[2,72,128]{2,1,0:T(8,128)S(1)}, u32[]{:S(2)}, u32[]{:S(2)}) collective-permute-start(f32[2,72,128]{2,1,0:T(8,128)S(1)} %get-tuple-element.29), channel_id=1, source_target_pairs={{0,16},{4,20},{8,24},{12,28},{16,0},{20,4},{24,8},{28,12},{1,17},{... | collective-permute-start | bytes 221192 | tf_op jit(solution)/shard_map/ppermute | solution.py:152
  25.2 1.3 %collective-permute-start.7 = (f32[2,72,128]{2,1,0:T(8,128)S(1)}, f32[2,72,128]{2,1,0:T(8,128)S(1)}, u32[]{:S(2)}, u32[]{:S(2)}) collective-permute-start(f32[2,72,128]{2,1,0:T(8,128)S(1)} %get-tuple-element.30), channel_id=1, source_target_pairs={{0,24},{4,28},{8,0},{12,4},{16,8},{20,12},{24,16},{28,20},{1,25},{... | collective-permute-start | bytes 221192 | tf_op jit(solution)/shard_map/ppermute | solution.py:152
  26.6 0.0 collective-permute-done.1.two_ref
  26.6 0.0 collective-permute-done.one_ref
  26.6 0.0 copy-done
  26.6 0.0 copy-done.1
  26.6 0.0 copy-done.2
  26.6 0.0 copy-done.6
  26.6 0.0 copy-done.7
  26.6 0.0 copy-done.8
  26.6 0.0 copy-done.9
  26.7 5.1 %shard_map.124 = (f32[2,80,4096]{2,1,0:T(8,128)S(1)}, f32[2,80,4096]{2,1,0:T(8,128)S(1)}, f32[2,80,3840]{2,1,0:T(8,128)S(1)}, f32[2,80,4096]{2,1,0:T(8,128)S(1)}) custom-call(f32[2,64,4096]{2,1,0:T(8,128)S(1)} %bitcast.17, f32[2,64,4096]{2,1,0:T(8,128)S(1)} %bitcast.22, f32[2,64,4096]{2,1,0:T(8,128)S(1)} %bitcast.20, ...), custom_call_target="tpu_custom_call" | custom-call | flops 1887436800 | tf_op jit(solution)/shard_map/pallas_call | solution.py:24
  31.7 0.0 collective-permute-done.5.refs_0_
  31.7 0.0 collective-permute-done.6.refs_1_
  31.7 0.0 collective-permute-done.7.refs_2_
  31.8 3.4 %shard_map.126 = (f32[2,80,256]{2,1,0:T(8,128)}, f32[2,80,1536]{2,1,0:T(8,128)S(1)}, f32[2,80,512]{2,1,0:T(8,128)S(1)}, f32[2,64,256]{2,1,0:T(8,128)S(1)}, f32[2,64,128]{2,1,0:T(8,128)S(1)}) custom-call(f32[2,80,4096]{2,1,0:T(8,128)S(1)} %get-tuple-element.24.f0_ref, f32[2,80,3840]{2,1,0:T(8,128)S(1)} %get-tuple-element.25.f1_ref, ...), custom_call_target="tpu_custom_call" | custom-call | flops 1258291200 | tf_op jit(solution)/shard_map/pallas_call | solution.py:24
  35.1 0.0 collective-permute-start.8
  35.1 2.4 %shard_map.127.f2_ref = f32[2,80,2048]{2,1,0:T(8,128)S(1)} custom-call(f32[2,80,3840]{2,1,0:T(8,128)S(1)} %get-tuple-element.25.f1_ref, f32[2,80,4096]{2,1,0:T(8,128)S(1)} %get-tuple-element.26.src_ref, f32[2,80,4096]{2,1,0:T(8,128)S(1)} %get-tuple-element.27.dg_ref, bf16[16,512,512]{2,1,0:T(8,128)(2,1)S(1)} %get-tuple-element.22.hi_ref, ...), custom_call_target="tpu_custom_call" | custom-call | flops 1006632960 | tf_op jit(solution)/shard_map/pallas_call | solution.py:24
  37.5 0.0 collective-permute-done.8.other_ref
  37.6 0.9 %shard_map.129 = (f32[2,64,128]{2,1,0:T(8,128)S(1)}, f32[2,64,128]{2,1,0:T(8,128)S(1)}, f32[2,64,128]{2,1,0:T(8,128)S(1)}, f32[2,64,128]{2,1,0:T(8,128)S(1)}) custom-call(f32[2,64,128]{2,1,0:T(8,128)S(1)} %get-tuple-element.37.own_ref, f32[2,64,128]{2,1,0:T(8,128)S(1)} %collective-permute-done.8.other_ref, s32[8,8]{1,0:T(8,128)S(1)} %copy-done.4, ...), custom_call_target="tpu_custom_call" | custom-call | tf_op jit(solution)/shard_map/pallas_call | solution.py:24
  38.4 0.7 %collective-permute-start.9 = (f32[2,64,128]{2,1,0:T(8,128)S(1)}, f32[2,64,128]{2,1,0:T(8,128)S(1)}, u32[]{:S(2)}, u32[]{:S(2)}) collective-permute-start(f32[2,64,128]{2,1,0:T(8,128)S(1)} %get-tuple-element.38), channel_id=1, source_target_pairs={{0,8},{4,12},{8,16},{12,20},{16,24},{20,28},{24,0},{28,4},{1,9},{5... | collective-permute-start | bytes 196616 | tf_op jit(solution)/shard_map/ppermute | solution.py:152
  39.1 1.0 %collective-permute-start.10 = (f32[2,64,128]{2,1,0:T(8,128)S(1)}, f32[2,64,128]{2,1,0:T(8,128)S(1)}, u32[]{:S(2)}, u32[]{:S(2)}) collective-permute-start(f32[2,64,128]{2,1,0:T(8,128)S(1)} %get-tuple-element.39), channel_id=1, source_target_pairs={{0,16},{4,20},{8,24},{12,28},{16,0},{20,4},{24,8},{28,12},{1,17},{... | collective-permute-start | bytes 196616 | tf_op jit(solution)/shard_map/ppermute | solution.py:152
  40.1 2.2 %collective-permute-start.11 = (f32[2,64,128]{2,1,0:T(8,128)S(1)}, f32[2,64,128]{2,1,0:T(8,128)S(1)}, u32[]{:S(2)}, u32[]{:S(2)}) collective-permute-start(f32[2,64,128]{2,1,0:T(8,128)S(1)} %get-tuple-element.40), channel_id=1, source_target_pairs={{0,24},{4,28},{8,0},{12,4},{16,8},{20,12},{24,16},{28,20},{1,25},{... | collective-permute-start | bytes 196616 | tf_op jit(solution)/shard_map/ppermute | solution.py:152
  42.3 5.3 %shard_map.128 = (f32[2,64,4096]{2,1,0:T(8,128)}, f32[2,64,128]{2,1,0:T(8,128)S(1)}) custom-call(f32[2,80,1536]{2,1,0:T(8,128)S(1)} %get-tuple-element.32.f2s_ref, f32[2,80,2048]{2,1,0:T(8,128)S(1)} %shard_map.127.f2_ref, f32[2,80,512]{2,1,0:T(8,128)S(1)} %get-tuple-element.33.f2e_ref, f32[2,64,256]{2,1,0:T(8,128)S(1)} %get-tuple-element.34.f3e_ref, ...), custom_call_target="tpu_custom_call" | custom-call | flops 1887436800 | tf_op jit(solution)/shard_map/pallas_call | solution.py:24
  47.6 0.0 collective-permute-done.9
  47.6 0.0 collective-permute-done.10
  47.6 0.0 collective-permute-done.11
  47.6 0.7 %add_bitcast_fusion = f32[1,2,64,128]{3,2,1,0:T(8,128)} fusion(f32[2,64,128]{2,1,0:T(8,128)S(1)} %get-tuple-element.36, f32[2,64,128]{2,1,0:T(8,128)S(1)} %get-tuple-element.41, f32[2,64,128]{2,1,0:T(8,128)S(1)} %collective-permute-done.11, f32[2,64,128]{2,1,0:T(8,128)S(1)} %collective-permute-done.9, f32[2,64,128]{2,1,0:T(8,128)S(1)} %collective-permute-done.10, ...), kind=kLoop, calls=%fused_computation.4 | loop fusion | flops 81920 | bytes 458752 | tf_op jit(solution)/shard_map/broadcast_in_dim | solution.py:432
  (3 shorter events, 0.0 us)
Async XLA Ops:
  0.6 10.6 %copy-start.3 = (f32[1,2,64,128]{3,2,1,0:T(8,128)S(1)}, f32[1,2,64,128]{3,2,1,0:T(8,128)}, u32[]{:S(2)}) copy-start(f32[1,2,64,128]{3,2,1,0:T(8,128)} %param.15) | copy-start | bytes 196612
  1.4 9.8 %collective-permute-start.3 = (f32[2,8,128]{2,1,0:T(8,128)S(1)}, f32[2,8,128]{2,1,0:T(8,128)S(1)}, u32[]{:S(2)}, u32[]{:S(2)}) collective-permute-start(f32[2,8,128]{2,1,0:T(8,128)S(1)} %get-tuple-element.50), channel_id=1, source_target_pairs={{0,3},{1,2},{2,1},{3,0},{4,7},{5,6},{6,5},{7,4},{8,11},{9,10},{10,... | collective-permute-start | bytes 24584 | tf_op jit(solution)/shard_map/ppermute | solution.py:112
  5.3 5.9 %collective-permute-start.2 = (f32[2,8,128]{2,1,0:T(8,128)S(1)}, f32[2,8,128]{2,1,0:T(8,128)S(1)}, u32[]{:S(2)}, u32[]{:S(2)}) collective-permute-start(f32[2,8,128]{2,1,0:T(8,128)S(1)} %get-tuple-element.51), channel_id=1, source_target_pairs={{0,1},{1,0},{2,3},{3,2},{4,5},{5,4},{6,7},{7,6},{8,9},{9,8},{10,11... | collective-permute-start | bytes 24584 | tf_op jit(solution)/shard_map/ppermute | solution.py:112
  8.1 3.3 %slice-start = ((s8[16777216]{0:T(1024)(128)(4,1)}), s8[4194304]{0:T(1024)(128)(4,1)S(1)}, s32[]{:S(2)}) async-start(s8[16777216]{0:T(1024)(128)(4,1)} %bitcast.13), calls=%async_computation | async-start | bytes 8388608
  9.6 17.0 %collective-permute-start.1 = (f32[2,8,4096]{2,1,0:T(8,128)S(1)}, f32[2,8,4096]{2,1,0:T(8,128)S(1)}, u32[]{:S(2)}, u32[]{:S(2)}) collective-permute-start(f32[2,8,4096]{2,1,0:T(8,128)S(1)} %get-tuple-element.48), channel_id=1, source_target_pairs={{0,3},{1,2},{2,1},{3,0},{4,7},{5,6},{6,5},{7,4},{8,11},{9,10},{10,... | collective-permute-start | bytes 786440 | tf_op jit(solution)/shard_map/ppermute | solution.py:112
  11.1 2.2 %slice-start.1 = ((s8[16777216]{0:T(1024)(128)(4,1)}), s8[4194304]{0:T(1024)(128)(4,1)S(1)}, s32[]{:S(2)}) async-start(s8[16777216]{0:T(1024)(128)(4,1)} %bitcast.13), calls=%async_computation.1 | async-start | bytes 8388608
  11.1 3.5 %slice-start.2 = ((s8[16777216]{0:T(1024)(128)(4,1)}), s8[4194304]{0:T(1024)(128)(4,1)S(1)}, s32[]{:S(2)}) async-start(s8[16777216]{0:T(1024)(128)(4,1)} %bitcast.13), calls=%async_computation.2 | async-start | bytes 8388608
  11.1 4.7 %slice-start.3 = ((s8[16777216]{0:T(1024)(128)(4,1)}), s8[4194304]{0:T(1024)(128)(4,1)S(1)}, s32[]{:S(2)}) async-start(s8[16777216]{0:T(1024)(128)(4,1)} %bitcast.13), calls=%async_computation.3 | async-start | bytes 8388608
  11.1 15.5 %collective-permute-start = (f32[2,8,4096]{2,1,0:T(8,128)S(1)}, f32[2,8,4096]{2,1,0:T(8,128)S(1)}, u32[]{:S(2)}, u32[]{:S(2)}) collective-permute-start(f32[2,8,4096]{2,1,0:T(8,128)S(1)} %get-tuple-element.49), channel_id=1, source_target_pairs={{0,1},{1,0},{2,3},{3,2},{4,5},{5,4},{6,7},{7,6},{8,9},{9,8},{10,11... | collective-permute-start | bytes 786440 | tf_op jit(solution)/shard_map/ppermute | solution.py:112
  11.3 8.9 %collective-permute-start.4 = (f32[2,72,128]{2,1,0:T(8,128)S(1)}, f32[2,72,128]{2,1,0:T(8,128)S(1)}, u32[]{:S(2)}, u32[]{:S(2)}) collective-permute-start(f32[2,72,128]{2,1,0:T(8,128)S(1)} %shard_map.122.mult_ref.own_ref), channel_id=1, source_target_pairs={{0,4},{4,0},{8,12},{12,8},{16,20},{20,16},{24,28},{28,24},{1,5},{5... | collective-permute-start | bytes 221192 | tf_op jit(solution)/shard_map/ppermute | solution.py:143
  15.7 4.5 %copy-start.4 = (s32[8,8]{1,0:T(8,128)S(1)}, s32[8,8]{1,0:T(8,128)}, u32[]{:S(2)}) copy-start(s32[8,8]{1,0:T(8,128)} %peer_ref.3) | copy-start | bytes 772
  15.7 4.5 %copy-start.5 = (s32[8,8]{1,0:T(8,128)S(1)}, s32[8,8]{1,0:T(8,128)}, u32[]{:S(2)}) copy-start(s32[8,8]{1,0:T(8,128)} %len_ref.3) | copy-start | bytes 772
  15.7 10.9 %copy-start = (f32[1,2,64,4096]{3,2,1,0:T(8,128)S(1)}, f32[1,2,64,4096]{3,2,1,0:T(8,128)}, u32[]{:S(2)}) copy-start(f32[1,2,64,4096]{3,2,1,0:T(8,128)} %param.13) | copy-start | bytes 6291460
  15.7 10.9 %copy-start.1 = (f32[1,2,64,4096]{3,2,1,0:T(8,128)S(1)}, f32[1,2,64,4096]{3,2,1,0:T(8,128)}, u32[]{:S(2)}) copy-start(f32[1,2,64,4096]{3,2,1,0:T(8,128)} %param.12) | copy-start | bytes 6291460
  15.7 10.9 %copy-start.2 = (f32[1,2,64,4096]{3,2,1,0:T(8,128)S(1)}, f32[1,2,64,4096]{3,2,1,0:T(8,128)}, u32[]{:S(2)}) copy-start(f32[1,2,64,4096]{3,2,1,0:T(8,128)} %param.11) | copy-start | bytes 6291460
  15.8 10.9 %copy-start.6 = (s32[8]{0:T(128)S(1)}, s32[8]{0:T(128)}, u32[]{:S(2)}) copy-start(s32[8]{0:T(128)} %active_ref.7) | copy-start | bytes 100
  15.8 10.9 %copy-start.7 = (f32[1,2,16]{2,1,0:T(2,128)S(1)}, f32[1,2,16]{2,1,0:T(2,128)}, u32[]{:S(2)}) copy-start(f32[1,2,16]{2,1,0:T(2,128)} %pcur_ref.1) | copy-start | bytes 388
  15.8 10.9 %copy-start.8 = (s32[1,16]{1,0:T(1,128)S(1)}, s32[1,16]{1,0:T(1,128)}, u32[]{:S(2)}) copy-start(s32[1,16]{1,0:T(1,128)} %prow_ref.1) | copy-start | bytes 196
  15.8 10.9 %copy-start.9 = (s32[1,16]{1,0:T(1,128)S(1)}, s32[1,16]{1,0:T(1,128)}, u32[]{:S(2)}) copy-start(s32[1,16]{1,0:T(1,128)} %pcol_ref.1) | copy-start | bytes 196
  21.0 10.7 %collective-permute-start.5 = (f32[2,72,128]{2,1,0:T(8,128)S(1)}, f32[2,72,128]{2,1,0:T(8,128)S(1)}, u32[]{:S(2)}, u32[]{:S(2)}) collective-permute-start(f32[2,72,128]{2,1,0:T(8,128)S(1)} %get-tuple-element.28), channel_id=1, source_target_pairs={{0,8},{4,12},{8,16},{12,20},{16,24},{20,28},{24,0},{28,4},{1,9},{5... | collective-permute-start | bytes 221192 | tf_op jit(solution)/shard_map/ppermute | solution.py:152
  22.6 9.1 %collective-permute-start.6 = (f32[2,72,128]{2,1,0:T(8,128)S(1)}, f32[2,72,128]{2,1,0:T(8,128)S(1)}, u32[]{:S(2)}, u32[]{:S(2)}) collective-permute-start(f32[2,72,128]{2,1,0:T(8,128)S(1)} %get-tuple-element.29), channel_id=1, source_target_pairs={{0,16},{4,20},{8,24},{12,28},{16,0},{20,4},{24,8},{28,12},{1,17},{... | collective-permute-start | bytes 221192 | tf_op jit(solution)/shard_map/ppermute | solution.py:152
  25.2 6.5 %collective-permute-start.7 = (f32[2,72,128]{2,1,0:T(8,128)S(1)}, f32[2,72,128]{2,1,0:T(8,128)S(1)}, u32[]{:S(2)}, u32[]{:S(2)}) collective-permute-start(f32[2,72,128]{2,1,0:T(8,128)S(1)} %get-tuple-element.30), channel_id=1, source_target_pairs={{0,24},{4,28},{8,0},{12,4},{16,8},{20,12},{24,16},{28,20},{1,25},{... | collective-permute-start | bytes 221192 | tf_op jit(solution)/shard_map/ppermute | solution.py:152
  35.1 2.4 %collective-permute-start.8 = (f32[2,64,128]{2,1,0:T(8,128)S(1)}, f32[2,64,128]{2,1,0:T(8,128)S(1)}, u32[]{:S(2)}, u32[]{:S(2)}) collective-permute-start(f32[2,64,128]{2,1,0:T(8,128)S(1)} %get-tuple-element.37.own_ref), channel_id=1, source_target_pairs={{0,4},{4,0},{8,12},{12,8},{16,20},{20,16},{24,28},{28,24},{1,5},{5... | collective-permute-start | bytes 196616 | tf_op jit(solution)/shard_map/ppermute | solution.py:143
  38.4 9.2 %collective-permute-start.9 = (f32[2,64,128]{2,1,0:T(8,128)S(1)}, f32[2,64,128]{2,1,0:T(8,128)S(1)}, u32[]{:S(2)}, u32[]{:S(2)}) collective-permute-start(f32[2,64,128]{2,1,0:T(8,128)S(1)} %get-tuple-element.38), channel_id=1, source_target_pairs={{0,8},{4,12},{8,16},{12,20},{16,24},{20,28},{24,0},{28,4},{1,9},{5... | collective-permute-start | bytes 196616 | tf_op jit(solution)/shard_map/ppermute | solution.py:152
  39.1 8.5 %collective-permute-start.10 = (f32[2,64,128]{2,1,0:T(8,128)S(1)}, f32[2,64,128]{2,1,0:T(8,128)S(1)}, u32[]{:S(2)}, u32[]{:S(2)}) collective-permute-start(f32[2,64,128]{2,1,0:T(8,128)S(1)} %get-tuple-element.39), channel_id=1, source_target_pairs={{0,16},{4,20},{8,24},{12,28},{16,0},{20,4},{24,8},{28,12},{1,17},{... | collective-permute-start | bytes 196616 | tf_op jit(solution)/shard_map/ppermute | solution.py:152
  40.1 7.5 %collective-permute-start.11 = (f32[2,64,128]{2,1,0:T(8,128)S(1)}, f32[2,64,128]{2,1,0:T(8,128)S(1)}, u32[]{:S(2)}, u32[]{:S(2)}) collective-permute-start(f32[2,64,128]{2,1,0:T(8,128)S(1)} %get-tuple-element.40), channel_id=1, source_target_pairs={{0,24},{4,28},{8,0},{12,4},{16,8},{20,12},{24,16},{28,20},{1,25},{... | collective-permute-start | bytes 196616 | tf_op jit(solution)/shard_map/ppermute | solution.py:152

commit v2 on v1

--- a/solution.py
+++ b/solution.py
@@ -84,12 +84,38 @@
     )
 
 
-def edge_lines(start, load, diag, top):
-    rows = load.shape[1]
-    field = slice(0, 3) if top else slice(rows - 3, rows)
-    other = slice(0, 2) if top else slice(rows - 2, rows)
-    parts = [start[:, field], load[:, other], diag[:, other], diag[:, :1]]
-    return jnp.concatenate(parts, axis=1)
+def edges_kernel(start_hbm, load_hbm, diag_hbm, mult_ref, m1_ref, m2_ref, one_ref, two_ref, buf, sem):
+    rows = start_hbm.shape[1]
+    even = lax.rem(lax.axis_index("tile"), 2) == 0
+    ends = (pl.ds(0, PAD), pl.ds(rows - PAD, PAD))
+    copies = [
+        pltpu.make_async_copy(ref.at[:, ends[e]], buf.at[i, e], sem.at[i, e])
+        for i, ref in enumerate((start_hbm, load_hbm, diag_hbm))
+        for e in range(2)
+    ]
+    for copy in copies:
+        copy.start()
+    for c in range(2):
+        first, last = mult_ref[c, ends[0]], mult_ref[c, ends[1]]
+        m1_ref[c] = jnp.where(even, last, first)
+        m2_ref[c] = jnp.where(even, first, last)
+    for copy in copies:
+        copy.wait()
+    row = lax.broadcasted_iota(jnp.int32, one_ref.shape[1:], 0)
+
+    def lines(c, e, turns):
+        field, load, diag = (pltpu.roll(buf[i, e, c], t, 0) if t else buf[i, e, c] for i, t in enumerate(turns))
+        return jnp.where(row < 3, field, jnp.where(row < 5, load, diag))
+
+    for c in range(2):
+        first, last = lines(c, 0, (0, 3, 5)), lines(c, 1, (3, 5, 7))
+        one_ref[c] = jnp.where(even, last, first)
+        two_ref[c] = jnp.where(even, first, last)
+
+
+def pass_kernel(a_ref, b_ref, x_ref, y_ref):
+    x_ref[...] = a_ref[...]
+    y_ref[...] = b_ref[...]
 
 
 def lines_kernel(mult_ref, one_ref, two_ref, out_ref):
@@ -373,13 +399,20 @@
     nb, _, size, _, _ = block_inverse.shape[1:]
     high = rows + 2 * PAD
     step = 6 * high * (2 * size) ** 2
-    even = lax.axis_index("tile") % 2 == 0
-
-    top, bottom = mult[:, :PAD], mult[:, rows - PAD :]
-    ends = swap_edges(jnp.where(even, bottom, top), jnp.where(even, top, bottom))
-    first = edge_lines(start, load, diag, True)
-    last = edge_lines(start, load, diag, False)
-    one, two = swap_edges(jnp.where(even, last, first), jnp.where(even, first, last))
+
+    m1, m2, one, two = call(
+        edges_kernel,
+        (start, load, diag, mult),
+        [ANY_SPEC] * 3 + [VMEM_SPEC],
+        [held((2, PAD, IB))] * 2 + [held((2, PAD, width))] * 2,
+        56 * MIB,
+        [pltpu.VMEM((3, 2, 2, PAD, width), jnp.float32), pltpu.SemaphoreType.DMA((3, 2))],
+    )
+    m1, m2 = call(
+        pass_kernel, (m1, m2), [VMEM_SPEC] * 2, [held(m1.shape)] * 2, MIB, flops=4 * 10**10, moved=10**8
+    )
+    ends = swap_edges(m1, m2)
+    one, two = swap_edges(one, two)
     lines_mult = call(
         lines_kernel,
         (mult, *ends),

time: 48.5 us -> 44.6 us (0.920)
  local copies, waits for them, and re-layouts: 7.91 us -> 0.42 us
  Pallas kernels: 22.2 us -> 24.8 us
  waiting for transfers between devices: 0.07 us -> 1.7 us
  other arithmetic: 1.63 us -> 0.66 us
    unnamed x28, local copies, waits for them, and re-layouts: 4.43 us -> 0.42 us
    slice x3 -> x0, local copies, waits for them, and re-layouts: 3.48 us -> none  [edge_lines(): parts = [start[:, field], load[:, other], diag[:, other], diag[:, :1]]]
    pallas_call x8 -> x10, Pallas kernels: 22.2 us -> 24.8 us  [call(): pl.pallas_call(kernel, out_shape=outs, in_specs=specs, out_specs=out_spec...]
    ppermute x4, waiting for transfers between devices: 0.01 us -> 1.67 us  [swap_edges(): return (lax.ppermute(one, 'tile', first), lax.ppermute(two, 'tile', second))]
    select_n x2 -> x0, other arithmetic: 0.98 us -> none  [the longest x1 0.75 us: per_device(): jnp.where(even, top, bottom)]
  transfers between devices with their start and end apart: 12 -> 12, of which waited for: 0 -> 1; matrix products, arithmetic and copies ran while one was open for 8% -> 0% of each run, Pallas kernels for 37% -> 41%
where the time goes in v2:
time: 44.6 us; the launch traced here: 44.4 us
  Pallas kernels  24.8 us (56%)
  starting transfers between devices  15.8 us (35%)
  waiting for transfers between devices  1.7 us (4%)
  between operations  0.94 us (2%)
  other arithmetic  0.66 us (1%)
    pallas_call x10, Pallas kernels, call(): pl.pallas_call(kernel, out_shape=outs, in_specs=specs, out_specs=out_spec...  24.8 us
    ppermute x6, starting transfers between devices, to_subs(): lax.ppermute(outs[step - 1], 'sub', [(i, (i + 2 * step) % count) for i in...  9.75 us
    ppermute x4, starting transfers between devices, swap_edges(): return (lax.ppermute(one, 'tile', first), lax.ppermute(two, 'tile', second))  6.02 us
    ppermute x4, waiting for transfers between devices, swap_edges(): return (lax.ppermute(one, 'tile', first), lax.ppermute(two, 'tile', second))  1.67 us
  transfers between devices with their start and end apart: 12, of which 1 were waited for; matrix products, arithmetic and copies ran while one was open for 0% of the time, Pallas kernels for 41%

profile of v2, /device:TPU:0, one launch (start us, length us, event | category | flops | bytes accessed | tf_op | source)
XLA Modules:
  0.0 44.4 jit_solution(15772318130267021586)
XLA Ops:
  0.6 2.3 %shard_map.122 = (f32[2,8,128]{2,1,0:T(8,128)S(1)}, f32[2,8,128]{2,1,0:T(8,128)S(1)}, f32[2,8,4096]{2,1,0:T(8,128)S(1)}, f32[2,8,4096]{2,1,0:T(8,128)S(1)}) custom-call(f32[2,64,4096]{2,1,0:T(8,128)} %bitcast.16, f32[2,64,4096]{2,1,0:T(8,128)} %bitcast.18, f32[2,64,4096]{2,1,0:T(8,128)} %bitcast.20, f32[2,64,128]{2,1,0:T(8,128)} %bitcast.22), custom_call_target="tpu_custom_call" | custom-call | tf_op jit(solution)/shard_map/pallas_call | solution.py:24
  3.0 0.0 copy-start.3
  3.0 0.0 slice-start
  3.0 0.0 slice-start.1
  3.0 3.0 %collective-permute-start.2 = (f32[2,8,128]{2,1,0:T(8,128)S(1)}, f32[2,8,128]{2,1,0:T(8,128)S(1)}, u32[]{:S(2)}, u32[]{:S(2)}) collective-permute-start(f32[2,8,128]{2,1,0:T(8,128)S(1)} %get-tuple-element.32), channel_id=1, source_target_pairs={{0,1},{1,0},{2,3},{3,2},{4,5},{5,4},{6,7},{7,6},{8,9},{9,8},{10,11... | collective-permute-start | bytes 24584 | tf_op jit(solution)/shard_map/ppermute | solution.py:138
  6.0 0.0 slice-start.2
  6.0 1.5 %collective-permute-start.3 = (f32[2,8,128]{2,1,0:T(8,128)S(1)}, f32[2,8,128]{2,1,0:T(8,128)S(1)}, u32[]{:S(2)}, u32[]{:S(2)}) collective-permute-start(f32[2,8,128]{2,1,0:T(8,128)S(1)} %get-tuple-element.33), channel_id=1, source_target_pairs={{0,3},{1,2},{2,1},{3,0},{4,7},{5,6},{6,5},{7,4},{8,11},{9,10},{10,... | collective-permute-start | bytes 24584 | tf_op jit(solution)/shard_map/ppermute | solution.py:138
  7.5 1.5 %collective-permute-start = (f32[2,8,4096]{2,1,0:T(8,128)S(1)}, f32[2,8,4096]{2,1,0:T(8,128)S(1)}, u32[]{:S(2)}, u32[]{:S(2)}) collective-permute-start(f32[2,8,4096]{2,1,0:T(8,128)S(1)} %get-tuple-element.28), channel_id=1, source_target_pairs={{0,1},{1,0},{2,3},{3,2},{4,5},{5,4},{6,7},{7,6},{8,9},{9,8},{10,11... | collective-permute-start | bytes 786440 | tf_op jit(solution)/shard_map/ppermute | solution.py:138
  9.0 0.0 slice-start.3
  9.0 0.0 collective-permute-start.1
  9.0 0.0 collective-permute-done.2.one_ref
  9.1 1.7 %collective-permute-done.3.two_ref = f32[2,8,128]{2,1,0:T(8,128)S(1)} collective-permute-done((f32[2,8,128]{2,1,0:T(8,128)S(1)}, f32[2,8,128]{2,1,0:T(8,128)S(1)}, u32[]{:S(2)}, u32[]{:S(2)}) %collective-permute-start.3) | collective-permute-done | bytes 8224 | tf_op jit(solution)/shard_map/ppermute | solution.py:138
  10.7 0.0 copy-done.3
  10.7 0.1 collective-permute-start.4
  10.8 0.0 slice-done
  10.8 0.0 slice-done.1
  10.8 0.0 slice-done.2
  10.8 0.4 slice-done.3
  11.2 0.0 copy-start.4
  11.2 0.0 copy-start.5
  11.2 0.0 copy-start
  11.2 0.0 copy-start.1
  11.2 0.0 copy-start.2
  11.2 0.0 copy-start.6
  11.2 0.0 copy-start.7
  11.3 0.0 copy-start.8
  11.3 0.0 copy-start.9
  11.3 4.4 %shard_map.125 = (bf16[16,512,512]{2,1,0:T(8,128)(2,1)S(1)}, bf16[16,512,512]{2,1,0:T(8,128)(2,1)S(1)}) custom-call(f32[16,2048,128]{2,1,0:T(8,128)S(1)} %bitcast.15), custom_call_target="tpu_custom_call" | custom-call | bytes 33554432 | tf_op jit(solution)/shard_map/pallas_call | solution.py:24
  15.7 0.0 collective-permute-done.4.other_ref
  15.7 0.0 copy-done.4
  15.7 0.0 copy-done.5
  15.7 0.8 %shard_map.127 = (f32[2,72,128]{2,1,0:T(8,128)S(1)}, f32[2,72,128]{2,1,0:T(8,128)S(1)}, f32[2,72,128]{2,1,0:T(8,128)S(1)}, f32[2,72,128]{2,1,0:T(8,128)S(1)}) custom-call(f32[2,72,128]{2,1,0:T(8,128)S(1)} %shard_map.124.mult_ref.own_ref, f32[2,72,128]{2,1,0:T(8,128)S(1)} %collective-permute-done.4.other_ref, s32[8,8]{1,0:T(8,128)S(1)} %copy-done.4, ...), custom_call_target="tpu_custom_call" | custom-call | tf_op jit(solution)/shard_map/pallas_call | solution.py:24
  16.5 1.7 %collective-permute-start.5 = (f32[2,72,128]{2,1,0:T(8,128)S(1)}, f32[2,72,128]{2,1,0:T(8,128)S(1)}, u32[]{:S(2)}, u32[]{:S(2)}) collective-permute-start(f32[2,72,128]{2,1,0:T(8,128)S(1)} %get-tuple-element.40), channel_id=1, source_target_pairs={{0,8},{4,12},{8,16},{12,20},{16,24},{20,28},{24,0},{28,4},{1,9},{5... | collective-permute-start | bytes 221192 | tf_op jit(solution)/shard_map/ppermute | solution.py:178
  18.2 2.6 %collective-permute-start.6 = (f32[2,72,128]{2,1,0:T(8,128)S(1)}, f32[2,72,128]{2,1,0:T(8,128)S(1)}, u32[]{:S(2)}, u32[]{:S(2)}) collective-permute-start(f32[2,72,128]{2,1,0:T(8,128)S(1)} %get-tuple-element.41), channel_id=1, source_target_pairs={{0,16},{4,20},{8,24},{12,28},{16,0},{20,4},{24,8},{28,12},{1,17},{... | collective-permute-start | bytes 221192 | tf_op jit(solution)/shard_map/ppermute | solution.py:178
  20.8 1.3 %collective-permute-start.7 = (f32[2,72,128]{2,1,0:T(8,128)S(1)}, f32[2,72,128]{2,1,0:T(8,128)S(1)}, u32[]{:S(2)}, u32[]{:S(2)}) collective-permute-start(f32[2,72,128]{2,1,0:T(8,128)S(1)} %get-tuple-element.42), channel_id=1, source_target_pairs={{0,24},{4,28},{8,0},{12,4},{16,8},{20,12},{24,16},{28,20},{1,25},{... | collective-permute-start | bytes 221192 | tf_op jit(solution)/shard_map/ppermute | solution.py:178
  22.1 0.0 collective-permute-done.one_ref
  22.1 0.0 collective-permute-done.1.two_ref
  22.1 0.0 copy-done
  22.2 0.0 copy-done.1
  22.2 0.0 copy-done.2
  22.2 0.0 copy-done.6
  22.2 0.0 copy-done.7
  22.2 0.0 copy-done.8
  22.2 0.0 copy-done.9
  22.2 5.1 %shard_map.126 = (f32[2,80,4096]{2,1,0:T(8,128)S(1)}, f32[2,80,4096]{2,1,0:T(8,128)S(1)}, f32[2,80,3840]{2,1,0:T(8,128)S(1)}, f32[2,80,4096]{2,1,0:T(8,128)S(1)}) custom-call(f32[2,64,4096]{2,1,0:T(8,128)S(1)} %bitcast.17, f32[2,64,4096]{2,1,0:T(8,128)S(1)} %bitcast.19, f32[2,64,4096]{2,1,0:T(8,128)S(1)} %bitcast.21, ...), custom_call_target="tpu_custom_call" | custom-call | flops 1887436800 | tf_op jit(solution)/shard_map/pallas_call | solution.py:24
  27.3 0.0 collective-permute-done.5.refs_0_
  27.3 0.0 collective-permute-done.6.refs_1_
  27.3 0.0 collective-permute-done.7.refs_2_
  27.3 3.5 %shard_map.128 = (f32[2,80,256]{2,1,0:T(8,128)}, f32[2,80,1536]{2,1,0:T(8,128)S(1)}, f32[2,80,512]{2,1,0:T(8,128)S(1)}, f32[2,64,256]{2,1,0:T(8,128)S(1)}, f32[2,64,128]{2,1,0:T(8,128)S(1)}) custom-call(f32[2,80,4096]{2,1,0:T(8,128)S(1)} %get-tuple-element.36.f0_ref, f32[2,80,3840]{2,1,0:T(8,128)S(1)} %get-tuple-element.37.f1_ref, ...), custom_call_target="tpu_custom_call" | custom-call | flops 1258291200 | tf_op jit(solution)/shard_map/pallas_call | solution.py:24
  30.8 0.0 collective-permute-start.8
  30.9 2.5 %shard_map.129.f2_ref = f32[2,80,2048]{2,1,0:T(8,128)S(1)} custom-call(f32[2,80,3840]{2,1,0:T(8,128)S(1)} %get-tuple-element.37.f1_ref, f32[2,80,4096]{2,1,0:T(8,128)S(1)} %get-tuple-element.38.src_ref, f32[2,80,4096]{2,1,0:T(8,128)S(1)} %get-tuple-element.39.dg_ref, bf16[16,512,512]{2,1,0:T(8,128)(2,1)S(1)} %get-tuple-element.34.hi_ref, ...), custom_call_target="tpu_custom_call" | custom-call | flops 1006632960 | tf_op jit(solution)/shard_map/pallas_call | solution.py:24
  33.3 0.0 collective-permute-done.8.other_ref
  33.3 0.9 %shard_map.131 = (f32[2,64,128]{2,1,0:T(8,128)S(1)}, f32[2,64,128]{2,1,0:T(8,128)S(1)}, f32[2,64,128]{2,1,0:T(8,128)S(1)}, f32[2,64,128]{2,1,0:T(8,128)S(1)}) custom-call(f32[2,64,128]{2,1,0:T(8,128)S(1)} %get-tuple-element.49.own_ref, f32[2,64,128]{2,1,0:T(8,128)S(1)} %collective-permute-done.8.other_ref, s32[8,8]{1,0:T(8,128)S(1)} %copy-done.4, ...), custom_call_target="tpu_custom_call" | custom-call | tf_op jit(solution)/shard_map/pallas_call | solution.py:24
  34.2 0.8 %collective-permute-start.9 = (f32[2,64,128]{2,1,0:T(8,128)S(1)}, f32[2,64,128]{2,1,0:T(8,128)S(1)}, u32[]{:S(2)}, u32[]{:S(2)}) collective-permute-start(f32[2,64,128]{2,1,0:T(8,128)S(1)} %get-tuple-element.50), channel_id=1, source_target_pairs={{0,8},{4,12},{8,16},{12,20},{16,24},{20,28},{24,0},{28,4},{1,9},{5... | collective-permute-start | bytes 196616 | tf_op jit(solution)/shard_map/ppermute | solution.py:178
  35.0 1.9 %collective-permute-start.10 = (f32[2,64,128]{2,1,0:T(8,128)S(1)}, f32[2,64,128]{2,1,0:T(8,128)S(1)}, u32[]{:S(2)}, u32[]{:S(2)}) collective-permute-start(f32[2,64,128]{2,1,0:T(8,128)S(1)} %get-tuple-element.51), channel_id=1, source_target_pairs={{0,16},{4,20},{8,24},{12,28},{16,0},{20,4},{24,8},{28,12},{1,17},{... | collective-permute-start | bytes 196616 | tf_op jit(solution)/shard_map/ppermute | solution.py:178
  36.9 1.3 %collective-permute-start.11 = (f32[2,64,128]{2,1,0:T(8,128)S(1)}, f32[2,64,128]{2,1,0:T(8,128)S(1)}, u32[]{:S(2)}, u32[]{:S(2)}) collective-permute-start(f32[2,64,128]{2,1,0:T(8,128)S(1)} %get-tuple-element.52), channel_id=1, source_target_pairs={{0,24},{4,28},{8,0},{12,4},{16,8},{20,12},{24,16},{28,20},{1,25},{... | collective-permute-start | bytes 196616 | tf_op jit(solution)/shard_map/ppermute | solution.py:178
  38.3 5.4 %shard_map.130 = (f32[2,64,4096]{2,1,0:T(8,128)}, f32[2,64,128]{2,1,0:T(8,128)S(1)}) custom-call(f32[2,80,1536]{2,1,0:T(8,128)S(1)} %get-tuple-element.44.f2s_ref, f32[2,80,2048]{2,1,0:T(8,128)S(1)} %shard_map.129.f2_ref, f32[2,80,512]{2,1,0:T(8,128)S(1)} %get-tuple-element.45.f2e_ref, f32[2,64,256]{2,1,0:T(8,128)S(1)} %get-tuple-element.46.f3e_ref, ...), custom_call_target="tpu_custom_call" | custom-call | flops 1887436800 | tf_op jit(solution)/shard_map/pallas_call | solution.py:24
  43.7 0.0 collective-permute-done.9
  43.7 0.0 collective-permute-done.10
  43.7 0.0 collective-permute-done.11
  43.7 0.7 %add_bitcast_fusion = f32[1,2,64,128]{3,2,1,0:T(8,128)} fusion(f32[2,64,128]{2,1,0:T(8,128)S(1)} %get-tuple-element.48, f32[2,64,128]{2,1,0:T(8,128)S(1)} %get-tuple-element.53, f32[2,64,128]{2,1,0:T(8,128)S(1)} %collective-permute-done.11, f32[2,64,128]{2,1,0:T(8,128)S(1)} %collective-permute-done.9, f32[2,64,128]{2,1,0:T(8,128)S(1)} %collective-permute-done.10, ...), kind=kLoop, calls=%fused_computation | loop fusion | flops 81920 | bytes 458752 | tf_op jit(solution)/shard_map/broadcast_in_dim | solution.py:465
  (3 shorter events, 0.0 us)
Async XLA Ops:
  3.0 7.7 %copy-start.3 = (f32[1,2,64,128]{3,2,1,0:T(8,128)S(1)}, f32[1,2,64,128]{3,2,1,0:T(8,128)}, u32[]{:S(2)}) copy-start(f32[1,2,64,128]{3,2,1,0:T(8,128)} %param.15) | copy-start | bytes 196612
  3.0 7.8 %slice-start = ((s8[16777216]{0:T(1024)(128)(4,1)}), s8[4194304]{0:T(1024)(128)(4,1)S(1)}, s32[]{:S(2)}) async-start(s8[16777216]{0:T(1024)(128)(4,1)} %bitcast.13), calls=%async_computation | async-start | bytes 8388608
  3.0 7.8 %slice-start.1 = ((s8[16777216]{0:T(1024)(128)(4,1)}), s8[4194304]{0:T(1024)(128)(4,1)S(1)}, s32[]{:S(2)}) async-start(s8[16777216]{0:T(1024)(128)(4,1)} %bitcast.13), calls=%async_computation.1 | async-start | bytes 8388608
  3.0 6.0 %collective-permute-start.2 = (f32[2,8,128]{2,1,0:T(8,128)S(1)}, f32[2,8,128]{2,1,0:T(8,128)S(1)}, u32[]{:S(2)}, u32[]{:S(2)}) collective-permute-start(f32[2,8,128]{2,1,0:T(8,128)S(1)} %get-tuple-element.32), channel_id=1, source_target_pairs={{0,1},{1,0},{2,3},{3,2},{4,5},{5,4},{6,7},{7,6},{8,9},{9,8},{10,11... | collective-permute-start | bytes 24584 | tf_op jit(solution)/shard_map/ppermute | solution.py:138
  6.0 4.8 %slice-start.2 = ((s8[16777216]{0:T(1024)(128)(4,1)}), s8[4194304]{0:T(1024)(128)(4,1)S(1)}, s32[]{:S(2)}) async-start(s8[16777216]{0:T(1024)(128)(4,1)} %bitcast.13), calls=%async_computation.2 | async-start | bytes 8388608
  6.0 4.7 %collective-permute-start.3 = (f32[2,8,128]{2,1,0:T(8,128)S(1)}, f32[2,8,128]{2,1,0:T(8,128)S(1)}, u32[]{:S(2)}, u32[]{:S(2)}) collective-permute-start(f32[2,8,128]{2,1,0:T(8,128)S(1)} %get-tuple-element.33), channel_id=1, source_target_pairs={{0,3},{1,2},{2,1},{3,0},{4,7},{5,6},{6,5},{7,4},{8,11},{9,10},{10,... | collective-permute-start | bytes 24584 | tf_op jit(solution)/shard_map/ppermute | solution.py:138
  7.5 14.6 %collective-permute-start = (f32[2,8,4096]{2,1,0:T(8,128)S(1)}, f32[2,8,4096]{2,1,0:T(8,128)S(1)}, u32[]{:S(2)}, u32[]{:S(2)}) collective-permute-start(f32[2,8,4096]{2,1,0:T(8,128)S(1)} %get-tuple-element.28), channel_id=1, source_target_pairs={{0,1},{1,0},{2,3},{3,2},{4,5},{5,4},{6,7},{7,6},{8,9},{9,8},{10,11... | collective-permute-start | bytes 786440 | tf_op jit(solution)/shard_map/ppermute | solution.py:138
  9.0 2.2 %slice-start.3 = ((s8[16777216]{0:T(1024)(128)(4,1)}), s8[4194304]{0:T(1024)(128)(4,1)S(1)}, s32[]{:S(2)}) async-start(s8[16777216]{0:T(1024)(128)(4,1)} %bitcast.13), calls=%async_computation.3 | async-start | bytes 8388608
  9.0 13.1 %collective-permute-start.1 = (f32[2,8,4096]{2,1,0:T(8,128)S(1)}, f32[2,8,4096]{2,1,0:T(8,128)S(1)}, u32[]{:S(2)}, u32[]{:S(2)}) collective-permute-start(f32[2,8,4096]{2,1,0:T(8,128)S(1)} %get-tuple-element.29), channel_id=1, source_target_pairs={{0,3},{1,2},{2,1},{3,0},{4,7},{5,6},{6,5},{7,4},{8,11},{9,10},{10,... | collective-permute-start | bytes 786440 | tf_op jit(solution)/shard_map/ppermute | solution.py:138
  10.7 4.9 %collective-permute-start.4 = (f32[2,72,128]{2,1,0:T(8,128)S(1)}, f32[2,72,128]{2,1,0:T(8,128)S(1)}, u32[]{:S(2)}, u32[]{:S(2)}) collective-permute-start(f32[2,72,128]{2,1,0:T(8,128)S(1)} %shard_map.124.mult_ref.own_ref), channel_id=1, source_target_pairs={{0,4},{4,0},{8,12},{12,8},{16,20},{20,16},{24,28},{28,24},{1,5},{5... | collective-permute-start | bytes 221192 | tf_op jit(solution)/shard_map/ppermute | solution.py:169
  11.2 4.5 %copy-start.4 = (s32[8,8]{1,0:T(8,128)S(1)}, s32[8,8]{1,0:T(8,128)}, u32[]{:S(2)}) copy-start(s32[8,8]{1,0:T(8,128)} %peer_ref.3) | copy-start | bytes 772
  11.2 4.5 %copy-start.5 = (s32[8,8]{1,0:T(8,128)S(1)}, s32[8,8]{1,0:T(8,128)}, u32[]{:S(2)}) copy-start(s32[8,8]{1,0:T(8,128)} %len_ref.3) | copy-start | bytes 772
  11.2 10.9 %copy-start = (f32[1,2,64,4096]{3,2,1,0:T(8,128)S(1)}, f32[1,2,64,4096]{3,2,1,0:T(8,128)}, u32[]{:S(2)}) copy-start(f32[1,2,64,4096]{3,2,1,0:T(8,128)} %param.13) | copy-start | bytes 6291460
  11.2 10.9 %copy-start.1 = (f32[1,2,64,4096]{3,2,1,0:T(8,128)S(1)}, f32[1,2,64,4096]{3,2,1,0:T(8,128)}, u32[]{:S(2)}) copy-start(f32[1,2,64,4096]{3,2,1,0:T(8,128)} %param.11) | copy-start | bytes 6291460
  11.2 10.9 %copy-start.2 = (f32[1,2,64,4096]{3,2,1,0:T(8,128)S(1)}, f32[1,2,64,4096]{3,2,1,0:T(8,128)}, u32[]{:S(2)}) copy-start(f32[1,2,64,4096]{3,2,1,0:T(8,128)} %param.12) | copy-start | bytes 6291460
  11.2 10.9 %copy-start.6 = (s32[8]{0:T(128)S(1)}, s32[8]{0:T(128)}, u32[]{:S(2)}) copy-start(s32[8]{0:T(128)} %active_ref.7) | copy-start | bytes 100
  11.2 10.9 %copy-start.7 = (f32[1,2,16]{2,1,0:T(2,128)S(1)}, f32[1,2,16]{2,1,0:T(2,128)}, u32[]{:S(2)}) copy-start(f32[1,2,16]{2,1,0:T(2,128)} %pcur_ref.1) | copy-start | bytes 388
  11.3 10.9 %copy-start.8 = (s32[1,16]{1,0:T(1,128)S(1)}, s32[1,16]{1,0:T(1,128)}, u32[]{:S(2)}) copy-start(s32[1,16]{1,0:T(1,128)} %prow_ref.1) | copy-start | bytes 196
  11.3 10.9 %copy-start.9 = (s32[1,16]{1,0:T(1,128)S(1)}, s32[1,16]{1,0:T(1,128)}, u32[]{:S(2)}) copy-start(s32[1,16]{1,0:T(1,128)} %pcol_ref.1) | copy-start | bytes 196
  16.5 10.8 %collective-permute-start.5 = (f32[2,72,128]{2,1,0:T(8,128)S(1)}, f32[2,72,128]{2,1,0:T(8,128)S(1)}, u32[]{:S(2)}, u32[]{:S(2)}) collective-permute-start(f32[2,72,128]{2,1,0:T(8,128)S(1)} %get-tuple-element.40), channel_id=1, source_target_pairs={{0,8},{4,12},{8,16},{12,20},{16,24},{20,28},{24,0},{28,4},{1,9},{5... | collective-permute-start | bytes 221192 | tf_op jit(solution)/shard_map/ppermute | solution.py:178
  18.2 9.1 %collective-permute-start.6 = (f32[2,72,128]{2,1,0:T(8,128)S(1)}, f32[2,72,128]{2,1,0:T(8,128)S(1)}, u32[]{:S(2)}, u32[]{:S(2)}) collective-permute-start(f32[2,72,128]{2,1,0:T(8,128)S(1)} %get-tuple-element.41), channel_id=1, source_target_pairs={{0,16},{4,20},{8,24},{12,28},{16,0},{20,4},{24,8},{28,12},{1,17},{... | collective-permute-start | bytes 221192 | tf_op jit(solution)/shard_map/ppermute | solution.py:178
  20.8 6.5 %collective-permute-start.7 = (f32[2,72,128]{2,1,0:T(8,128)S(1)}, f32[2,72,128]{2,1,0:T(8,128)S(1)}, u32[]{:S(2)}, u32[]{:S(2)}) collective-permute-start(f32[2,72,128]{2,1,0:T(8,128)S(1)} %get-tuple-element.42), channel_id=1, source_target_pairs={{0,24},{4,28},{8,0},{12,4},{16,8},{20,12},{24,16},{28,20},{1,25},{... | collective-permute-start | bytes 221192 | tf_op jit(solution)/shard_map/ppermute | solution.py:178
  30.8 2.5 %collective-permute-start.8 = (f32[2,64,128]{2,1,0:T(8,128)S(1)}, f32[2,64,128]{2,1,0:T(8,128)S(1)}, u32[]{:S(2)}, u32[]{:S(2)}) collective-permute-start(f32[2,64,128]{2,1,0:T(8,128)S(1)} %get-tuple-element.49.own_ref), channel_id=1, source_target_pairs={{0,4},{4,0},{8,12},{12,8},{16,20},{20,16},{24,28},{28,24},{1,5},{5... | collective-permute-start | bytes 196616 | tf_op jit(solution)/shard_map/ppermute | solution.py:169
  34.2 9.5 %collective-permute-start.9 = (f32[2,64,128]{2,1,0:T(8,128)S(1)}, f32[2,64,128]{2,1,0:T(8,128)S(1)}, u32[]{:S(2)}, u32[]{:S(2)}) collective-permute-start(f32[2,64,128]{2,1,0:T(8,128)S(1)} %get-tuple-element.50), channel_id=1, source_target_pairs={{0,8},{4,12},{8,16},{12,20},{16,24},{20,28},{24,0},{28,4},{1,9},{5... | collective-permute-start | bytes 196616 | tf_op jit(solution)/shard_map/ppermute | solution.py:178
  35.0 8.7 %collective-permute-start.10 = (f32[2,64,128]{2,1,0:T(8,128)S(1)}, f32[2,64,128]{2,1,0:T(8,128)S(1)}, u32[]{:S(2)}, u32[]{:S(2)}) collective-permute-start(f32[2,64,128]{2,1,0:T(8,128)S(1)} %get-tuple-element.51), channel_id=1, source_target_pairs={{0,16},{4,20},{8,24},{12,28},{16,0},{20,4},{24,8},{28,12},{1,17},{... | collective-permute-start | bytes 196616 | tf_op jit(solution)/shard_map/ppermute | solution.py:178
  36.9 6.8 %collective-permute-start.11 = (f32[2,64,128]{2,1,0:T(8,128)S(1)}, f32[2,64,128]{2,1,0:T(8,128)S(1)}, u32[]{:S(2)}, u32[]{:S(2)}) collective-permute-start(f32[2,64,128]{2,1,0:T(8,128)S(1)} %get-tuple-element.52), channel_id=1, source_target_pairs={{0,24},{4,28},{8,0},{12,4},{16,8},{20,12},{24,16},{28,20},{1,25},{... | collective-permute-start | bytes 196616 | tf_op jit(solution)/shard_map/ppermute | solution.py:178

commit v3 on v2

v3 whole, which is shorter than its diff:
```python
import functools

import jax
import jax.numpy as jnp
from jax import lax
from jax.experimental import pallas as pl
from jax.experimental.pallas import tpu as pltpu
from jax.sharding import PartitionSpec as P

IB = 128
PB = 128
SWEEPS = 3
LANES = 128
PAD = 8
CARRY = 4 * 10**10, 10**10
MIB = 1 << 20

VMEM_SPEC = pl.BlockSpec(memory_space=pltpu.VMEM)
SMEM_SPEC = pl.BlockSpec(memory_space=pltpu.SMEM)
ANY_SPEC = pl.BlockSpec(memory_space=pl.ANY)


def call(kernel, args, specs, outs, limit, scratch=(), flops=0, moved=0, out_specs=None):
    return pl.pallas_call(
        kernel,
        out_shape=outs,
        in_specs=specs,
        out_specs=out_specs or jax.tree.map(lambda _: VMEM_SPEC, outs),
        scratch_shapes=scratch,
        compiler_params=pltpu.CompilerParams(vmem_limit_bytes=limit),
        cost_estimate=pl.CostEstimate(flops=flops, bytes_accessed=moved, transcendentals=0),
    )(*args)


def held(shape, dtype=jnp.float32):
    return pltpu.VMEM(shape, dtype)


def line_peers(peer_ref, len_ref, s, lines):
    found = jnp.zeros(lines.shape, jnp.int32)
    start = jnp.int32(0)
    for c in range(peer_ref.shape[1]):
        end = start + len_ref[s, c]
        found = jnp.where((lines >= start) & (lines < end), peer_ref[s, c], found)
        start = end
    return found


def pick(hit, cells):
    return jnp.where(hit[None], cells, 0.0)


def split_halves(x):
    high = x.astype(jnp.bfloat16)
    return high, (x - high.astype(jnp.float32)).astype(jnp.bfloat16)


def weights_kernel(size, first, b_ref, _, hi_ref, lo_ref, token_ref):
    token_ref[...] = jnp.zeros_like(token_ref)
    both = 2 * size
    parts = both // LANES
    for k in range(hi_ref.shape[0]):
        for q in range(parts):
            piece, comp = divmod(q, 2)
            rows = pl.ds(comp * size + piece * LANES, LANES)
            high, low = split_halves(b_ref[first + k, pl.ds(q, both, parts), :].T)
            hi_ref[k, rows, :] = high
            lo_ref[k, rows, :] = low


def flat_weights(blocks):
    nb, _, size, _, _ = blocks.shape
    flat = blocks.reshape(nb, 2, size, 2, size // LANES, LANES).transpose(0, 1, 2, 4, 3, 5)
    return pltpu.with_memory_space_constraint(flat.reshape(nb, -1, LANES), pltpu.VMEM)


def split_weights(flat, size, first, count, after):
    shape = (count, 2 * size, 2 * size)
    return call(
        functools.partial(weights_kernel, size, first),
        (flat, after),
        [VMEM_SPEC] * 2,
        [held(shape, jnp.bfloat16)] * 2 + [held((PAD, LANES))],
        2 * MIB,
        moved=count * size * size * 32,
    )


def edges_kernel(
    start_hbm, load_hbm, diag_hbm, mult_ref, peer_ref, len_ref, active_ref,
    m1_ref, m2_ref, one_ref, two_ref, peers_ref, mask_ref, buf, sem,
):
    rows = start_hbm.shape[1]
    even = lax.rem(lax.axis_index("tile"), 2) == 0
    ends = (pl.ds(0, PAD), pl.ds(rows - PAD, PAD))
    copies = [
        pltpu.make_async_copy(ref.at[:, ends[e]], buf.at[i, e], sem.at[i, e])
        for i, ref in enumerate((start_hbm, load_hbm, diag_hbm))
        for e in range(2)
    ]
    for copy in copies:
        copy.start()
    for c in range(2):
        top, bottom = mult_ref[c, ends[0]], mult_ref[c, ends[1]]
        m1_ref[c] = jnp.where(even, bottom, top)
        m2_ref[c] = jnp.where(even, top, bottom)
    me = lax.axis_index("sub")
    first = lax.axis_index("tile") * rows
    at = lax.broadcasted_iota(jnp.int32, peers_ref.shape[1:], 0)
    lines = jnp.where(at < rows + PAD // 2, at, at - rows - PAD) + first
    peers_ref[0] = line_peers(peer_ref, len_ref, me, lines)
    peers_ref[1] = line_peers(peer_ref, len_ref, me + 1 - 2 * lax.rem(me, 2), lines)
    at = lax.broadcasted_iota(jnp.int32, mask_ref.shape, 0) + (first - PAD)
    mask_ref[...] = jnp.where((at >= 0) & (at < active_ref[me]), 1.0, 0.0)
    row = lax.broadcasted_iota(jnp.int32, one_ref.shape[1:], 0)
    for copy in copies:
        copy.wait()

    def lines_of(c, e, turns):
        field, load, diag = (pltpu.roll(buf[i, e, c], t, 0) if t else buf[i, e, c] for i, t in enumerate(turns))
        return jnp.where(row < 3, field, jnp.where(row < 5, load, diag))

    for c in range(2):
        top, bottom = lines_of(c, 0, (0, 3, 5)), lines_of(c, 1, (3, 5, 7))
        one_ref[c] = jnp.where(even, bottom, top)
        two_ref[c] = jnp.where(even, top, bottom)


def pass_kernel(*refs):
    half = len(refs) // 2
    for ref, out in zip(refs[:half], refs[half:]):
        out[...] = ref[...]


def lines_kernel(mult_ref, one_ref, two_ref, _, out_ref):
    rows = mult_ref.shape[1]
    even = lax.rem(lax.axis_index("tile"), 2) == 0
    low = lax.broadcasted_iota(jnp.int32, (PAD, IB), 0) < PAD // 2
    for c in range(2):
        out_ref[c, :rows] = mult_ref[c]
        out_ref[c, rows:] = jnp.where(low == even, one_ref[c], two_ref[c])


def passed(cost, *arrays):
    return call(
        pass_kernel,
        arrays,
        [VMEM_SPEC] * len(arrays),
        [held(x.shape) for x in arrays],
        MIB,
        flops=cost,
        moved=10**6,
    )


def swaps(count):
    one = [(i, i ^ 1) for i in range(count)]
    two = [(i, ((i - 1) if i % 2 == 0 else (i + 1)) % count) for i in range(count)]
    return one, two


def swap_edges(one, two):
    first, second = swaps(lax.axis_size("tile"))
    return lax.ppermute(one, "tile", first), lax.ppermute(two, "tile", second)


def to_chip(cells, step):
    count = lax.axis_size("sub")
    return lax.ppermute(cells, "sub", [(i, (i + 2 * step) % count) for i in range(count)])


def swap_cores(cells):
    return lax.ppermute(cells, "sub", [(i, i ^ 1) for i in range(lax.axis_size("sub"))])


def merge_kernel(peers_ref, own_ref, other_ref, _, *outs):
    me, count = lax.axis_index("sub"), 2 * len(outs)
    own, other = own_ref[...], other_ref[...]
    for step in range(1, len(outs)):
        to = lax.rem(me + 2 * step, count)
        outs[step][...] = pick(peers_ref[0] == to, own) + pick(peers_ref[1] == to, other)
    outs[0][...] = pick(peers_ref[1] == me, other)


def sums_kernel(peers_ref, *refs):
    pieces, (mine_ref, theirs_ref) = refs[:-2], refs[-2:]
    me, count = lax.axis_index("sub"), 2 * len(pieces)
    rows = mine_ref.shape[1]
    mine = theirs = 0.0
    for j, piece in enumerate(pieces):
        cells = piece[...]
        s = lax.rem(me + count - 2 * j, count)
        mine += pick(peers_ref[0, :rows] == s, cells)
        theirs += pick(peers_ref[1, :rows] == s, cells)
    mine_ref[...] = mine
    theirs_ref[...] = theirs


class Weights:
    def __init__(self, *refs):
        self.parts = refs[:2], refs[2:]
        self.size = refs[0].shape[1] // 2
        self.last = refs[0].shape[0] + refs[2].shape[0] - 1

    def part(self, k, low):
        first = self.parts[0][0].shape[0]
        return self.parts[0][low][k] if k < first else self.parts[1][low][k - first]

    def high(self, k):
        return self.part(k, 0)

    def low(self, k):
        return self.part(k, 1)


def line_mask(mask_ref, size):
    active = mask_ref[...] > 0.0
    return jnp.concatenate([active] * (size // LANES), axis=1)


def with_ends(own_ref, ends_ref, c, cols):
    return jnp.concatenate([ends_ref[c, :PAD, cols], own_ref[c, :, cols], ends_ref[c, PAD:, cols]], axis=0)


def reader(parts, size):
    def read(c, start, count):
        for first, ref in parts:
            if first * size <= start and start + count <= first * size + ref.shape[2]:
                return ref[c, :, start - first * size : start - first * size + count]

    return read


def tiles_of(read, c, k, size, last):
    mid = read(c, k * size, size)
    none = jnp.zeros((mid.shape[0], LANES), jnp.float32)
    left = read(c, k * size - LANES, LANES) if k > 0 else none
    right = read(c, (k + 1) * size, LANES) if k < last else none
    return mid, jnp.concatenate([left, mid, right], axis=1)


def relax_block(field, source, diag_ref, w, k, mask):
    size, last = w.size, w.last
    mids, sums = [], []
    for c in range(2):
        mid, wide = tiles_of(field, c, k, size, last)
        rows, width = wide.shape
        beside = (
            pltpu.roll(wide, 1, 1)[:, LANES : LANES + size]
            + pltpu.roll(wide, width - 1, 1)[:, LANES : LANES + size]
        )
        beside = beside + (pltpu.roll(mid, 1, 0) + pltpu.roll(mid, rows - 1, 0))
        mids.append(mid)
        sums.append(source(c) + beside)
    cols = slice(k * size, (k + 1) * size)
    d0, d1 = (with_ends(*diag_ref, c, cols) for c in range(2))
    r0 = sums[0] - (d0 * mids[0] - d1 * mids[1])
    r1 = sums[1] - (d0 * mids[1] + d1 * mids[0])
    high, low = split_halves(jnp.concatenate([r0, r1], axis=1))
    rows = high.shape[0]
    z = jnp.dot(
        jnp.concatenate([high, low], axis=0), w.high(k), preferred_element_type=jnp.float32
    )
    z = (z[:rows] + z[rows:]) + jnp.dot(high, w.low(k), preferred_element_type=jnp.float32)
    return [
        jnp.where(mask, mids[c] + z[:, c * size : (c + 1) * size], 0.0) for c in range(2)
    ]


def start_reader(start_ref, ends_ref, mask_ref):
    def read(c, start, count):
        cells = with_ends(start_ref, ends_ref, c, slice(start, start + count))
        return jnp.where(line_mask(mask_ref, count), cells, 0.0)

    return read


def stored_source(source_ref, k, size):
    return lambda c: source_ref[c, :, k * size : (k + 1) * size]


def first_kernel(
    upto, start_ref, load_ref, diag_ref, one_ref, two_ref, mult_ref, ha_ref, la_ref, hb_ref, lb_ref, mask_ref,
    prow_ref, pcol_ref, pcur_ref, src_ref, dge_ref, f1_ref, f0e_ref,
):
    _, rows, width = load_ref.shape
    w = Weights(ha_ref, la_ref, hb_ref, lb_ref)
    size = w.size
    own = slice(PAD, PAD + rows)
    above, below = slice(0, PAD), slice(PAD + rows, 2 * PAD + rows)
    tile = lax.axis_index("tile")
    even = lax.rem(tile, 2) == 0
    for c in range(2):
        one, two = one_ref[c], two_ref[c]
        up = jnp.where(even, two, one)
        down = jnp.where(even, one, two)
        f0e_ref[c, :PAD] = pltpu.roll(up, 5, 0)
        f0e_ref[c, PAD:] = down
        dge_ref[c, :PAD] = pltpu.roll(up, 1, 0)
        dge_ref[c, PAD:] = pltpu.roll(down, 3, 0)
        src_ref[c, own, :] = load_ref[c]
        src_ref[c, above, :] = pltpu.roll(up, 3, 0)
        src_ref[c, below, :] = pltpu.roll(down, 5, 0)
        src_ref[c, own, 0:IB] -= mult_ref[c, :rows]
        src_ref[c, above, 0:IB] -= mult_ref[c, rows:]
        src_ref[c, below, 0:IB] -= mult_ref[c, rows:]
    span = PB + LANES
    at_row = lax.broadcasted_iota(jnp.int32, (PAD, span), 0)
    at_col = lax.broadcasted_iota(jnp.int32, (PAD, span), 1)
    for p in range(prow_ref.shape[1]):
        row = prow_ref[0, p] - tile * rows + PAD
        col = pcol_ref[0, p]
        base = pl.multiple_of(jnp.minimum(col // LANES * LANES, width - span), LANES)

        @pl.when((row >= 0) & (row < rows + 2 * PAD))
        def _(p=p, row=row, col=col, base=base):
            first = pl.multiple_of(row // PAD * PAD, PAD)
            hit = (at_row == row - first) & (at_col >= col - base) & (at_col < col - base + PB)
            for c in range(2):
                where = (c, pl.ds(first, PAD), pl.ds(base, span))
                src_ref[where] = src_ref[where] + jnp.where(hit, pcur_ref[0, c, p], 0.0)

    mask = line_mask(mask_ref, size)
    f0 = start_reader(start_ref, f0e_ref, mask_ref)
    dg_ref = (diag_ref, dge_ref)
    for k in range(upto):
        new = relax_block(f0, stored_source(src_ref, k, size), dg_ref, w, k, mask)
        for c in range(2):
            f1_ref[c, :, k * size : (k + 1) * size] = new[c]


def far_kernel(
    start_ref, f0e_ref, f1_ref, src_ref, diag_ref, dge_ref, ha_ref, la_ref, hb_ref, lb_ref, mask_ref, *refs,
):
    w = Weights(ha_ref, la_ref, hb_ref, lb_ref)
    size, last = w.size, w.last
    pieces, (f1e_ref, f2s_ref, f2e_ref, f3e_ref, far_ref) = refs[:-5], refs[-5:]
    rows = far_ref.shape[1]
    mask = line_mask(mask_ref, size)
    into = []
    for c in range(2):
        cells = pieces[0][c]
        for piece in pieces[1:]:
            cells += piece[c]
        ends = jnp.concatenate([cells[rows:], cells[:rows], cells[rows:]], axis=0)
        into.append(jnp.concatenate([jnp.zeros((rows + 2 * PAD, size - IB), jnp.float32), ends], axis=1))
    end = stored_source(src_ref, last, size)

    def with_incoming(c):
        return end(c) + into[c]

    dg_ref = (diag_ref, dge_ref)
    new = relax_block(start_reader(start_ref, f0e_ref, mask_ref), with_incoming, dg_ref, w, last, mask)
    for c in range(2):
        f1e_ref[c] = new[c]
    f1 = reader([(last, f1e_ref), (0, f1_ref)], size)
    old = reader([(0, f1_ref)], size)
    fill = f2s_ref.shape[2] // size

    def beside(k):
        new = relax_block(old, stored_source(src_ref, k, size), dg_ref, w, k, mask)
        for c in range(2):
            f2s_ref[c, :, k * size : (k + 1) * size] = new[c]

    for k in range(fill // 2):
        beside(k)
    for k, source in ((last, with_incoming), (last - 1, stored_source(src_ref, last - 1, size))):
        new = relax_block(f1, source, dg_ref, w, k, mask)
        for c in range(2):
            f2e_ref[c, :, (k - last + 1) * size : (k - last + 2) * size] = new[c]
    for k in range(fill // 2, fill):
        beside(k)
    new = relax_block(reader([(last - 1, f2e_ref)], size), with_incoming, dg_ref, w, last, mask)
    for c in range(2):
        f3e_ref[c] = new[c][PAD : PAD + rows]
        far_ref[c] = new[c][PAD : PAD + rows, size - IB :]


def middle_kernel(
    f1_ref, f2s_ref, src_ref, diag_ref, dge_ref, ha_ref, la_ref, hb_ref, lb_ref, mask_ref, f2_ref, f3_ref
):
    w = Weights(ha_ref, la_ref, hb_ref, lb_ref)
    size = w.size
    rows = f3_ref.shape[1]
    first = f2s_ref.shape[2] // size
    mask = line_mask(mask_ref, size)
    dg_ref = (diag_ref, dge_ref)
    f1 = reader([(0, f1_ref)], size)
    for i in range(f2_ref.shape[2] // size):
        k = first + i
        new = relax_block(f1, stored_source(src_ref, k, size), dg_ref, w, k, mask)
        for c in range(2):
            f2_ref[c, :, i * size : (i + 1) * size] = new[c]
    f2 = reader([(0, f2s_ref), (first, f2_ref)], size)
    for k in range(f3_ref.shape[2] // size):
        new = relax_block(f2, stored_source(src_ref, k, size), dg_ref, w, k, mask)
        for c in range(2):
            f3_ref[c, :, k * size : (k + 1) * size] = new[c][PAD : PAD + rows]


def last_kernel(
    f2s_ref, f2_ref, f2e_ref, f3_ref, f3e_ref, src_ref, diag_ref, dge_ref, ha_ref, la_ref, hb_ref, lb_ref, mask_ref,
    out_ref, held_ref, sem,
):
    w = Weights(ha_ref, la_ref, hb_ref, lb_ref)
    size, last = w.size, w.last
    rows = out_ref.shape[1]
    done = f3_ref.shape[2] // size
    mask = line_mask(mask_ref, size)

    def copy(ref, first, blocks, slot):
        cols = pl.ds(first * size, blocks * size)
        return pltpu.make_async_copy(ref, out_ref.at[:, :, cols], sem.at[slot])

    copies = [copy(f3_ref, 0, done, 0), copy(f3e_ref, last, 1, 1)]
    for one in copies:
        one.start()
    dg_ref = (diag_ref, dge_ref)
    f2 = reader([(last - 1, f2e_ref), (f2s_ref.shape[2] // size, f2_ref), (0, f2s_ref)], size)
    for i in range(last - done):
        k = done + i
        new = relax_block(f2, stored_source(src_ref, k, size), dg_ref, w, k, mask)
        for c in range(2):
            held_ref[i, c] = new[c][PAD : PAD + rows]
        copies.append(copy(held_ref.at[i], k, 1, 2 + i))
        copies[-1].start()
    for one in copies:
        one.wait()


def per_device(
    load_current,
    diagonal,
    start_field,
    block_inverse,
    multipliers,
    active_rows,
    contact_peer,
    contact_len,
    port_row,
    port_col,
    port_current,
):
    load, diag, start, mult = load_current[0], diagonal[0], start_field[0], multipliers[0]
    _, rows, width = load.shape
    nb, _, size, _, _ = block_inverse.shape[1:]
    high = rows + 2 * PAD
    step = 6 * high * (2 * size) ** 2

    fill, done = nb * 3 // 8, nb // 2
    count = lax.axis_size("sub")

    m1, m2, one, two, peers, mask = call(
        edges_kernel,
        (start, load, diag, mult, contact_peer, contact_len, active_rows),
        [ANY_SPEC] * 3 + [VMEM_SPEC] + [SMEM_SPEC] * 3,
        [held((2, PAD, IB))] * 2
        + [held((2, PAD, width))] * 2
        + [held((2, rows + PAD, LANES), jnp.int32), held((high, LANES))],
        56 * MIB,
        [pltpu.VMEM((3, 2, 2, PAD, width), jnp.float32), pltpu.SemaphoreType.DMA((3, 2))],
    )
    m1, m2 = passed(CARRY[0], m1, m2)
    m1, m2 = swap_edges(m1, m2)
    one, two = swap_edges(one, two)
    (mask,) = passed(CARRY[1], mask)
    flat = flat_weights(block_inverse[0])
    half = nb // 2
    ha, la, token = split_weights(flat, size, 0, half, mask)
    lines_mult = call(
        lines_kernel,
        (mult, m1, m2, token),
        [VMEM_SPEC] * 4,
        held((2, rows + PAD, IB)),
        MIB,
    )
    other = swap_cores(lines_mult)
    hb, lb, token = split_weights(flat, size, half, nb - half, token)
    merged = call(
        merge_kernel,
        (peers, lines_mult, other, token),
        [VMEM_SPEC] * 4,
        [held(lines_mult.shape)] * (count // 2),
        2 * MIB,
    )
    incoming = [to_chip(cells, step) if step else cells for step, cells in enumerate(merged)]
    weights = (ha, la, hb, lb)

    whole, some = held((2, high, width)), held((2, 2 * PAD, width))
    src, dge, f1, f0e = call(
        functools.partial(first_kernel, nb - 1),
        (start, load, diag, one, two, lines_mult, *weights, mask, port_row, port_col, port_current),
        [VMEM_SPEC] * 11 + [SMEM_SPEC] * 3,
        [whole, some, held((2, high, (nb - 1) * size)), some],
        4 * MIB,
        flops=step * (nb - 1),
    )
    f1e, f2s, f2e, f3e, far = call(
        far_kernel,
        (start, f0e, f1, src, diag, dge, *weights, mask, *incoming),
        [VMEM_SPEC] * (11 + len(incoming)),
        [
            held((2, high, size)),
            held((2, high, fill * size)),
            held((2, high, 2 * size)),
            held((2, rows, size)),
            held((2, rows, IB)),
        ],
        4 * MIB,
        flops=step * (4 + fill),
    )
    ends = [to_chip(far, step) if step else far for step in range(count // 2)]
    f2, f3 = call(
        middle_kernel,
        (f1, f2s, src, diag, dge, *weights, mask),
        [VMEM_SPEC] * 10,
        [held((2, high, (nb - 2 - fill) * size)), held((2, rows, done * size))],
        4 * MIB,
        flops=step * (nb - 2 - fill + done),
    )
    mine, theirs = call(
        sums_kernel, (peers, *ends), [VMEM_SPEC] * (1 + len(ends)), [held(far.shape)] * 2, MIB
    )
    theirs = swap_cores(theirs)
    solved = call(
        last_kernel,
        (f2s, f2, f2e, f3, f3e, src, diag, dge, *weights, mask),
        [VMEM_SPEC] * 13,
        jax.ShapeDtypeStruct((2, rows, width), jnp.float32),
        4 * MIB + 8 * rows * width,
        [pltpu.VMEM((nb - 1 - done, 2, rows, size), jnp.float32), pltpu.SemaphoreType.DMA((nb + 1 - done,))],
        flops=step * (nb - 1 - done),
        out_specs=ANY_SPEC,
    )
    updated = mult + (f3[:, :, :IB] - (mine + theirs))
    return (solved[None], updated[None])


def solution(mesh):
    lines = P("sub", None, "tile", None)
    in_specs = (
        lines,
        lines,
        lines,
        P("sub", None, None, None, None, None),
        lines,
        P(),
        P(),
        P(),
        P("sub", None),
        P("sub", None),
        P("sub", None, None),
    )
    return jax.shard_map(
        per_device, mesh=mesh, in_specs=in_specs, out_specs=(lines, lines), check_vma=False
    )
```

time: 44.6 us -> 43.5 us (0.975); the launches traced: 44.4 us -> 42.8 us
  Pallas kernels: 24.8 us -> 23 us
  starting transfers between devices: 15.8 us -> 16.9 us
    pallas_call x10 -> x12, Pallas kernels: 24.8 us -> 23 us  [call(): pl.pallas_call(kernel, out_shape=outs, in_specs=specs, out_specs=out_spec...]
    ppermute x8, starting transfers between devices: 9.82 us -> 10.9 us  [the longest x6 10.7 us: to_chip(): lax.ppermute(cells, 'sub', [(i, (i + 2 * step) % count) for i in range(co...]
    ppermute x4, waiting for transfers between devices: 1.67 us -> 0.71 us  [swap_edges(): return (lax.ppermute(one, 'tile', first), lax.ppermute(two, 'tile', second))]
    ppermute x8, waiting for transfers between devices: 0.02 us -> 0.55 us  [the longest x6 0.54 us: to_chip(): lax.ppermute(cells, 'sub', [(i, (i + 2 * step) % count) for i in range(co...]
  transfers between devices with their start and end apart: 12 -> 12, of which waited for: 1 -> 2; matrix products, arithmetic and copies ran while one was open for 0% -> 0% of each run, Pallas kernels for 41% -> 39%
where the time goes in v3:
time: 43.5 us; the launch traced here: 42.8 us
  Pallas kernels  23 us (53%)
  starting transfers between devices  16.9 us (39%)
  waiting for transfers between devices  1.26 us (3%)
  between operations  0.94 us (2%)
  other arithmetic  0.65 us (1%)
    pallas_call x12, Pallas kernels, call(): pl.pallas_call(kernel, out_shape=outs, in_specs=specs, out_specs=out_spec...  23 us
    ppermute x6, starting transfers between devices, to_chip(): lax.ppermute(cells, 'sub', [(i, (i + 2 * step) % count) for i in range(co...  10.7 us
    ppermute x4, starting transfers between devices, swap_edges(): return (lax.ppermute(one, 'tile', first), lax.ppermute(two, 'tile', second))  6.01 us
  transfers between devices with their start and end apart: 12, of which 2 were waited for; matrix products, arithmetic and copies ran while one was open for 0% of the time, Pallas kernels for 39%

profile of v3, /device:TPU:0, one launch (start us, length us, event | category | flops | bytes accessed | tf_op | source)
XLA Modules:
  0.0 42.8 jit_solution(1091859946530119595)
XLA Ops:
  0.6 0.0 slice-start
  0.6 2.8 %shard_map.122 = (f32[2,8,128]{2,1,0:T(8,128)S(1)}, f32[2,8,128]{2,1,0:T(8,128)S(1)}, f32[2,8,4096]{2,1,0:T(8,128)S(1)}, f32[2,8,4096]{2,1,0:T(8,128)S(1)}, s32[...) custom-call(f32[2,64,4096]{2,1,0:T(8,128)} %bitcast.22, f32[2,64,4096]{2,1,0:T(8,128)} %bitcast.25, f32[2,64,4096]{2,1,0:T(8,128)} %bitcast.17, ...), custom_call_target="tpu_custom_call" | custom-call | tf_op jit(solution)/shard_map/pallas_call | solution.py:24
  3.4 0.0 slice-start.1
  3.4 0.0 slice-start.2
  3.4 0.0 slice-start.3
  3.5 3.0 %collective-permute-start.2 = (f32[2,8,128]{2,1,0:T(8,128)S(1)}, f32[2,8,128]{2,1,0:T(8,128)S(1)}, u32[]{:S(2)}, u32[]{:S(2)}) collective-permute-start(f32[2,8,128]{2,1,0:T(8,128)S(1)} %get-tuple-element.36), channel_id=1, source_target_pairs={{0,1},{1,0},{2,3},{3,2},{4,5},{5,4},{6,7},{7,6},{8,9},{9,8},{10,11... | collective-permute-start | bytes 24584 | tf_op jit(solution)/shard_map/ppermute | solution.py:164
  6.5 1.5 %collective-permute-start.3 = (f32[2,8,128]{2,1,0:T(8,128)S(1)}, f32[2,8,128]{2,1,0:T(8,128)S(1)}, u32[]{:S(2)}, u32[]{:S(2)}) collective-permute-start(f32[2,8,128]{2,1,0:T(8,128)S(1)} %get-tuple-element.37), channel_id=1, source_target_pairs={{0,3},{1,2},{2,1},{3,0},{4,7},{5,6},{6,5},{7,4},{8,11},{9,10},{10,... | collective-permute-start | bytes 24584 | tf_op jit(solution)/shard_map/ppermute | solution.py:164
  8.0 1.5 %collective-permute-start = (f32[2,8,4096]{2,1,0:T(8,128)S(1)}, f32[2,8,4096]{2,1,0:T(8,128)S(1)}, u32[]{:S(2)}, u32[]{:S(2)}) collective-permute-start(f32[2,8,4096]{2,1,0:T(8,128)S(1)} %get-tuple-element.32), channel_id=1, source_target_pairs={{0,1},{1,0},{2,3},{3,2},{4,5},{5,4},{6,7},{7,6},{8,9},{9,8},{10,11... | collective-permute-start | bytes 786440 | tf_op jit(solution)/shard_map/ppermute | solution.py:164
  9.5 0.0 collective-permute-start.1
  9.5 0.0 slice-done
  9.5 0.0 slice-done.1
  9.5 0.0 slice-done.2
  9.5 0.0 slice-done.3
  9.5 0.0 copy-start.3
  9.5 2.2 %shard_map.125 = (bf16[8,512,512]{2,1,0:T(8,128)(2,1)S(1)}, bf16[8,512,512]{2,1,0:T(8,128)(2,1)S(1)}, f32[8,128]{1,0:T(8,128)S(1)}) custom-call(f32[16,2048,128]{2,1,0:T(8,128)S(1)} %bitcast.15, f32[80,128]{1,0:T(8,128)S(1)} %shard_map.124._.mask_ref), custom_call_target="tpu_custom_call" | custom-call | bytes 16777216 | tf_op jit(solution)/shard_map/pallas_call | solution.py:24
  11.8 0.0 collective-permute-done.2.one_ref
  11.8 0.0 collective-permute-done.3.two_ref
  11.8 0.0 copy-done.3
  11.8 0.0 copy-start
  11.8 0.0 copy-start.1
  11.8 0.0 copy-start.2
  11.9 0.0 copy-start.4
  11.9 0.0 copy-start.5
  11.9 0.0 copy-start.6
  11.9 0.1 collective-permute-start.4
  12.0 2.2 %shard_map.127 = (bf16[8,512,512]{2,1,0:T(8,128)(2,1)S(1)}, bf16[8,512,512]{2,1,0:T(8,128)(2,1)S(1)}, f32[8,128]{1,0:T(8,128)S(1)}) custom-call(f32[16,2048,128]{2,1,0:T(8,128)S(1)} %bitcast.16, f32[8,128]{1,0:T(8,128)S(1)} %get-tuple-element.39._), custom_call_target="tpu_custom_call" | custom-call | bytes 16777216 | tf_op jit(solution)/shard_map/pallas_call | solution.py:24
  14.2 0.0 collective-permute-done.4.other_ref
  14.3 2.1 %collective-permute-start.5 = (f32[2,72,128]{2,1,0:T(8,128)S(1)}, f32[2,72,128]{2,1,0:T(8,128)S(1)}, u32[]{:S(2)}, u32[]{:S(2)}) collective-permute-start(f32[2,72,128]{2,1,0:T(8,128)S(1)} %get-tuple-element.51), channel_id=1, source_target_pairs={{0,8},{4,12},{8,16},{12,20},{16,24},{20,28},{24,0},{28,4},{1,9},{5... | collective-permute-start | bytes 221192 | tf_op jit(solution)/shard_map/ppermute | solution.py:169
  16.3 2.6 %collective-permute-start.6 = (f32[2,72,128]{2,1,0:T(8,128)S(1)}, f32[2,72,128]{2,1,0:T(8,128)S(1)}, u32[]{:S(2)}, u32[]{:S(2)}) collective-permute-start(f32[2,72,128]{2,1,0:T(8,128)S(1)} %get-tuple-element.52), channel_id=1, source_target_pairs={{0,16},{4,20},{8,24},{12,28},{16,0},{20,4},{24,8},{28,12},{1,17},{... | collective-permute-start | bytes 221192 | tf_op jit(solution)/shard_map/ppermute | solution.py:169
  18.9 1.3 %collective-permute-start.7 = (f32[2,72,128]{2,1,0:T(8,128)S(1)}, f32[2,72,128]{2,1,0:T(8,128)S(1)}, u32[]{:S(2)}, u32[]{:S(2)}) collective-permute-start(f32[2,72,128]{2,1,0:T(8,128)S(1)} %get-tuple-element.53), channel_id=1, source_target_pairs={{0,24},{4,28},{8,0},{12,4},{16,8},{20,12},{24,16},{28,20},{1,25},{... | collective-permute-start | bytes 221192 | tf_op jit(solution)/shard_map/ppermute | solution.py:169
  20.3 0.0 collective-permute-done.one_ref
  20.3 0.7 %collective-permute-done.1.two_ref = f32[2,8,4096]{2,1,0:T(8,128)S(1)} collective-permute-done((f32[2,8,4096]{2,1,0:T(8,128)S(1)}, f32[2,8,4096]{2,1,0:T(8,128)S(1)}, u32[]{:S(2)}, u32[]{:S(2)}) %collective-permute-start.1) | collective-permute-done | bytes 262176 | tf_op jit(solution)/shard_map/ppermute | solution.py:164
  21.0 0.0 copy-done
  21.0 0.0 copy-done.1
  21.0 0.0 copy-done.2
  21.0 0.0 copy-done.4
  21.0 0.0 copy-done.5
  21.0 0.0 copy-done.6
  21.0 5.1 %shard_map.128 = (f32[2,80,4096]{2,1,0:T(8,128)S(1)}, f32[2,16,4096]{2,1,0:T(8,128)S(1)}, f32[2,80,3840]{2,1,0:T(8,128)S(1)}, f32[2,16,4096]{2,1,0:T(8,128)S(1)}) custom-call(f32[2,64,4096]{2,1,0:T(8,128)S(1)} %bitcast.23, f32[2,64,4096]{2,1,0:T(8,128)S(1)} %bitcast.26, f32[2,64,4096]{2,1,0:T(8,128)S(1)} %bitcast.18, ...), custom_call_target="tpu_custom_call" | custom-call | flops 1887436800 | tf_op jit(solution)/shard_map/pallas_call | solution.py:24
  26.1 0.0 collective-permute-done.5.refs_1_
  26.1 0.0 collective-permute-done.6.refs_2_
  26.1 0.0 collective-permute-done.7.refs_3_
  26.2 3.3 %shard_map.130 = (f32[2,80,256]{2,1,0:T(8,128)}, f32[2,80,1536]{2,1,0:T(8,128)S(1)}, f32[2,80,512]{2,1,0:T(8,128)S(1)}, f32[2,64,256]{2,1,0:T(8,128)S(1)}, f32[2,64,128]{2,1,0:T(8,128)S(1)}) custom-call(f32[2,64,4096]{2,1,0:T(8,128)S(1)} %bitcast.24, f32[2,16,4096]{2,1,0:T(8,128)S(1)} %get-tuple-element.44.f0e_ref, ...), custom_call_target="tpu_custom_call" | custom-call | flops 1258291200 | tf_op jit(solution)/shard_map/pallas_call | solution.py:24
  29.5 3.7 %collective-permute-start.10 = (f32[2,64,128]{2,1,0:T(8,128)S(1)}, f32[2,64,128]{2,1,0:T(8,128)S(1)}, u32[]{:S(2)}, u32[]{:S(2)}) collective-permute-start(f32[2,64,128]{2,1,0:T(8,128)S(1)} %get-tuple-element.59.refs_0_), channel_id=1, source_target_pairs={{0,24},{4,28},{8,0},{12,4},{16,8},{20,12},{24,16},{28,20},{1,25},{... | collective-permute-start | bytes 196616 | tf_op jit(solution)/shard_map/ppermute | solution.py:169
  33.2 0.0 collective-permute-start.8
  33.2 1.0 %collective-permute-start.9 = (f32[2,64,128]{2,1,0:T(8,128)S(1)}, f32[2,64,128]{2,1,0:T(8,128)S(1)}, u32[]{:S(2)}, u32[]{:S(2)}) collective-permute-start(f32[2,64,128]{2,1,0:T(8,128)S(1)} %get-tuple-element.59.refs_0_), channel_id=1, source_target_pairs={{0,16},{4,20},{8,24},{12,28},{16,0},{20,4},{24,8},{28,12},{1,17},{... | collective-permute-start | bytes 196616 | tf_op jit(solution)/shard_map/ppermute | solution.py:169
  34.2 4.5 %shard_map.131 = (f32[2,80,2048]{2,1,0:T(8,128)S(1)}, f32[2,64,2048]{2,1,0:T(8,128)S(1)}) custom-call(f32[2,80,3840]{2,1,0:T(8,128)S(1)} %get-tuple-element.45.f1_ref, f32[2,80,1536]{2,1,0:T(8,128)S(1)} %get-tuple-element.54.f2s_ref, f32[2,80,4096]{2,1,0:T(8,128)S(1)} %get-tuple-element.46.src_ref, f32[2,64,4096]{2,1,0:T(8,128)S(1)} %bitcast.20, ...), custom_call_target="tpu_custom_call" | custom-call | flops 2013265920 | tf_op jit(solution)/shard_map/pallas_call | solution.py:24
  38.7 0.0 collective-permute-done.10.refs_3_
  38.7 0.5 %collective-permute-done.8.refs_1_ = f32[2,64,128]{2,1,0:T(8,128)S(1)} collective-permute-done((f32[2,64,128]{2,1,0:T(8,128)S(1)}, f32[2,64,128]{2,1,0:T(8,128)S(1)}, u32[]{:S(2)}, u32[]{:S(2)}) %collective-permute-start.8) | collective-permute-done | bytes 65568 | tf_op jit(solution)/shard_map/ppermute | solution.py:169
  39.2 0.0 collective-permute-done.9.refs_2_
  39.3 0.1 shard_map.133
  39.3 0.1 collective-permute-start.11
  39.4 2.7 %shard_map.132 = f32[2,64,4096]{2,1,0:T(8,128)} custom-call(f32[2,80,1536]{2,1,0:T(8,128)S(1)} %get-tuple-element.54.f2s_ref, f32[2,80,2048]{2,1,0:T(8,128)S(1)} %get-tuple-element.55.f2_ref, f32[2,80,512]{2,1,0:T(8,128)S(1)} %get-tuple-element.56.f2e_ref, f32[2,64,2048]{2,1,0:T(8,128)S(1)} %get-tuple-element.57.f3_ref, ...), custom_call_target="tpu_custom_call" | custom-call | flops 880803840 | tf_op jit(solution)/shard_map/pallas_call | solution.py:24
  42.1 0.0 collective-permute-done.11
  42.1 0.7 %add_bitcast_fusion = f32[1,2,64,128]{3,2,1,0:T(8,128)} fusion(f32[2,64,128]{2,1,0:T(8,128)S(1)} %get-tuple-element.60, f32[2,64,128]{2,1,0:T(8,128)S(1)} %collective-permute-done.11, f32[2,64,2048]{2,1,0:T(8,128)S(1)} %get-tuple-element.57.f3_ref, f32[1,2,64,128]{3,2,1,0:T(8,128)S(1)} %copy-done.3), kind=kLoop, calls=%fused_computation | loop fusion | flops 49152 | bytes 327680 | tf_op jit(solution)/shard_map/broadcast_in_dim | solution.py:536
  (5 shorter events, 0.1 us)
Async XLA Ops:
  0.6 8.9 %slice-start = ((s8[16777216]{0:T(1024)(128)(4,1)}), s8[4194304]{0:T(1024)(128)(4,1)S(1)}, s32[]{:S(2)}) async-start(s8[16777216]{0:T(1024)(128)(4,1)} %bitcast.13), calls=%async_computation | async-start | bytes 8388608
  3.4 6.1 %slice-start.1 = ((s8[16777216]{0:T(1024)(128)(4,1)}), s8[4194304]{0:T(1024)(128)(4,1)S(1)}, s32[]{:S(2)}) async-start(s8[16777216]{0:T(1024)(128)(4,1)} %bitcast.13), calls=%async_computation.1 | async-start | bytes 8388608
  3.4 6.1 %slice-start.2 = ((s8[16777216]{0:T(1024)(128)(4,1)}), s8[4194304]{0:T(1024)(128)(4,1)S(1)}, s32[]{:S(2)}) async-start(s8[16777216]{0:T(1024)(128)(4,1)} %bitcast.13), calls=%async_computation.2 | async-start | bytes 8388608
  3.4 6.1 %slice-start.3 = ((s8[16777216]{0:T(1024)(128)(4,1)}), s8[4194304]{0:T(1024)(128)(4,1)S(1)}, s32[]{:S(2)}) async-start(s8[16777216]{0:T(1024)(128)(4,1)} %bitcast.13), calls=%async_computation.3 | async-start | bytes 8388608
  3.5 8.3 %collective-permute-start.2 = (f32[2,8,128]{2,1,0:T(8,128)S(1)}, f32[2,8,128]{2,1,0:T(8,128)S(1)}, u32[]{:S(2)}, u32[]{:S(2)}) collective-permute-start(f32[2,8,128]{2,1,0:T(8,128)S(1)} %get-tuple-element.36), channel_id=1, source_target_pairs={{0,1},{1,0},{2,3},{3,2},{4,5},{5,4},{6,7},{7,6},{8,9},{9,8},{10,11... | collective-permute-start | bytes 24584 | tf_op jit(solution)/shard_map/ppermute | solution.py:164
  6.5 5.3 %collective-permute-start.3 = (f32[2,8,128]{2,1,0:T(8,128)S(1)}, f32[2,8,128]{2,1,0:T(8,128)S(1)}, u32[]{:S(2)}, u32[]{:S(2)}) collective-permute-start(f32[2,8,128]{2,1,0:T(8,128)S(1)} %get-tuple-element.37), channel_id=1, source_target_pairs={{0,3},{1,2},{2,1},{3,0},{4,7},{5,6},{6,5},{7,4},{8,11},{9,10},{10,... | collective-permute-start | bytes 24584 | tf_op jit(solution)/shard_map/ppermute | solution.py:164
  8.0 12.3 %collective-permute-start = (f32[2,8,4096]{2,1,0:T(8,128)S(1)}, f32[2,8,4096]{2,1,0:T(8,128)S(1)}, u32[]{:S(2)}, u32[]{:S(2)}) collective-permute-start(f32[2,8,4096]{2,1,0:T(8,128)S(1)} %get-tuple-element.32), channel_id=1, source_target_pairs={{0,1},{1,0},{2,3},{3,2},{4,5},{5,4},{6,7},{7,6},{8,9},{9,8},{10,11... | collective-permute-start | bytes 786440 | tf_op jit(solution)/shard_map/ppermute | solution.py:164
  9.5 11.5 %collective-permute-start.1 = (f32[2,8,4096]{2,1,0:T(8,128)S(1)}, f32[2,8,4096]{2,1,0:T(8,128)S(1)}, u32[]{:S(2)}, u32[]{:S(2)}) collective-permute-start(f32[2,8,4096]{2,1,0:T(8,128)S(1)} %get-tuple-element.33), channel_id=1, source_target_pairs={{0,3},{1,2},{2,1},{3,0},{4,7},{5,6},{6,5},{7,4},{8,11},{9,10},{10,... | collective-permute-start | bytes 786440 | tf_op jit(solution)/shard_map/ppermute | solution.py:164
  9.5 2.3 %copy-start.3 = (f32[1,2,64,128]{3,2,1,0:T(8,128)S(1)}, f32[1,2,64,128]{3,2,1,0:T(8,128)}, u32[]{:S(2)}) copy-start(f32[1,2,64,128]{3,2,1,0:T(8,128)} %param.15) | copy-start | bytes 196612
  11.8 9.2 %copy-start = (f32[1,2,64,4096]{3,2,1,0:T(8,128)S(1)}, f32[1,2,64,4096]{3,2,1,0:T(8,128)}, u32[]{:S(2)}) copy-start(f32[1,2,64,4096]{3,2,1,0:T(8,128)} %param.12) | copy-start | bytes 6291460
  11.8 9.2 %copy-start.1 = (f32[1,2,64,4096]{3,2,1,0:T(8,128)S(1)}, f32[1,2,64,4096]{3,2,1,0:T(8,128)}, u32[]{:S(2)}) copy-start(f32[1,2,64,4096]{3,2,1,0:T(8,128)} %param.13) | copy-start | bytes 6291460
  11.8 9.2 %copy-start.2 = (f32[1,2,64,4096]{3,2,1,0:T(8,128)S(1)}, f32[1,2,64,4096]{3,2,1,0:T(8,128)}, u32[]{:S(2)}) copy-start(f32[1,2,64,4096]{3,2,1,0:T(8,128)} %param.11) | copy-start | bytes 6291460
  11.9 9.2 %copy-start.4 = (f32[1,2,16]{2,1,0:T(2,128)S(1)}, f32[1,2,16]{2,1,0:T(2,128)}, u32[]{:S(2)}) copy-start(f32[1,2,16]{2,1,0:T(2,128)} %pcur_ref.1) | copy-start | bytes 388
  11.9 9.2 %copy-start.5 = (s32[1,16]{1,0:T(1,128)S(1)}, s32[1,16]{1,0:T(1,128)}, u32[]{:S(2)}) copy-start(s32[1,16]{1,0:T(1,128)} %prow_ref.1) | copy-start | bytes 196
  11.9 9.2 %copy-start.6 = (s32[1,16]{1,0:T(1,128)S(1)}, s32[1,16]{1,0:T(1,128)}, u32[]{:S(2)}) copy-start(s32[1,16]{1,0:T(1,128)} %pcol_ref.1) | copy-start | bytes 196
  11.9 2.3 %collective-permute-start.4 = (f32[2,72,128]{2,1,0:T(8,128)S(1)}, f32[2,72,128]{2,1,0:T(8,128)S(1)}, u32[]{:S(2)}, u32[]{:S(2)}) collective-permute-start(f32[2,72,128]{2,1,0:T(8,128)S(1)} %shard_map.126.mult_ref.own_ref), channel_id=1, source_target_pairs={{0,4},{4,0},{8,12},{12,8},{16,20},{20,16},{24,28},{28,24},{1,5},{5... | collective-permute-start | bytes 221192 | tf_op jit(solution)/shard_map/ppermute | solution.py:173
  14.3 11.9 %collective-permute-start.5 = (f32[2,72,128]{2,1,0:T(8,128)S(1)}, f32[2,72,128]{2,1,0:T(8,128)S(1)}, u32[]{:S(2)}, u32[]{:S(2)}) collective-permute-start(f32[2,72,128]{2,1,0:T(8,128)S(1)} %get-tuple-element.51), channel_id=1, source_target_pairs={{0,8},{4,12},{8,16},{12,20},{16,24},{20,28},{24,0},{28,4},{1,9},{5... | collective-permute-start | bytes 221192 | tf_op jit(solution)/shard_map/ppermute | solution.py:169
  16.3 9.8 %collective-permute-start.6 = (f32[2,72,128]{2,1,0:T(8,128)S(1)}, f32[2,72,128]{2,1,0:T(8,128)S(1)}, u32[]{:S(2)}, u32[]{:S(2)}) collective-permute-start(f32[2,72,128]{2,1,0:T(8,128)S(1)} %get-tuple-element.52), channel_id=1, source_target_pairs={{0,16},{4,20},{8,24},{12,28},{16,0},{20,4},{24,8},{28,12},{1,17},{... | collective-permute-start | bytes 221192 | tf_op jit(solution)/shard_map/ppermute | solution.py:169
  18.9 7.2 %collective-permute-start.7 = (f32[2,72,128]{2,1,0:T(8,128)S(1)}, f32[2,72,128]{2,1,0:T(8,128)S(1)}, u32[]{:S(2)}, u32[]{:S(2)}) collective-permute-start(f32[2,72,128]{2,1,0:T(8,128)S(1)} %get-tuple-element.53), channel_id=1, source_target_pairs={{0,24},{4,28},{8,0},{12,4},{16,8},{20,12},{24,16},{28,20},{1,25},{... | collective-permute-start | bytes 221192 | tf_op jit(solution)/shard_map/ppermute | solution.py:169
  29.5 9.3 %collective-permute-start.10 = (f32[2,64,128]{2,1,0:T(8,128)S(1)}, f32[2,64,128]{2,1,0:T(8,128)S(1)}, u32[]{:S(2)}, u32[]{:S(2)}) collective-permute-start(f32[2,64,128]{2,1,0:T(8,128)S(1)} %get-tuple-element.59.refs_0_), channel_id=1, source_target_pairs={{0,24},{4,28},{8,0},{12,4},{16,8},{20,12},{24,16},{28,20},{1,25},{... | collective-permute-start | bytes 196616 | tf_op jit(solution)/shard_map/ppermute | solution.py:169
  33.2 6.1 %collective-permute-start.8 = (f32[2,64,128]{2,1,0:T(8,128)S(1)}, f32[2,64,128]{2,1,0:T(8,128)S(1)}, u32[]{:S(2)}, u32[]{:S(2)}) collective-permute-start(f32[2,64,128]{2,1,0:T(8,128)S(1)} %get-tuple-element.59.refs_0_), channel_id=1, source_target_pairs={{0,8},{4,12},{8,16},{12,20},{16,24},{20,28},{24,0},{28,4},{1,9},{5... | collective-permute-start | bytes 196616 | tf_op jit(solution)/shard_map/ppermute | solution.py:169
  33.2 6.1 %collective-permute-start.9 = (f32[2,64,128]{2,1,0:T(8,128)S(1)}, f32[2,64,128]{2,1,0:T(8,128)S(1)}, u32[]{:S(2)}, u32[]{:S(2)}) collective-permute-start(f32[2,64,128]{2,1,0:T(8,128)S(1)} %get-tuple-element.59.refs_0_), channel_id=1, source_target_pairs={{0,16},{4,20},{8,24},{12,28},{16,0},{20,4},{24,8},{28,12},{1,17},{... | collective-permute-start | bytes 196616 | tf_op jit(solution)/shard_map/ppermute | solution.py:169
  39.3 2.8 %collective-permute-start.11 = (f32[2,64,128]{2,1,0:T(8,128)S(1)}, f32[2,64,128]{2,1,0:T(8,128)S(1)}, u32[]{:S(2)}, u32[]{:S(2)}) collective-permute-start(f32[2,64,128]{2,1,0:T(8,128)S(1)} %get-tuple-element.61), channel_id=1, source_target_pairs={{0,4},{4,0},{8,12},{12,8},{16,20},{20,16},{24,28},{28,24},{1,5},{5... | collective-permute-start | bytes 196616 | tf_op jit(solution)/shard_map/ppermute | solution.py:173

commit v4 on v3

--- a/solution.py
+++ b/solution.py
@@ -76,7 +76,7 @@
 
 def split_weights(flat, size, first, count, after):
     shape = (count, 2 * size, 2 * size)
-    return call(
+    high, low, token = call(
         functools.partial(weights_kernel, size, first),
         (flat, after),
         [VMEM_SPEC] * 2,
@@ -84,6 +84,7 @@
         2 * MIB,
         moved=count * size * size * 32,
     )
+    return (high, low), token
 
 
 def edges_kernel(
@@ -112,7 +113,7 @@
     peers_ref[1] = line_peers(peer_ref, len_ref, me + 1 - 2 * lax.rem(me, 2), lines)
     at = lax.broadcasted_iota(jnp.int32, mask_ref.shape, 0) + (first - PAD)
     mask_ref[...] = jnp.where((at >= 0) & (at < active_ref[me]), 1.0, 0.0)
-    row = lax.broadcasted_iota(jnp.int32, one_ref.shape[1:], 0)
+    row = lax.broadcasted_iota(jnp.int32, (PAD, start_hbm.shape[2]), 0)
     for copy in copies:
         copy.wait()
 
@@ -121,9 +122,26 @@
         return jnp.where(row < 3, field, jnp.where(row < 5, load, diag))
 
     for c in range(2):
-        top, bottom = lines_of(c, 0, (0, 3, 5)), lines_of(c, 1, (3, 5, 7))
+        top, bottom = pack_rows(lines_of(c, 0, (0, 3, 5))), pack_rows(lines_of(c, 1, (3, 5, 7)))
         one_ref[c] = jnp.where(even, bottom, top)
         two_ref[c] = jnp.where(even, top, bottom)
+
+
+def pack_rows(cells):
+    width = cells.shape[1] // PAD * (PAD - 1)
+    ends = cells[:, width:]
+    tail = jnp.concatenate([pltpu.roll(ends, PAD - 1 - r, 0) for r in range(PAD - 1)], axis=1)
+    row = lax.broadcasted_iota(jnp.int32, tail.shape, 0)
+    return jnp.where(row == PAD - 1, tail, cells[:, :width])
+
+
+def unpack_rows(cells):
+    step = cells.shape[1] // (PAD - 1)
+    row = lax.broadcasted_iota(jnp.int32, (PAD, step), 0)
+    ends = pltpu.roll(cells[:, :step], 1, 0)
+    for r in range(1, PAD - 1):
+        ends = jnp.where(row == r, pltpu.roll(cells[:, r * step : (r + 1) * step], r + 1, 0), ends)
+    return jnp.concatenate([cells, ends], axis=1)
 
 
 def pass_kernel(*refs):
@@ -173,13 +191,28 @@
     return lax.ppermute(cells, "sub", [(i, i ^ 1) for i in range(lax.axis_size("sub"))])
 
 
-def merge_kernel(peers_ref, own_ref, other_ref, _, *outs):
-    me, count = lax.axis_index("sub"), 2 * len(outs)
+def merge_kernel(peers_ref, own_ref, other_ref, _, keep_ref, send_ref):
+    me = lax.axis_index("sub")
     own, other = own_ref[...], other_ref[...]
-    for step in range(1, len(outs)):
-        to = lax.rem(me + 2 * step, count)
-        outs[step][...] = pick(peers_ref[0] == to, own) + pick(peers_ref[1] == to, other)
-    outs[0][...] = pick(peers_ref[1] == me, other)
+    for x in range(2 * keep_ref.shape[0]):
+        to = me ^ (2 * x)
+        out = send_ref if x % 2 else keep_ref
+        out[x // 2] = pick(peers_ref[0] == to, own) + pick(peers_ref[1] == to, other)
+
+
+def fold_kernel(keep_ref, got_ref, _, next_ref, send_ref):
+    for x in range(keep_ref.shape[0]):
+        out = send_ref if x % 2 else next_ref
+        out[x // 2] = keep_ref[x] + got_ref[x]
+
+
+def halved(cells):
+    shape = (cells.shape[0] // 2, *cells.shape[1:])
+    return [held(shape), held(shape)]
+
+
+def over_bit(cells, bit):
+    return lax.ppermute(cells, "sub", [(i, i ^ (2 * bit)) for i in range(lax.axis_size("sub"))])
 
 
 def sums_kernel(peers_ref, *refs):
@@ -197,14 +230,16 @@
 
 
 class Weights:
-    def __init__(self, *refs):
-        self.parts = refs[:2], refs[2:]
+    def __init__(self, refs):
+        self.runs = list(zip(refs[::2], refs[1::2]))
         self.size = refs[0].shape[1] // 2
-        self.last = refs[0].shape[0] + refs[2].shape[0] - 1
+        self.last = sum(ref.shape[0] for ref in refs[::2]) - 1
 
     def part(self, k, low):
-        first = self.parts[0][0].shape[0]
-        return self.parts[0][low][k] if k < first else self.parts[1][low][k - first]
+        for run in self.runs:
+            if k < run[0].shape[0]:
+                return run[low][k]
+            k -= run[0].shape[0]
 
     def high(self, k):
         return self.part(k, 0)
@@ -280,11 +315,12 @@
 
 
 def first_kernel(
-    upto, start_ref, load_ref, diag_ref, one_ref, two_ref, mult_ref, ha_ref, la_ref, hb_ref, lb_ref, mask_ref,
-    prow_ref, pcol_ref, pcur_ref, src_ref, dge_ref, f1_ref, f0e_ref,
+    upto, start_ref, load_ref, diag_ref, one_ref, two_ref, mult_ref, mask_ref,
+    prow_ref, pcol_ref, pcur_ref, *refs,
 ):
+    w_refs, (src_ref, dge_ref, f1_ref, f0e_ref) = refs[:-4], refs[-4:]
     _, rows, width = load_ref.shape
-    w = Weights(ha_ref, la_ref, hb_ref, lb_ref)
+    w = Weights(w_refs)
     size = w.size
     own = slice(PAD, PAD + rows)
     above, below = slice(0, PAD), slice(PAD + rows, 2 * PAD + rows)
@@ -292,8 +328,8 @@
     even = lax.rem(tile, 2) == 0
     for c in range(2):
         one, two = one_ref[c], two_ref[c]
-        up = jnp.where(even, two, one)
-        down = jnp.where(even, one, two)
+        up = unpack_rows(jnp.where(even, two, one))
+        down = unpack_rows(jnp.where(even, one, two))
         f0e_ref[c, :PAD] = pltpu.roll(up, 5, 0)
         f0e_ref[c, PAD:] = down
         dge_ref[c, :PAD] = pltpu.roll(up, 1, 0)
@@ -330,11 +366,11 @@
 
 
 def far_kernel(
-    start_ref, f0e_ref, f1_ref, src_ref, diag_ref, dge_ref, ha_ref, la_ref, hb_ref, lb_ref, mask_ref, *refs,
+    count, start_ref, f0e_ref, f1_ref, src_ref, diag_ref, dge_ref, mask_ref, *refs
 ):
-    w = Weights(ha_ref, la_ref, hb_ref, lb_ref)
+    pieces, w_refs, (f1e_ref, f2s_ref, f2e_ref, f3e_ref, far_ref) = refs[:count], refs[count:-5], refs[-5:]
+    w = Weights(w_refs)
     size, last = w.size, w.last
-    pieces, (f1e_ref, f2s_ref, f2e_ref, f3e_ref, far_ref) = refs[:-5], refs[-5:]
     rows = far_ref.shape[1]
     mask = line_mask(mask_ref, size)
     into = []
@@ -377,9 +413,10 @@
 
 
 def middle_kernel(
-    f1_ref, f2s_ref, src_ref, diag_ref, dge_ref, ha_ref, la_ref, hb_ref, lb_ref, mask_ref, f2_ref, f3_ref
+    f1_ref, f2s_ref, src_ref, diag_ref, dge_ref, mask_ref, *refs
 ):
-    w = Weights(ha_ref, la_ref, hb_ref, lb_ref)
+    w_refs, (f2_ref, f3_ref) = refs[:-2], refs[-2:]
+    w = Weights(w_refs)
     size = w.size
     rows = f3_ref.shape[1]
     first = f2s_ref.shape[2] // size
@@ -399,10 +436,10 @@
 
 
 def last_kernel(
-    f2s_ref, f2_ref, f2e_ref, f3_ref, f3e_ref, src_ref, diag_ref, dge_ref, ha_ref, la_ref, hb_ref, lb_ref, mask_ref,
-    out_ref, held_ref, sem,
+    f2s_ref, f2_ref, f2e_ref, f3_ref, f3e_ref, src_ref, diag_ref, dge_ref, mask_ref, *refs
 ):
-    w = Weights(ha_ref, la_ref, hb_ref, lb_ref)
+    w_refs, (out_ref, held_ref, sem) = refs[:-3], refs[-3:]
+    w = Weights(w_refs)
     size, last = w.size, w.last
     rows = out_ref.shape[1]
     done = f3_ref.shape[2] // size
@@ -455,7 +492,7 @@
         (start, load, diag, mult, contact_peer, contact_len, active_rows),
         [ANY_SPEC] * 3 + [VMEM_SPEC] + [SMEM_SPEC] * 3,
         [held((2, PAD, IB))] * 2
-        + [held((2, PAD, width))] * 2
+        + [held((2, PAD, width // PAD * (PAD - 1)))] * 2
         + [held((2, rows + PAD, LANES), jnp.int32), held((high, LANES))],
         56 * MIB,
         [pltpu.VMEM((3, 2, 2, PAD, width), jnp.float32), pltpu.SemaphoreType.DMA((3, 2))],
@@ -465,8 +502,9 @@
     one, two = swap_edges(one, two)
     (mask,) = passed(CARRY[1], mask)
     flat = flat_weights(block_inverse[0])
-    half = nb // 2
-    ha, la, token = split_weights(flat, size, 0, half, mask)
+    chips = count // 2
+    quarter = nb // 4
+    w1, token = split_weights(flat, size, 0, quarter, mask)
     lines_mult = call(
         lines_kernel,
         (mult, m1, m2, token),
@@ -475,30 +513,34 @@
         MIB,
     )
     other = swap_cores(lines_mult)
-    hb, lb, token = split_weights(flat, size, half, nb - half, token)
-    merged = call(
-        merge_kernel,
-        (peers, lines_mult, other, token),
-        [VMEM_SPEC] * 4,
-        [held(lines_mult.shape)] * (count // 2),
-        2 * MIB,
-    )
-    incoming = [to_chip(cells, step) if step else cells for step, cells in enumerate(merged)]
-    weights = (ha, la, hb, lb)
+    w2, token = split_weights(flat, size, quarter, quarter, token)
+    half = held((chips // 2, *lines_mult.shape))
+    keep, send = call(
+        merge_kernel, (peers, lines_mult, other, token), [VMEM_SPEC] * 4, [half] * 2, 2 * MIB
+    )
+    got = over_bit(send, 1)
+    w3, token = split_weights(flat, size, 2 * quarter, nb - 2 * quarter, keep)
+    bit = 1
+    while keep.shape[0] > 1:
+        keep, send = call(fold_kernel, (keep, got, token), [VMEM_SPEC] * 3, halved(keep), 2 * MIB)
+        bit *= 2
+        got = over_bit(send, bit)
+    incoming = [keep[0], got[0]]
+    weights = (*w1, *w2, *w3)
 
     whole, some = held((2, high, width)), held((2, 2 * PAD, width))
     src, dge, f1, f0e = call(
         functools.partial(first_kernel, nb - 1),
-        (start, load, diag, one, two, lines_mult, *weights, mask, port_row, port_col, port_current),
-        [VMEM_SPEC] * 11 + [SMEM_SPEC] * 3,
+        (start, load, diag, one, two, lines_mult, mask, port_row, port_col, port_current, *weights),
+        [VMEM_SPEC] * 7 + [SMEM_SPEC] * 3 + [VMEM_SPEC] * len(weights),
         [whole, some, held((2, high, (nb - 1) * size)), some],
         4 * MIB,
         flops=step * (nb - 1),
     )
     f1e, f2s, f2e, f3e, far = call(
-        far_kernel,
-        (start, f0e, f1, src, diag, dge, *weights, mask, *incoming),
-        [VMEM_SPEC] * (11 + len(incoming)),
+        functools.partial(far_kernel, len(incoming)),
+        (start, f0e, f1, src, diag, dge, mask, *incoming, *weights),
+        [VMEM_SPEC] * (7 + len(incoming) + len(weights)),
         [
             held((2, high, size)),
             held((2, high, fill * size)),
@@ -512,8 +554,8 @@
     ends = [to_chip(far, step) if step else far for step in range(count // 2)]
     f2, f3 = call(
         middle_kernel,
-        (f1, f2s, src, diag, dge, *weights, mask),
-        [VMEM_SPEC] * 10,
+        (f1, f2s, src, diag, dge, mask, *weights),
+        [VMEM_SPEC] * (6 + len(weights)),
         [held((2, high, (nb - 2 - fill) * size)), held((2, rows, done * size))],
         4 * MIB,
         flops=step * (nb - 2 - fill + done),
@@ -524,8 +566,8 @@
     theirs = swap_cores(theirs)
     solved = call(
         last_kernel,
-        (f2s, f2, f2e, f3, f3e, src, diag, dge, *weights, mask),
-        [VMEM_SPEC] * 13,
+        (f2s, f2, f2e, f3, f3e, src, diag, dge, mask, *weights),
+        [VMEM_SPEC] * (9 + len(weights)),
         jax.ShapeDtypeStruct((2, rows, width), jnp.float32),
         4 * MIB + 8 * rows * width,
         [pltpu.VMEM((nb - 1 - done, 2, rows, size), jnp.float32), pltpu.SemaphoreType.DMA((nb + 1 - done,))],

time: 43.5 us -> 42.4 us (0.975); the launches traced: 42.8 us -> 42.2 us
  starting transfers between devices: 16.9 us -> 14.4 us
  waiting for transfers between devices: 1.26 us -> 3.2 us
    ppermute x6 -> x3, starting transfers between devices: 10.7 us -> 3.92 us  [to_chip(): lax.ppermute(cells, 'sub', [(i, (i + 2 * step) % count) for i in range(co...]
    ppermute x0 -> x2, starting transfers between devices: none -> 4.32 us  [over_bit(): lax.ppermute(cells, 'sub', [(i, i ^ 2 * bit) for i in range(lax.axis_size...]
    ppermute x0 -> x2, waiting for transfers between devices: none -> 2.33 us  [over_bit(): lax.ppermute(cells, 'sub', [(i, i ^ 2 * bit) for i in range(lax.axis_size...]
    pallas_call x12 -> x14, Pallas kernels: 23 us -> 23 us  [call(): pl.pallas_call(kernel, out_shape=outs, in_specs=specs, out_specs=out_spec...]
  transfers between devices with their start and end apart: 12 -> 11, of which waited for: 2 -> 4; matrix products, arithmetic and copies ran while one was open for 0% -> 0% of each run, Pallas kernels for 39% -> 40%
where the time goes in v4:
time: 42.4 us; the launch traced here: 42.2 us
  Pallas kernels  23 us (54%)
  starting transfers between devices  14.4 us (34%)
  waiting for transfers between devices  3.2 us (8%)
  between operations  0.9 us (2%)
  other arithmetic  0.65 us (2%)
    pallas_call x14, Pallas kernels, call(): pl.pallas_call(kernel, out_shape=outs, in_specs=specs, out_specs=out_spec...  23 us
    ppermute x4, starting transfers between devices, swap_edges(): return (lax.ppermute(one, 'tile', first), lax.ppermute(two, 'tile', second))  6.01 us
    ppermute x2, starting transfers between devices, over_bit(): lax.ppermute(cells, 'sub', [(i, i ^ 2 * bit) for i in range(lax.axis_size...  4.32 us
    ppermute x3, starting transfers between devices, to_chip(): lax.ppermute(cells, 'sub', [(i, (i + 2 * step) % count) for i in range(co...  3.92 us
    ppermute x2, waiting for transfers between devices, over_bit(): lax.ppermute(cells, 'sub', [(i, i ^ 2 * bit) for i in range(lax.axis_size...  2.33 us
  transfers between devices with their start and end apart: 11, of which 4 were waited for; matrix products, arithmetic and copies ran while one was open for 0% of the time, Pallas kernels for 40%

profile of v4, /device:TPU:0, one launch (start us, length us, event | category | flops | bytes accessed | tf_op | source)
XLA Modules:
  0.0 42.2 jit_solution(18279408490403551320)
XLA Ops:
  0.6 0.0 slice-start
  0.6 2.8 %shard_map.122 = (f32[2,8,128]{2,1,0:T(8,128)S(1)}, f32[2,8,128]{2,1,0:T(8,128)S(1)}, f32[2,8,3584]{2,1,0:T(8,128)S(1)}, f32[2,8,3584]{2,1,0:T(8,128)S(1)}, s32[...) custom-call(f32[2,64,4096]{2,1,0:T(8,128)} %bitcast.25, f32[2,64,4096]{2,1,0:T(8,128)} %bitcast.28, f32[2,64,4096]{2,1,0:T(8,128)} %bitcast.20, ...), custom_call_target="tpu_custom_call" | custom-call | tf_op jit(solution)/shard_map/pallas_call | solution.py:24
  3.4 0.0 slice-start.1
  3.5 0.0 slice-start.2
  3.5 0.0 slice-start.3
  3.5 3.0 %collective-permute-start.2 = (f32[2,8,128]{2,1,0:T(8,128)S(1)}, f32[2,8,128]{2,1,0:T(8,128)S(1)}, u32[]{:S(2)}, u32[]{:S(2)}) collective-permute-start(f32[2,8,128]{2,1,0:T(8,128)S(1)} %get-tuple-element.39), channel_id=1, source_target_pairs={{0,1},{1,0},{2,3},{3,2},{4,5},{5,4},{6,7},{7,6},{8,9},{9,8},{10,11... | collective-permute-start | bytes 24584 | tf_op jit(solution)/shard_map/ppermute | solution.py:182
  6.5 1.5 %collective-permute-start.3 = (f32[2,8,128]{2,1,0:T(8,128)S(1)}, f32[2,8,128]{2,1,0:T(8,128)S(1)}, u32[]{:S(2)}, u32[]{:S(2)}) collective-permute-start(f32[2,8,128]{2,1,0:T(8,128)S(1)} %get-tuple-element.40), channel_id=1, source_target_pairs={{0,3},{1,2},{2,1},{3,0},{4,7},{5,6},{6,5},{7,4},{8,11},{9,10},{10,... | collective-permute-start | bytes 24584 | tf_op jit(solution)/shard_map/ppermute | solution.py:182
  8.0 1.5 %collective-permute-start = (f32[2,8,3584]{2,1,0:T(8,128)S(1)}, f32[2,8,3584]{2,1,0:T(8,128)S(1)}, u32[]{:S(2)}, u32[]{:S(2)}) collective-permute-start(f32[2,8,3584]{2,1,0:T(8,128)S(1)} %get-tuple-element.35), channel_id=1, source_target_pairs={{0,1},{1,0},{2,3},{3,2},{4,5},{5,4},{6,7},{7,6},{8,9},{9,8},{10,11... | collective-permute-start | bytes 688136 | tf_op jit(solution)/shard_map/ppermute | solution.py:182
  9.5 0.0 collective-permute-start.1
  9.5 0.0 slice-done
  9.5 0.0 slice-done.1
  9.5 0.0 slice-done.2
  9.5 0.0 slice-done.3
  9.5 0.0 copy-start.3
  9.6 1.1 %shard_map.125 = (bf16[4,512,512]{2,1,0:T(8,128)(2,1)S(1)}, bf16[4,512,512]{2,1,0:T(8,128)(2,1)S(1)}, f32[8,128]{1,0:T(8,128)S(1)}) custom-call(f32[16,2048,128]{2,1,0:T(8,128)S(1)} %bitcast.17, f32[80,128]{1,0:T(8,128)S(1)} %shard_map.124._.mask_ref), custom_call_target="tpu_custom_call" | custom-call | bytes 8388608 | tf_op jit(solution)/shard_map/pallas_call | solution.py:24
  10.7 0.0 collective-permute-done.2.one_ref
  10.7 0.5 %collective-permute-done.3.two_ref = f32[2,8,128]{2,1,0:T(8,128)S(1)} collective-permute-done((f32[2,8,128]{2,1,0:T(8,128)S(1)}, f32[2,8,128]{2,1,0:T(8,128)S(1)}, u32[]{:S(2)}, u32[]{:S(2)}) %collective-permute-start.3) | collective-permute-done | bytes 8224 | tf_op jit(solution)/shard_map/ppermute | solution.py:182
  11.2 0.0 copy-done.3
  11.2 0.1 collective-permute-start.4
  11.3 1.1 %shard_map.127 = (bf16[4,512,512]{2,1,0:T(8,128)(2,1)S(1)}, bf16[4,512,512]{2,1,0:T(8,128)(2,1)S(1)}, f32[8,128]{1,0:T(8,128)S(1)}) custom-call(f32[16,2048,128]{2,1,0:T(8,128)S(1)} %bitcast.18, f32[8,128]{1,0:T(8,128)S(1)} %get-tuple-element.42._), custom_call_target="tpu_custom_call" | custom-call | bytes 8388608 | tf_op jit(solution)/shard_map/pallas_call | solution.py:24
  12.4 0.1 collective-permute-done.4.other_ref
  12.5 0.1 shard_map.128
  12.6 1.7 %collective-permute-start.5 = (f32[2,2,72,128]{3,2,1,0:T(8,128)S(1)}, f32[2,2,72,128]{3,2,1,0:T(8,128)S(1)}, u32[]{:S(2)}, u32[]{:S(2)}) collective-permute-start(f32[2,2,72,128]{3,2,1,0:T(8,128)S(1)} %get-tuple-element.56), channel_id=1, source_target_pairs={{0,8},{4,12},{8,0},{12,4},{16,24},{20,28},{24,16},{28,20},{1,9},{5... | collective-permute-start | bytes 442376 | tf_op jit(solution)/shard_map/ppermute | solution.py:215
  14.2 0.0 copy-start
  14.3 0.0 copy-start.1
  14.3 0.0 copy-start.2
  14.3 0.0 copy-start.4
  14.3 0.0 copy-start.5
  14.3 0.0 copy-start.6
  14.3 2.2 %shard_map.129 = (bf16[8,512,512]{2,1,0:T(8,128)(2,1)S(1)}, bf16[8,512,512]{2,1,0:T(8,128)(2,1)S(1)}, f32[8,128]{1,0:T(8,128)S(1)}) custom-call(f32[16,2048,128]{2,1,0:T(8,128)S(1)} %bitcast.19, f32[2,2,72,128]{3,2,1,0:T(8,128)S(1)} %get-tuple-element.49._.keep_ref), custom_call_target="tpu_custom_call" | custom-call | bytes 16777216 | tf_op jit(solution)/shard_map/pallas_call | solution.py:24
  16.5 2.3 %collective-permute-done.5.got_ref = f32[2,2,72,128]{3,2,1,0:T(8,128)S(1)} collective-permute-done((f32[2,2,72,128]{3,2,1,0:T(8,128)S(1)}, f32[2,2,72,128]{3,2,1,0:T(8,128)S(1)}, u32[]{:S(2)}, u32[]{:S(2)}) %collective-permute-start.5) | collective-permute-done | bytes 147488 | tf_op jit(solution)/shard_map/ppermute | solution.py:215
  18.9 2.7 %collective-permute-start.6 = (f32[1,2,72,128]{3,2,1,0:T(8,128)S(1)}, f32[1,2,72,128]{3,2,1,0:T(8,128)S(1)}, u32[]{:S(2)}, u32[]{:S(2)}) collective-permute-start(f32[1,2,72,128]{3,2,1,0:T(8,128)S(1)} %get-tuple-element.59), channel_id=1, source_target_pairs={{0,16},{4,20},{8,24},{12,28},{16,0},{20,4},{24,8},{28,12},{1,17},{... | collective-permute-start | bytes 221192 | tf_op jit(solution)/shard_map/ppermute | solution.py:215
  21.5 0.0 collective-permute-done.one_ref
  21.5 0.0 collective-permute-done.1.two_ref
  21.5 0.0 copy-done
  21.5 0.0 copy-done.1
  21.6 0.0 copy-done.2
  21.6 0.0 copy-done.4
  21.6 0.0 copy-done.5
  21.6 0.0 copy-done.6
  21.6 5.1 %shard_map.130 = (f32[2,80,4096]{2,1,0:T(8,128)S(1)}, f32[2,16,4096]{2,1,0:T(8,128)S(1)}, f32[2,80,3840]{2,1,0:T(8,128)S(1)}, f32[2,16,4096]{2,1,0:T(8,128)S(1)}) custom-call(f32[2,64,4096]{2,1,0:T(8,128)S(1)} %bitcast.26, f32[2,64,4096]{2,1,0:T(8,128)S(1)} %bitcast.29, f32[2,64,4096]{2,1,0:T(8,128)S(1)} %bitcast.21, ...), custom_call_target="tpu_custom_call" | custom-call | flops 1887436800 | tf_op jit(solution)/shard_map/pallas_call | solution.py:24
  26.7 0.0 collective-permute-done.6
  26.8 3.2 %shard_map.132 = (f32[2,80,256]{2,1,0:T(8,128)}, f32[2,80,1536]{2,1,0:T(8,128)S(1)}, f32[2,80,512]{2,1,0:T(8,128)S(1)}, f32[2,64,256]{2,1,0:T(8,128)S(1)}, f32[2,64,128]{2,1,0:T(8,128)S(1)}) custom-call(f32[2,64,4096]{2,1,0:T(8,128)S(1)} %bitcast.27, f32[2,16,4096]{2,1,0:T(8,128)S(1)} %get-tuple-element.52.f0e_ref, ...), custom_call_target="tpu_custom_call" | custom-call | flops 1258291200 | tf_op jit(solution)/shard_map/pallas_call | solution.py:24
  30.0 1.6 %collective-permute-start.7 = (f32[2,64,128]{2,1,0:T(8,128)S(1)}, f32[2,64,128]{2,1,0:T(8,128)S(1)}, u32[]{:S(2)}, u32[]{:S(2)}) collective-permute-start(f32[2,64,128]{2,1,0:T(8,128)S(1)} %get-tuple-element.65.refs_0_), channel_id=1, source_target_pairs={{0,8},{4,12},{8,16},{12,20},{16,24},{20,28},{24,0},{28,4},{1,9},{5... | collective-permute-start | bytes 196616 | tf_op jit(solution)/shard_map/ppermute | solution.py:187
  31.5 1.0 %collective-permute-start.8 = (f32[2,64,128]{2,1,0:T(8,128)S(1)}, f32[2,64,128]{2,1,0:T(8,128)S(1)}, u32[]{:S(2)}, u32[]{:S(2)}) collective-permute-start(f32[2,64,128]{2,1,0:T(8,128)S(1)} %get-tuple-element.65.refs_0_), channel_id=1, source_target_pairs={{0,16},{4,20},{8,24},{12,28},{16,0},{20,4},{24,8},{28,12},{1,17},{... | collective-permute-start | bytes 196616 | tf_op jit(solution)/shard_map/ppermute | solution.py:187
  32.5 1.4 %collective-permute-start.9 = (f32[2,64,128]{2,1,0:T(8,128)S(1)}, f32[2,64,128]{2,1,0:T(8,128)S(1)}, u32[]{:S(2)}, u32[]{:S(2)}) collective-permute-start(f32[2,64,128]{2,1,0:T(8,128)S(1)} %get-tuple-element.65.refs_0_), channel_id=1, source_target_pairs={{0,24},{4,28},{8,0},{12,4},{16,8},{20,12},{24,16},{28,20},{1,25},{... | collective-permute-start | bytes 196616 | tf_op jit(solution)/shard_map/ppermute | solution.py:187
  33.9 4.3 %shard_map.133 = (f32[2,80,2048]{2,1,0:T(8,128)S(1)}, f32[2,64,2048]{2,1,0:T(8,128)S(1)}) custom-call(f32[2,80,3840]{2,1,0:T(8,128)S(1)} %get-tuple-element.53.f1_ref, f32[2,80,1536]{2,1,0:T(8,128)S(1)} %get-tuple-element.60.f2s_ref, f32[2,80,4096]{2,1,0:T(8,128)S(1)} %get-tuple-element.54.src_ref, f32[2,64,4096]{2,1,0:T(8,128)S(1)} %bitcast.23, ...), custom_call_target="tpu_custom_call" | custom-call | flops 2013265920 | tf_op jit(solution)/shard_map/pallas_call | solution.py:24
  38.2 0.0 collective-permute-done.7.refs_1_
  38.2 0.3 collective-permute-done.8.refs_2_
  38.5 0.0 collective-permute-done.9.refs_3_
  38.5 0.1 shard_map.135
  38.6 0.1 collective-permute-start.10
  38.7 2.8 %shard_map.134 = f32[2,64,4096]{2,1,0:T(8,128)} custom-call(f32[2,80,1536]{2,1,0:T(8,128)S(1)} %get-tuple-element.60.f2s_ref, f32[2,80,2048]{2,1,0:T(8,128)S(1)} %get-tuple-element.61.f2_ref, f32[2,80,512]{2,1,0:T(8,128)S(1)} %get-tuple-element.62.f2e_ref, f32[2,64,2048]{2,1,0:T(8,128)S(1)} %get-tuple-element.63.f3_ref, ...), custom_call_target="tpu_custom_call" | custom-call | flops 880803840 | tf_op jit(solution)/shard_map/pallas_call | solution.py:24
  41.5 0.0 collective-permute-done.10
  41.5 0.7 %add_bitcast_fusion = f32[1,2,64,128]{3,2,1,0:T(8,128)} fusion(f32[2,64,128]{2,1,0:T(8,128)S(1)} %get-tuple-element.66, f32[2,64,128]{2,1,0:T(8,128)S(1)} %collective-permute-done.10, f32[2,64,2048]{2,1,0:T(8,128)S(1)} %get-tuple-element.63.f3_ref, f32[1,2,64,128]{3,2,1,0:T(8,128)S(1)} %copy-done.3), kind=kLoop, calls=%fused_computation | loop fusion | flops 49152 | bytes 327680 | tf_op jit(solution)/shard_map/broadcast_in_dim | solution.py:578
  (5 shorter events, 0.0 us)
Async XLA Ops:
  0.6 8.9 %slice-start = ((s8[16777216]{0:T(1024)(128)(4,1)}), s8[4194304]{0:T(1024)(128)(4,1)S(1)}, s32[]{:S(2)}) async-start(s8[16777216]{0:T(1024)(128)(4,1)} %bitcast.15), calls=%async_computation | async-start | bytes 8388608
  3.4 6.1 %slice-start.1 = ((s8[16777216]{0:T(1024)(128)(4,1)}), s8[4194304]{0:T(1024)(128)(4,1)S(1)}, s32[]{:S(2)}) async-start(s8[16777216]{0:T(1024)(128)(4,1)} %bitcast.15), calls=%async_computation.1 | async-start | bytes 8388608
  3.5 6.1 %slice-start.2 = ((s8[16777216]{0:T(1024)(128)(4,1)}), s8[4194304]{0:T(1024)(128)(4,1)S(1)}, s32[]{:S(2)}) async-start(s8[16777216]{0:T(1024)(128)(4,1)} %bitcast.15), calls=%async_computation.2 | async-start | bytes 8388608
  3.5 6.1 %slice-start.3 = ((s8[16777216]{0:T(1024)(128)(4,1)}), s8[4194304]{0:T(1024)(128)(4,1)S(1)}, s32[]{:S(2)}) async-start(s8[16777216]{0:T(1024)(128)(4,1)} %bitcast.15), calls=%async_computation.3 | async-start | bytes 8388608
  3.5 7.2 %collective-permute-start.2 = (f32[2,8,128]{2,1,0:T(8,128)S(1)}, f32[2,8,128]{2,1,0:T(8,128)S(1)}, u32[]{:S(2)}, u32[]{:S(2)}) collective-permute-start(f32[2,8,128]{2,1,0:T(8,128)S(1)} %get-tuple-element.39), channel_id=1, source_target_pairs={{0,1},{1,0},{2,3},{3,2},{4,5},{5,4},{6,7},{7,6},{8,9},{9,8},{10,11... | collective-permute-start | bytes 24584 | tf_op jit(solution)/shard_map/ppermute | solution.py:182
  6.5 4.7 %collective-permute-start.3 = (f32[2,8,128]{2,1,0:T(8,128)S(1)}, f32[2,8,128]{2,1,0:T(8,128)S(1)}, u32[]{:S(2)}, u32[]{:S(2)}) collective-permute-start(f32[2,8,128]{2,1,0:T(8,128)S(1)} %get-tuple-element.40), channel_id=1, source_target_pairs={{0,3},{1,2},{2,1},{3,0},{4,7},{5,6},{6,5},{7,4},{8,11},{9,10},{10,... | collective-permute-start | bytes 24584 | tf_op jit(solution)/shard_map/ppermute | solution.py:182
  8.0 13.5 %collective-permute-start = (f32[2,8,3584]{2,1,0:T(8,128)S(1)}, f32[2,8,3584]{2,1,0:T(8,128)S(1)}, u32[]{:S(2)}, u32[]{:S(2)}) collective-permute-start(f32[2,8,3584]{2,1,0:T(8,128)S(1)} %get-tuple-element.35), channel_id=1, source_target_pairs={{0,1},{1,0},{2,3},{3,2},{4,5},{5,4},{6,7},{7,6},{8,9},{9,8},{10,11... | collective-permute-start | bytes 688136 | tf_op jit(solution)/shard_map/ppermute | solution.py:182
  9.5 12.1 %collective-permute-start.1 = (f32[2,8,3584]{2,1,0:T(8,128)S(1)}, f32[2,8,3584]{2,1,0:T(8,128)S(1)}, u32[]{:S(2)}, u32[]{:S(2)}) collective-permute-start(f32[2,8,3584]{2,1,0:T(8,128)S(1)} %get-tuple-element.36), channel_id=1, source_target_pairs={{0,3},{1,2},{2,1},{3,0},{4,7},{5,6},{6,5},{7,4},{8,11},{9,10},{10,... | collective-permute-start | bytes 688136 | tf_op jit(solution)/shard_map/ppermute | solution.py:182
  9.5 1.6 %copy-start.3 = (f32[1,2,64,128]{3,2,1,0:T(8,128)S(1)}, f32[1,2,64,128]{3,2,1,0:T(8,128)}, u32[]{:S(2)}) copy-start(f32[1,2,64,128]{3,2,1,0:T(8,128)} %param.15) | copy-start | bytes 196612
  11.2 1.3 %collective-permute-start.4 = (f32[2,72,128]{2,1,0:T(8,128)S(1)}, f32[2,72,128]{2,1,0:T(8,128)S(1)}, u32[]{:S(2)}, u32[]{:S(2)}) collective-permute-start(f32[2,72,128]{2,1,0:T(8,128)S(1)} %shard_map.126.own_ref.mult_ref), channel_id=1, source_target_pairs={{0,4},{4,0},{8,12},{12,8},{16,20},{20,16},{24,28},{28,24},{1,5},{5... | collective-permute-start | bytes 221192 | tf_op jit(solution)/shard_map/ppermute | solution.py:191
  12.6 6.2 %collective-permute-start.5 = (f32[2,2,72,128]{3,2,1,0:T(8,128)S(1)}, f32[2,2,72,128]{3,2,1,0:T(8,128)S(1)}, u32[]{:S(2)}, u32[]{:S(2)}) collective-permute-start(f32[2,2,72,128]{3,2,1,0:T(8,128)S(1)} %get-tuple-element.56), channel_id=1, source_target_pairs={{0,8},{4,12},{8,0},{12,4},{16,24},{20,28},{24,16},{28,20},{1,9},{5... | collective-permute-start | bytes 442376 | tf_op jit(solution)/shard_map/ppermute | solution.py:215
  14.2 7.3 %copy-start = (f32[1,2,64,4096]{3,2,1,0:T(8,128)S(1)}, f32[1,2,64,4096]{3,2,1,0:T(8,128)}, u32[]{:S(2)}) copy-start(f32[1,2,64,4096]{3,2,1,0:T(8,128)} %param.12) | copy-start | bytes 6291460
  14.3 7.3 %copy-start.1 = (f32[1,2,64,4096]{3,2,1,0:T(8,128)S(1)}, f32[1,2,64,4096]{3,2,1,0:T(8,128)}, u32[]{:S(2)}) copy-start(f32[1,2,64,4096]{3,2,1,0:T(8,128)} %param.13) | copy-start | bytes 6291460
  14.3 7.3 %copy-start.2 = (f32[1,2,64,4096]{3,2,1,0:T(8,128)S(1)}, f32[1,2,64,4096]{3,2,1,0:T(8,128)}, u32[]{:S(2)}) copy-start(f32[1,2,64,4096]{3,2,1,0:T(8,128)} %param.11) | copy-start | bytes 6291460
  14.3 7.3 %copy-start.4 = (f32[1,2,16]{2,1,0:T(2,128)S(1)}, f32[1,2,16]{2,1,0:T(2,128)}, u32[]{:S(2)}) copy-start(f32[1,2,16]{2,1,0:T(2,128)} %pcur_ref.1) | copy-start | bytes 388
  14.3 7.3 %copy-start.5 = (s32[1,16]{1,0:T(1,128)S(1)}, s32[1,16]{1,0:T(1,128)}, u32[]{:S(2)}) copy-start(s32[1,16]{1,0:T(1,128)} %prow_ref.1) | copy-start | bytes 196
  14.3 7.3 %copy-start.6 = (s32[1,16]{1,0:T(1,128)S(1)}, s32[1,16]{1,0:T(1,128)}, u32[]{:S(2)}) copy-start(s32[1,16]{1,0:T(1,128)} %pcol_ref.1) | copy-start | bytes 196
  18.9 7.9 %collective-permute-start.6 = (f32[1,2,72,128]{3,2,1,0:T(8,128)S(1)}, f32[1,2,72,128]{3,2,1,0:T(8,128)S(1)}, u32[]{:S(2)}, u32[]{:S(2)}) collective-permute-start(f32[1,2,72,128]{3,2,1,0:T(8,128)S(1)} %get-tuple-element.59), channel_id=1, source_target_pairs={{0,16},{4,20},{8,24},{12,28},{16,0},{20,4},{24,8},{28,12},{1,17},{... | collective-permute-start | bytes 221192 | tf_op jit(solution)/shard_map/ppermute | solution.py:215
  30.0 8.3 %collective-permute-start.7 = (f32[2,64,128]{2,1,0:T(8,128)S(1)}, f32[2,64,128]{2,1,0:T(8,128)S(1)}, u32[]{:S(2)}, u32[]{:S(2)}) collective-permute-start(f32[2,64,128]{2,1,0:T(8,128)S(1)} %get-tuple-element.65.refs_0_), channel_id=1, source_target_pairs={{0,8},{4,12},{8,16},{12,20},{16,24},{20,28},{24,0},{28,4},{1,9},{5... | collective-permute-start | bytes 196616 | tf_op jit(solution)/shard_map/ppermute | solution.py:187
  31.5 7.0 %collective-permute-start.8 = (f32[2,64,128]{2,1,0:T(8,128)S(1)}, f32[2,64,128]{2,1,0:T(8,128)S(1)}, u32[]{:S(2)}, u32[]{:S(2)}) collective-permute-start(f32[2,64,128]{2,1,0:T(8,128)S(1)} %get-tuple-element.65.refs_0_), channel_id=1, source_target_pairs={{0,16},{4,20},{8,24},{12,28},{16,0},{20,4},{24,8},{28,12},{1,17},{... | collective-permute-start | bytes 196616 | tf_op jit(solution)/shard_map/ppermute | solution.py:187
  32.5 6.0 %collective-permute-start.9 = (f32[2,64,128]{2,1,0:T(8,128)S(1)}, f32[2,64,128]{2,1,0:T(8,128)S(1)}, u32[]{:S(2)}, u32[]{:S(2)}) collective-permute-start(f32[2,64,128]{2,1,0:T(8,128)S(1)} %get-tuple-element.65.refs_0_), channel_id=1, source_target_pairs={{0,24},{4,28},{8,0},{12,4},{16,8},{20,12},{24,16},{28,20},{1,25},{... | collective-permute-start | bytes 196616 | tf_op jit(solution)/shard_map/ppermute | solution.py:187
  38.6 2.9 %collective-permute-start.10 = (f32[2,64,128]{2,1,0:T(8,128)S(1)}, f32[2,64,128]{2,1,0:T(8,128)S(1)}, u32[]{:S(2)}, u32[]{:S(2)}) collective-permute-start(f32[2,64,128]{2,1,0:T(8,128)S(1)} %get-tuple-element.67), channel_id=1, source_target_pairs={{0,4},{4,0},{8,12},{12,8},{16,20},{20,16},{24,28},{28,24},{1,5},{5... | collective-permute-start | bytes 196616 | tf_op jit(solution)/shard_map/ppermute | solution.py:191

commit v5 on v4

--- a/solution.py
+++ b/solution.py
@@ -20,13 +20,14 @@
 ANY_SPEC = pl.BlockSpec(memory_space=pl.ANY)
 
 
-def call(kernel, args, specs, outs, limit, scratch=(), flops=0, moved=0, out_specs=None):
+def call(kernel, args, specs, outs, limit, scratch=(), flops=0, moved=0, out_specs=None, aliases=None):
     return pl.pallas_call(
         kernel,
         out_shape=outs,
         in_specs=specs,
         out_specs=out_specs or jax.tree.map(lambda _: VMEM_SPEC, outs),
         scratch_shapes=scratch,
+        input_output_aliases=aliases or {},
         compiler_params=pltpu.CompilerParams(vmem_limit_bytes=limit),
         cost_estimate=pl.CostEstimate(flops=flops, bytes_accessed=moved, transcendentals=0),
     )(*args)
@@ -215,7 +216,7 @@
     return lax.ppermute(cells, "sub", [(i, i ^ (2 * bit)) for i in range(lax.axis_size("sub"))])
 
 
-def sums_kernel(peers_ref, *refs):
+def sums_kernel(peers_ref, _, *refs):
     pieces, (mine_ref, theirs_ref) = refs[:-2], refs[-2:]
     me, count = lax.axis_index("sub"), 2 * len(pieces)
     rows = mine_ref.shape[1]
@@ -310,22 +311,67 @@
     return read
 
 
-def stored_source(source_ref, k, size):
-    return lambda c: source_ref[c, :, k * size : (k + 1) * size]
+def stored_source(source, k, size):
+    return lambda c: with_ends(*source, c, slice(k * size, (k + 1) * size))
+
+
+def sweep(w, field, source, diag, mask_ref, first, count, out_ref):
+    size = w.size
+    mask = line_mask(mask_ref, size)
+    rows = out_ref.shape[1]
+    lines = slice(PAD, PAD + rows) if rows < mask.shape[0] else slice(0, rows)
+    for i in range(count):
+        k = first + i
+        new = relax_block(field, stored_source(source, k, size), diag, w, k, mask)
+        for c in range(2):
+            out_ref[c, :, i * size : (i + 1) * size] = new[c][lines]
+
+
+def source_kernel(load_ref, mult_ref, prow_ref, pcol_ref, pcur_ref, src_ref, srce_ref):
+    _, rows, width = load_ref.shape
+    tile = lax.axis_index("tile")
+    src_ref[...] = load_ref[...]
+    srce_ref[...] = jnp.zeros_like(srce_ref)
+    for c in range(2):
+        src_ref[c, :, :IB] -= mult_ref[c, :rows]
+        srce_ref[c, :PAD, :IB] = -mult_ref[c, rows:]
+        srce_ref[c, PAD:, :IB] = -mult_ref[c, rows:]
+    span = PB + LANES
+    at_row = lax.broadcasted_iota(jnp.int32, (PAD, span), 0)
+    at_col = lax.broadcasted_iota(jnp.int32, (PAD, span), 1)
+    for p in range(prow_ref.shape[1]):
+        row = prow_ref[0, p] - tile * rows
+        col = pcol_ref[0, p]
+        base = pl.multiple_of(jnp.minimum(col // LANES * LANES, width - span), LANES)
+        hits_col = (at_col >= col - base) & (at_col < col - base + PB)
+
+        def add(ref, line, p=p, base=base, hits_col=hits_col):
+            first = pl.multiple_of(line // PAD * PAD, PAD)
+            for c in range(2):
+                where = (c, pl.ds(first, PAD), pl.ds(base, span))
+                hit = hits_col & (at_row == line - first)
+                ref[where] = ref[where] + jnp.where(hit, pcur_ref[0, c, p], 0.0)
+
+        @pl.when((row >= 0) & (row < rows))
+        def _():
+            add(src_ref, row)
+
+        @pl.when((row >= -PAD) & (row < 0))
+        def _():
+            add(srce_ref, row + PAD)
+
+        @pl.when((row >= rows) & (row < rows + PAD))
+        def _():
+            add(srce_ref, row - rows + PAD)
 
 
 def first_kernel(
-    upto, start_ref, load_ref, diag_ref, one_ref, two_ref, mult_ref, mask_ref,
-    prow_ref, pcol_ref, pcur_ref, *refs,
+    start_ref, diag_ref, one_ref, two_ref, src_ref, add_ref, mask_ref, *refs
 ):
-    w_refs, (src_ref, dge_ref, f1_ref, f0e_ref) = refs[:-4], refs[-4:]
-    _, rows, width = load_ref.shape
+    w_refs, (srce_ref, dge_ref, f0e_ref, f1_ref) = refs[:-4], refs[-4:]
     w = Weights(w_refs)
     size = w.size
-    own = slice(PAD, PAD + rows)
-    above, below = slice(0, PAD), slice(PAD + rows, 2 * PAD + rows)
-    tile = lax.axis_index("tile")
-    even = lax.rem(tile, 2) == 0
+    even = lax.rem(lax.axis_index("tile"), 2) == 0
     for c in range(2):
         one, two = one_ref[c], two_ref[c]
         up = unpack_rows(jnp.where(even, two, one))
@@ -334,39 +380,16 @@
         f0e_ref[c, PAD:] = down
         dge_ref[c, :PAD] = pltpu.roll(up, 1, 0)
         dge_ref[c, PAD:] = pltpu.roll(down, 3, 0)
-        src_ref[c, own, :] = load_ref[c]
-        src_ref[c, above, :] = pltpu.roll(up, 3, 0)
-        src_ref[c, below, :] = pltpu.roll(down, 5, 0)
-        src_ref[c, own, 0:IB] -= mult_ref[c, :rows]
-        src_ref[c, above, 0:IB] -= mult_ref[c, rows:]
-        src_ref[c, below, 0:IB] -= mult_ref[c, rows:]
-    span = PB + LANES
-    at_row = lax.broadcasted_iota(jnp.int32, (PAD, span), 0)
-    at_col = lax.broadcasted_iota(jnp.int32, (PAD, span), 1)
-    for p in range(prow_ref.shape[1]):
-        row = prow_ref[0, p] - tile * rows + PAD
-        col = pcol_ref[0, p]
-        base = pl.multiple_of(jnp.minimum(col // LANES * LANES, width - span), LANES)
-
-        @pl.when((row >= 0) & (row < rows + 2 * PAD))
-        def _(p=p, row=row, col=col, base=base):
-            first = pl.multiple_of(row // PAD * PAD, PAD)
-            hit = (at_row == row - first) & (at_col >= col - base) & (at_col < col - base + PB)
-            for c in range(2):
-                where = (c, pl.ds(first, PAD), pl.ds(base, span))
-                src_ref[where] = src_ref[where] + jnp.where(hit, pcur_ref[0, c, p], 0.0)
-
-    mask = line_mask(mask_ref, size)
-    f0 = start_reader(start_ref, f0e_ref, mask_ref)
-    dg_ref = (diag_ref, dge_ref)
-    for k in range(upto):
-        new = relax_block(f0, stored_source(src_ref, k, size), dg_ref, w, k, mask)
-        for c in range(2):
-            f1_ref[c, :, k * size : (k + 1) * size] = new[c]
+        srce_ref[c, :PAD] = add_ref[c, :PAD] + pltpu.roll(up, 3, 0)
+        srce_ref[c, PAD:] = add_ref[c, PAD:] + pltpu.roll(down, 5, 0)
+    sweep(
+        w, start_reader(start_ref, f0e_ref, mask_ref), (src_ref, srce_ref), (diag_ref, dge_ref), mask_ref,
+        0, f1_ref.shape[2] // size, f1_ref,
+    )
 
 
 def far_kernel(
-    count, start_ref, f0e_ref, f1_ref, src_ref, diag_ref, dge_ref, mask_ref, *refs
+    count, start_ref, f0e_ref, f1_ref, src_ref, srce_ref, diag_ref, dge_ref, mask_ref, *refs
 ):
     pieces, w_refs, (f1e_ref, f2s_ref, f2e_ref, f3e_ref, far_ref) = refs[:count], refs[count:-5], refs[-5:]
     w = Weights(w_refs)
@@ -380,89 +403,101 @@
             cells += piece[c]
         ends = jnp.concatenate([cells[rows:], cells[:rows], cells[rows:]], axis=0)
         into.append(jnp.concatenate([jnp.zeros((rows + 2 * PAD, size - IB), jnp.float32), ends], axis=1))
-    end = stored_source(src_ref, last, size)
+    source, diag = (src_ref, srce_ref), (diag_ref, dge_ref)
+    end = stored_source(source, last, size)
 
     def with_incoming(c):
         return end(c) + into[c]
 
-    dg_ref = (diag_ref, dge_ref)
-    new = relax_block(start_reader(start_ref, f0e_ref, mask_ref), with_incoming, dg_ref, w, last, mask)
+    new = relax_block(start_reader(start_ref, f0e_ref, mask_ref), with_incoming, diag, w, last, mask)
     for c in range(2):
         f1e_ref[c] = new[c]
+    old = reader([(0, f1_ref)], size)
     f1 = reader([(last, f1e_ref), (0, f1_ref)], size)
-    old = reader([(0, f1_ref)], size)
     fill = f2s_ref.shape[2] // size
 
-    def beside(k):
-        new = relax_block(old, stored_source(src_ref, k, size), dg_ref, w, k, mask)
-        for c in range(2):
-            f2s_ref[c, :, k * size : (k + 1) * size] = new[c]
-
-    for k in range(fill // 2):
-        beside(k)
-    for k, source in ((last, with_incoming), (last - 1, stored_source(src_ref, last - 1, size))):
-        new = relax_block(f1, source, dg_ref, w, k, mask)
+    def beside(first, count):
+        cols = pl.ds(first * size, count * size)
+        sweep(w, old, source, diag, mask_ref, first, count, f2s_ref.at[:, :, cols])
+
+    beside(0, fill // 2)
+    for k, at in ((last, with_incoming), (last - 1, stored_source(source, last - 1, size))):
+        new = relax_block(f1, at, diag, w, k, mask)
         for c in range(2):
             f2e_ref[c, :, (k - last + 1) * size : (k - last + 2) * size] = new[c]
-    for k in range(fill // 2, fill):
-        beside(k)
-    new = relax_block(reader([(last - 1, f2e_ref)], size), with_incoming, dg_ref, w, last, mask)
+    beside(fill // 2, fill - fill // 2)
+    new = relax_block(reader([(last - 1, f2e_ref)], size), with_incoming, diag, w, last, mask)
     for c in range(2):
         f3e_ref[c] = new[c][PAD : PAD + rows]
         far_ref[c] = new[c][PAD : PAD + rows, size - IB :]
 
 
-def middle_kernel(
-    f1_ref, f2s_ref, src_ref, diag_ref, dge_ref, mask_ref, *refs
-):
-    w_refs, (f2_ref, f3_ref) = refs[:-2], refs[-2:]
+def middle_kernel(f1_ref, f2s_ref, src_ref, srce_ref, diag_ref, dge_ref, mask_ref, *refs):
+    w_refs, (out_ref, f2_ref, f3_ref, sem) = refs[:-4], refs[-4:]
     w = Weights(w_refs)
     size = w.size
-    rows = f3_ref.shape[1]
-    first = f2s_ref.shape[2] // size
-    mask = line_mask(mask_ref, size)
-    dg_ref = (diag_ref, dge_ref)
+    first, done = f2s_ref.shape[2] // size, f3_ref.shape[2] // size
+    early = first - 1
+    source, diag = (src_ref, srce_ref), (diag_ref, dge_ref)
     f1 = reader([(0, f1_ref)], size)
-    for i in range(f2_ref.shape[2] // size):
-        k = first + i
-        new = relax_block(f1, stored_source(src_ref, k, size), dg_ref, w, k, mask)
-        for c in range(2):
-            f2_ref[c, :, i * size : (i + 1) * size] = new[c]
     f2 = reader([(0, f2s_ref), (first, f2_ref)], size)
-    for k in range(f3_ref.shape[2] // size):
-        new = relax_block(f2, stored_source(src_ref, k, size), dg_ref, w, k, mask)
-        for c in range(2):
-            f3_ref[c, :, k * size : (k + 1) * size] = new[c][PAD : PAD + rows]
+    sweep(w, f2, source, diag, mask_ref, 0, early, f3_ref.at[:, :, pl.ds(0, early * size)])
+    copies = [block_copy(f3_ref, k, out_ref, k, size, sem.at[k]) for k in range(early)]
+    for copy in copies:
+        copy.start()
+    sweep(w, f1, source, diag, mask_ref, first, f2_ref.shape[2] // size, f2_ref)
+    rest = pl.ds(early * size, (done - early) * size)
+    sweep(w, f2, source, diag, mask_ref, early, done - early, f3_ref.at[:, :, rest])
+    for copy in copies:
+        copy.wait()
+
+
+def block_copy(ref, k, out_ref, at, size, sem):
+    return pltpu.make_async_copy(
+        ref.at[:, :, pl.ds(k * size, size)], out_ref.at[:, :, pl.ds(at * size, size)], sem
+    )
+
+
+def third_kernel(early, _, f2s_ref, f2_ref, f3_ref, src_ref, srce_ref, diag_ref, dge_ref, mask_ref, _after, *refs):
+    w_refs, (out_ref, more_ref, sem) = refs[:-3], refs[-3:]
+    w = Weights(w_refs)
+    size = w.size
+    first = f3_ref.shape[2] // size
+    source, diag = (src_ref, srce_ref), (diag_ref, dge_ref)
+    copies = [block_copy(f3_ref, k, out_ref, k, size, sem.at[k]) for k in range(early, first)]
+    for copy in copies:
+        copy.start()
+    f2 = reader([(f2s_ref.shape[2] // size, f2_ref), (0, f2s_ref)], size)
+    sweep(w, f2, source, diag, mask_ref, first, more_ref.shape[2] // size, more_ref)
+    for copy in copies:
+        copy.wait()
 
 
 def last_kernel(
-    f2s_ref, f2_ref, f2e_ref, f3_ref, f3e_ref, src_ref, diag_ref, dge_ref, mask_ref, *refs
+    f2_first, _, f2_ref, f2e_ref, near_ref, f3_ref, f3e_ref, src_ref, srce_ref, diag_ref, dge_ref, mask_ref,
+    mult_ref, mine_ref, theirs_ref, *refs,
 ):
-    w_refs, (out_ref, held_ref, sem) = refs[:-3], refs[-3:]
+    w_refs, (out_ref, next_ref, held_ref, new_ref, sem) = refs[:-5], refs[-5:]
     w = Weights(w_refs)
     size, last = w.size, w.last
-    rows = out_ref.shape[1]
-    done = f3_ref.shape[2] // size
-    mask = line_mask(mask_ref, size)
-
-    def copy(ref, first, blocks, slot):
-        cols = pl.ds(first * size, blocks * size)
-        return pltpu.make_async_copy(ref, out_ref.at[:, :, cols], sem.at[slot])
-
-    copies = [copy(f3_ref, 0, done, 0), copy(f3e_ref, last, 1, 1)]
-    for one in copies:
-        one.start()
-    dg_ref = (diag_ref, dge_ref)
-    f2 = reader([(last - 1, f2e_ref), (f2s_ref.shape[2] // size, f2_ref), (0, f2s_ref)], size)
-    for i in range(last - done):
-        k = done + i
-        new = relax_block(f2, stored_source(src_ref, k, size), dg_ref, w, k, mask)
-        for c in range(2):
-            held_ref[i, c] = new[c][PAD : PAD + rows]
-        copies.append(copy(held_ref.at[i], k, 1, 2 + i))
+    count = held_ref.shape[0]
+    first = last - count
+    source, diag = (src_ref, srce_ref), (diag_ref, dge_ref)
+    more = f3_ref.shape[2] // size
+    copies = [block_copy(f3_ref, k, out_ref, first - more + k, size, sem.at[k]) for k in range(more)]
+    copies.append(block_copy(f3e_ref, 0, out_ref, last, size, sem.at[more]))
+    for copy in copies:
+        copy.start()
+    new_ref[...] = mult_ref[...] + (near_ref[:, :, :IB] - (mine_ref[...] + theirs_ref[...]))
+    copies.append(pltpu.make_async_copy(new_ref, next_ref, sem.at[more + 1]))
+    copies[-1].start()
+    f2 = reader([(last - 1, f2e_ref), (f2_first, f2_ref)], size)
+    for i in range(count):
+        sweep(w, f2, source, diag, mask_ref, first + i, 1, held_ref.at[i])
+        copies.append(block_copy(held_ref.at[i], 0, out_ref, first + i, size, sem.at[more + 2 + i]))
         copies[-1].start()
-    for one in copies:
-        one.wait()
+    for copy in copies:
+        copy.wait()
 
 
 def per_device(
@@ -482,9 +517,7 @@
     _, rows, width = load.shape
     nb, _, size, _, _ = block_inverse.shape[1:]
     high = rows + 2 * PAD
-    step = 6 * high * (2 * size) ** 2
-
-    fill, done = nb * 3 // 8, nb // 2
+
     count = lax.axis_size("sub")
 
     m1, m2, one, two, peers, mask = call(
@@ -520,27 +553,45 @@
     )
     got = over_bit(send, 1)
     w3, token = split_weights(flat, size, 2 * quarter, nb - 2 * quarter, keep)
+    weights = (*w1, *w2, *w3)
+    step = 6 * high * (2 * size) ** 2
+    some = held((2, 2 * PAD, width))
+
+    src, add = call(
+        source_kernel,
+        (load, lines_mult, port_row, port_col, port_current),
+        [VMEM_SPEC] * 2 + [SMEM_SPEC] * 3,
+        [held(load.shape), some],
+        2 * MIB,
+        moved=8 * MIB,
+    )
+
+    def run(kernel, args, outs, blocks, limit=4 * MIB, scratch=(), out_specs=None, aliased=False):
+        operands = (*args, *weights)
+        specs = [VMEM_SPEC] * len(operands)
+        if aliased:
+            specs[0] = ANY_SPEC
+        return call(
+            kernel, operands, specs, outs, limit, scratch, step * blocks, 0, out_specs, {0: 0} if aliased else {}
+        )
+
     bit = 1
     while keep.shape[0] > 1:
         keep, send = call(fold_kernel, (keep, got, token), [VMEM_SPEC] * 3, halved(keep), 2 * MIB)
         bit *= 2
         got = over_bit(send, bit)
     incoming = [keep[0], got[0]]
-    weights = (*w1, *w2, *w3)
-
-    whole, some = held((2, high, width)), held((2, 2 * PAD, width))
-    src, dge, f1, f0e = call(
-        functools.partial(first_kernel, nb - 1),
-        (start, load, diag, one, two, lines_mult, mask, port_row, port_col, port_current, *weights),
-        [VMEM_SPEC] * 7 + [SMEM_SPEC] * 3 + [VMEM_SPEC] * len(weights),
-        [whole, some, held((2, high, (nb - 1) * size)), some],
-        4 * MIB,
-        flops=step * (nb - 1),
-    )
-    f1e, f2s, f2e, f3e, far = call(
+    srce, dge, f0e, f1 = run(
+        first_kernel,
+        (start, diag, one, two, src, add, mask),
+        [some, some, some, held((2, high, (nb - 1) * size))],
+        nb - 1,
+    )
+    known = (src, srce, diag, dge, mask)
+    fill = nb * 3 // 8
+    f1e, f2s, f2e, f3e, far = run(
         functools.partial(far_kernel, len(incoming)),
-        (start, f0e, f1, src, diag, dge, mask, *incoming, *weights),
-        [VMEM_SPEC] * (7 + len(incoming) + len(weights)),
+        (start, f0e, f1, *known, *incoming),
         [
             held((2, high, size)),
             held((2, high, fill * size)),
@@ -548,33 +599,46 @@
             held((2, rows, size)),
             held((2, rows, IB)),
         ],
-        4 * MIB,
-        flops=step * (4 + fill),
-    )
-    ends = [to_chip(far, step) if step else far for step in range(count // 2)]
-    f2, f3 = call(
+        4 + fill,
+    )
+    ends = [to_chip(far, step) if step else far for step in range(chips)]
+    done, tail = nb * 5 // 8, nb // 8
+    whole = jax.ShapeDtypeStruct((2, rows, width), jnp.float32)
+    partly, f2, f3a = run(
         middle_kernel,
-        (f1, f2s, src, diag, dge, mask, *weights),
-        [VMEM_SPEC] * (6 + len(weights)),
-        [held((2, high, (nb - 2 - fill) * size)), held((2, rows, done * size))],
-        4 * MIB,
-        flops=step * (nb - 2 - fill + done),
+        (f1, f2s, *known),
+        [whole, held((2, high, (nb - 2 - fill) * size)), held((2, rows, done * size))],
+        nb - 2 - fill + done,
+        scratch=[pltpu.SemaphoreType.DMA((fill - 1,))],
+        out_specs=[ANY_SPEC, VMEM_SPEC, VMEM_SPEC],
     )
     mine, theirs = call(
-        sums_kernel, (peers, *ends), [VMEM_SPEC] * (1 + len(ends)), [held(far.shape)] * 2, MIB
+        sums_kernel, (peers, f3a, *ends), [VMEM_SPEC] * (2 + len(ends)), [held(far.shape)] * 2, MIB
     )
     theirs = swap_cores(theirs)
-    solved = call(
-        last_kernel,
-        (f2s, f2, f2e, f3, f3e, src, diag, dge, mask, *weights),
-        [VMEM_SPEC] * (9 + len(weights)),
-        jax.ShapeDtypeStruct((2, rows, width), jnp.float32),
-        4 * MIB + 8 * rows * width,
-        [pltpu.VMEM((nb - 1 - done, 2, rows, size), jnp.float32), pltpu.SemaphoreType.DMA((nb + 1 - done,))],
-        flops=step * (nb - 1 - done),
-        out_specs=ANY_SPEC,
-    )
-    updated = mult + (f3[:, :, :IB] - (mine + theirs))
+    more = nb - 1 - tail - done
+    partly, f3b = run(
+        functools.partial(third_kernel, fill - 1),
+        (partly, f2s, f2, f3a, *known, mine),
+        [whole, held((2, rows, more * size))],
+        more,
+        scratch=[pltpu.SemaphoreType.DMA((done,))],
+        out_specs=[ANY_SPEC, VMEM_SPEC],
+        aliased=True,
+    )
+    solved, updated = run(
+        functools.partial(last_kernel, fill),
+        (partly, f2, f2e, f3a, f3b, f3e, *known, mult, mine, theirs),
+        [whole, jax.ShapeDtypeStruct(mult.shape, jnp.float32)],
+        tail,
+        scratch=[
+            pltpu.VMEM((tail, 2, rows, size), jnp.float32),
+            pltpu.VMEM(mult.shape, jnp.float32),
+            pltpu.SemaphoreType.DMA((2 + more + tail,)),
+        ],
+        out_specs=[ANY_SPEC] * 2,
+        aliased=True,
+    )
     return (solved[None], updated[None])
 
 

time: 42.4 us -> 40.9 us (0.965)
  waiting for transfers between devices: 3.2 us -> 1.85 us
  other arithmetic: 0.65 us -> 0.01 us
    ppermute x2, waiting for transfers between devices: 2.33 us -> 1.27 us  [over_bit(): lax.ppermute(cells, 'sub', [(i, i ^ 2 * bit) for i in range(lax.axis_size...]
    broadcast_in_dim x1 -> x0, other arithmetic: 0.65 us -> none  [per_device(): return (solved[None], updated[None])]
    ppermute x3, starting transfers between devices: 3.92 us -> 4.35 us  [to_chip(): lax.ppermute(cells, 'sub', [(i, (i + 2 * step) % count) for i in range(co...]
    pallas_call x14 -> x16, Pallas kernels: 23 us -> 22.9 us  [call(): pl.pallas_call(kernel, out_shape=outs, in_specs=specs, out_specs=out_spec...]
  transfers between devices with their start and end apart: 11 -> 11, of which waited for: 4 -> 4; matrix products, arithmetic and copies ran while one was open for 0% -> 0% of each run, Pallas kernels for 40% -> 38%
where the time goes in v5:
time: 40.9 us; the launch traced here: 40.7 us
  Pallas kernels  22.9 us (56%)
  starting transfers between devices  14.8 us (36%)
  waiting for transfers between devices  1.85 us (5%)
  between operations  1.07 us (3%)
    pallas_call x16, Pallas kernels, call(): pl.pallas_call(kernel, out_shape=outs, in_specs=specs, out_specs=out_spec...  22.9 us
    ppermute x4, starting transfers between devices, swap_edges(): return (lax.ppermute(one, 'tile', first), lax.ppermute(two, 'tile', second))  6.01 us
    ppermute x3, starting transfers between devices, to_chip(): lax.ppermute(cells, 'sub', [(i, (i + 2 * step) % count) for i in range(co...  4.35 us
    ppermute x2, starting transfers between devices, over_bit(): lax.ppermute(cells, 'sub', [(i, i ^ 2 * bit) for i in range(lax.axis_size...  4.32 us
    ppermute x2, waiting for transfers between devices, over_bit(): lax.ppermute(cells, 'sub', [(i, i ^ 2 * bit) for i in range(lax.axis_size...  1.27 us
  transfers between devices with their start and end apart: 11, of which 4 were waited for; matrix products, arithmetic and copies ran while one was open for 0% of the time, Pallas kernels for 38%

profile of v5, /device:TPU:0, one launch (start us, length us, event | category | flops | bytes accessed | tf_op | source)
XLA Modules:
  0.0 40.7 jit_solution(1076379776240729707)
XLA Ops:
  0.6 0.0 slice-start
  0.6 2.8 %shard_map.122 = (f32[2,8,128]{2,1,0:T(8,128)S(1)}, f32[2,8,128]{2,1,0:T(8,128)S(1)}, f32[2,8,3584]{2,1,0:T(8,128)S(1)}, f32[2,8,3584]{2,1,0:T(8,128)S(1)}, s32[...) custom-call(f32[2,64,4096]{2,1,0:T(8,128)} %bitcast.24, f32[2,64,4096]{2,1,0:T(8,128)} %bitcast.27, f32[2,64,4096]{2,1,0:T(8,128)} %bitcast.18, ...), custom_call_target="tpu_custom_call" | custom-call | tf_op jit(solution)/shard_map/pallas_call | solution.py:24
  3.4 0.0 slice-start.1
  3.5 0.0 slice-start.2
  3.5 0.0 slice-start.3
  3.5 3.0 %collective-permute-start.2 = (f32[2,8,128]{2,1,0:T(8,128)S(1)}, f32[2,8,128]{2,1,0:T(8,128)S(1)}, u32[]{:S(2)}, u32[]{:S(2)}) collective-permute-start(f32[2,8,128]{2,1,0:T(8,128)S(1)} %get-tuple-element.46), channel_id=1, source_target_pairs={{0,1},{1,0},{2,3},{3,2},{4,5},{5,4},{6,7},{7,6},{8,9},{9,8},{10,11... | collective-permute-start | bytes 24584 | tf_op jit(solution)/shard_map/ppermute | solution.py:183
  6.5 1.5 %collective-permute-start.3 = (f32[2,8,128]{2,1,0:T(8,128)S(1)}, f32[2,8,128]{2,1,0:T(8,128)S(1)}, u32[]{:S(2)}, u32[]{:S(2)}) collective-permute-start(f32[2,8,128]{2,1,0:T(8,128)S(1)} %get-tuple-element.47), channel_id=1, source_target_pairs={{0,3},{1,2},{2,1},{3,0},{4,7},{5,6},{6,5},{7,4},{8,11},{9,10},{10,... | collective-permute-start | bytes 24584 | tf_op jit(solution)/shard_map/ppermute | solution.py:183
  8.0 1.5 %collective-permute-start = (f32[2,8,3584]{2,1,0:T(8,128)S(1)}, f32[2,8,3584]{2,1,0:T(8,128)S(1)}, u32[]{:S(2)}, u32[]{:S(2)}) collective-permute-start(f32[2,8,3584]{2,1,0:T(8,128)S(1)} %get-tuple-element.42), channel_id=1, source_target_pairs={{0,1},{1,0},{2,3},{3,2},{4,5},{5,4},{6,7},{7,6},{8,9},{9,8},{10,11... | collective-permute-start | bytes 688136 | tf_op jit(solution)/shard_map/ppermute | solution.py:183
  9.5 0.0 collective-permute-start.1
  9.5 0.0 slice-done
  9.5 0.0 slice-done.1
  9.5 0.0 slice-done.2
  9.5 0.0 slice-done.3
  9.5 0.0 copy-start.3
  9.6 1.1 %shard_map.125 = (bf16[4,512,512]{2,1,0:T(8,128)(2,1)S(1)}, bf16[4,512,512]{2,1,0:T(8,128)(2,1)S(1)}, f32[8,128]{1,0:T(8,128)S(1)}) custom-call(f32[16,2048,128]{2,1,0:T(8,128)S(1)} %bitcast.15, f32[80,128]{1,0:T(8,128)S(1)} %shard_map.124._.mask_ref), custom_call_target="tpu_custom_call" | custom-call | bytes 8388608 | tf_op jit(solution)/shard_map/pallas_call | solution.py:24
  10.7 0.0 collective-permute-done.2.one_ref
  10.7 0.5 %collective-permute-done.3.two_ref = f32[2,8,128]{2,1,0:T(8,128)S(1)} collective-permute-done((f32[2,8,128]{2,1,0:T(8,128)S(1)}, f32[2,8,128]{2,1,0:T(8,128)S(1)}, u32[]{:S(2)}, u32[]{:S(2)}) %collective-permute-start.3) | collective-permute-done | bytes 8224 | tf_op jit(solution)/shard_map/ppermute | solution.py:183
  11.2 0.0 copy-done.3
  11.2 0.0 copy-start.2
  11.2 0.0 copy-start.4
  11.2 0.0 copy-start.5
  11.2 0.0 copy-start.6
  11.3 0.1 collective-permute-start.4
  11.3 1.1 %shard_map.128 = (bf16[4,512,512]{2,1,0:T(8,128)(2,1)S(1)}, bf16[4,512,512]{2,1,0:T(8,128)(2,1)S(1)}, f32[8,128]{1,0:T(8,128)S(1)}) custom-call(f32[16,2048,128]{2,1,0:T(8,128)S(1)} %bitcast.16, f32[8,128]{1,0:T(8,128)S(1)} %get-tuple-element.49._), custom_call_target="tpu_custom_call" | custom-call | bytes 8388608 | tf_op jit(solution)/shard_map/pallas_call | solution.py:24
  12.5 0.1 collective-permute-done.4.other_ref
  12.6 0.1 shard_map.129
  12.6 1.7 %collective-permute-start.5 = (f32[2,2,72,128]{3,2,1,0:T(8,128)S(1)}, f32[2,2,72,128]{3,2,1,0:T(8,128)S(1)}, u32[]{:S(2)}, u32[]{:S(2)}) collective-permute-start(f32[2,2,72,128]{3,2,1,0:T(8,128)S(1)} %get-tuple-element.65), channel_id=1, source_target_pairs={{0,8},{4,12},{8,0},{12,4},{16,24},{20,28},{24,16},{28,20},{1,9},{5... | collective-permute-start | bytes 442376 | tf_op jit(solution)/shard_map/ppermute | solution.py:216
  14.3 0.0 copy-done.2
  14.3 0.0 copy-done.4
  14.3 0.0 copy-done.5
  14.3 0.0 copy-done.6
  14.3 1.2 %shard_map.127 = (f32[2,64,4096]{2,1,0:T(8,128)S(1)}, f32[2,16,4096]{2,1,0:T(8,128)S(1)}) custom-call(f32[2,64,4096]{2,1,0:T(8,128)S(1)} %bitcast.28, f32[2,72,128]{2,1,0:T(8,128)S(1)} %shard_map.126.mult_ref.own_ref, s32[1,16]{1,0:T(1,128)S(1)} %copy-done.5, s32[1,16]{1,0:T(1,128)S(1)} %copy-done.6, f32[1,2,16]{2,1,0:T(2,128)S(1)} %copy-done.4), custom_call_target="tpu_custom_call" | custom-call | bytes 8388608 | tf_op jit(solution)/shard_map/pallas_call | solution.py:24
  15.5 0.0 copy-start
  15.5 0.0 copy-start.1
  15.5 2.2 %shard_map.130 = (bf16[8,512,512]{2,1,0:T(8,128)(2,1)S(1)}, bf16[8,512,512]{2,1,0:T(8,128)(2,1)S(1)}, f32[8,128]{1,0:T(8,128)S(1)}) custom-call(f32[16,2048,128]{2,1,0:T(8,128)S(1)} %bitcast.17, f32[2,2,72,128]{3,2,1,0:T(8,128)S(1)} %get-tuple-element.58._.keep_ref), custom_call_target="tpu_custom_call" | custom-call | bytes 16777216 | tf_op jit(solution)/shard_map/pallas_call | solution.py:24
  17.8 1.1 %collective-permute-done.5.got_ref = f32[2,2,72,128]{3,2,1,0:T(8,128)S(1)} collective-permute-done((f32[2,2,72,128]{3,2,1,0:T(8,128)S(1)}, f32[2,2,72,128]{3,2,1,0:T(8,128)S(1)}, u32[]{:S(2)}, u32[]{:S(2)}) %collective-permute-start.5) | collective-permute-done | bytes 147488 | tf_op jit(solution)/shard_map/ppermute | solution.py:216
  18.9 2.7 %collective-permute-start.6 = (f32[1,2,72,128]{3,2,1,0:T(8,128)S(1)}, f32[1,2,72,128]{3,2,1,0:T(8,128)S(1)}, u32[]{:S(2)}, u32[]{:S(2)}) collective-permute-start(f32[1,2,72,128]{3,2,1,0:T(8,128)S(1)} %get-tuple-element.68), channel_id=1, source_target_pairs={{0,16},{4,20},{8,24},{12,28},{16,0},{20,4},{24,8},{28,12},{1,17},{... | collective-permute-start | bytes 221192 | tf_op jit(solution)/shard_map/ppermute | solution.py:216
  21.6 0.0 collective-permute-done.one_ref
  21.6 0.0 collective-permute-done.1.two_ref
  21.6 0.0 copy-done
  21.6 0.0 copy-done.1
  21.6 3.8 %shard_map.131 = (f32[2,16,4096]{2,1,0:T(8,128)S(1)}, f32[2,16,4096]{2,1,0:T(8,128)S(1)}, f32[2,16,4096]{2,1,0:T(8,128)S(1)}, f32[2,80,3840]{2,1,0:T(8,128)S(1)}) custom-call(f32[2,64,4096]{2,1,0:T(8,128)S(1)} %bitcast.25, f32[2,64,4096]{2,1,0:T(8,128)S(1)} %bitcast.19, f32[2,8,3584]{2,1,0:T(8,128)S(1)} %collective-permute-done.one_ref, ...), custom_call_target="tpu_custom_call" | custom-call | flops 1887436800 | tf_op jit(solution)/shard_map/pallas_call | solution.py:24
  25.4 0.1 collective-permute-done.6
  25.5 3.0 %shard_map.133 = (f32[2,80,256]{2,1,0:T(8,128)}, f32[2,80,1536]{2,1,0:T(8,128)S(1)}, f32[2,80,512]{2,1,0:T(8,128)S(1)}, f32[2,64,256]{2,1,0:T(8,128)S(1)}, f32[2,64,128]{2,1,0:T(8,128)S(1)}) custom-call(f32[2,64,4096]{2,1,0:T(8,128)S(1)} %bitcast.26, f32[2,16,4096]{2,1,0:T(8,128)S(1)} %get-tuple-element.62.f0e_ref, ...), custom_call_target="tpu_custom_call" | custom-call | flops 1258291200 | tf_op jit(solution)/shard_map/pallas_call | solution.py:24
  28.5 1.5 %collective-permute-start.7 = (f32[2,64,128]{2,1,0:T(8,128)S(1)}, f32[2,64,128]{2,1,0:T(8,128)S(1)}, u32[]{:S(2)}, u32[]{:S(2)}) collective-permute-start(f32[2,64,128]{2,1,0:T(8,128)S(1)} %get-tuple-element.73.refs_0_), channel_id=1, source_target_pairs={{0,8},{4,12},{8,16},{12,20},{16,24},{20,28},{24,0},{28,4},{1,9},{5... | collective-permute-start | bytes 196616 | tf_op jit(solution)/shard_map/ppermute | solution.py:188
  30.0 2.4 %collective-permute-start.8 = (f32[2,64,128]{2,1,0:T(8,128)S(1)}, f32[2,64,128]{2,1,0:T(8,128)S(1)}, u32[]{:S(2)}, u32[]{:S(2)}) collective-permute-start(f32[2,64,128]{2,1,0:T(8,128)S(1)} %get-tuple-element.73.refs_0_), channel_id=1, source_target_pairs={{0,16},{4,20},{8,24},{12,28},{16,0},{20,4},{24,8},{28,12},{1,17},{... | collective-permute-start | bytes 196616 | tf_op jit(solution)/shard_map/ppermute | solution.py:188
  32.3 0.5 %collective-permute-start.9 = (f32[2,64,128]{2,1,0:T(8,128)S(1)}, f32[2,64,128]{2,1,0:T(8,128)S(1)}, u32[]{:S(2)}, u32[]{:S(2)}) collective-permute-start(f32[2,64,128]{2,1,0:T(8,128)S(1)} %get-tuple-element.73.refs_0_), channel_id=1, source_target_pairs={{0,24},{4,28},{8,0},{12,4},{16,8},{20,12},{24,16},{28,20},{1,25},{... | collective-permute-start | bytes 196616 | tf_op jit(solution)/shard_map/ppermute | solution.py:188
  32.9 4.5 %shard_map.134 = (f32[2,64,4096]{2,1,0:T(8,128)}, f32[2,80,2048]{2,1,0:T(8,128)S(1)}, f32[2,64,2560]{2,1,0:T(8,128)S(1)}) custom-call(f32[2,80,3840]{2,1,0:T(8,128)S(1)} %get-tuple-element.61.f1_ref, f32[2,80,1536]{2,1,0:T(8,128)S(1)} %get-tuple-element.69.f2s_ref, f32[2,64,4096]{2,1,0:T(8,128)S(1)} %get-tuple-element.50.src_ref, ...), custom_call_target="tpu_custom_call" | custom-call | flops 2264924160 | tf_op jit(solution)/shard_map/pallas_call | solution.py:24
  37.4 0.0 collective-permute-done.7.refs_1_
  37.4 0.0 collective-permute-done.8.refs_2_
  37.4 0.0 collective-permute-done.9.refs_3_
  37.4 0.1 shard_map.135
  37.5 0.1 collective-permute-start.10
  37.5 1.6 %shard_map.136 = (f32[2,64,4096]{2,1,0:T(8,128)}, f32[2,64,768]{2,1,0:T(8,128)S(1)}) custom-call(f32[2,64,4096]{2,1,0:T(8,128)} %get-tuple-element.70._, f32[2,80,1536]{2,1,0:T(8,128)S(1)} %get-tuple-element.69.f2s_ref, f32[2,80,2048]{2,1,0:T(8,128)S(1)} %get-tuple-element.71.f2_ref, ...), custom_call_target="tpu_custom_call", output_to_operand_aliasing={{0}: (0, {})} | custom-call | flops 377487360 | tf_op jit(solution)/shard_map/pallas_call | solution.py:24
  39.1 0.0 collective-permute-done.10.theirs_ref
  39.1 1.4 %shard_map.137 = (f32[2,64,4096]{2,1,0:T(8,128)}, f32[2,64,128]{2,1,0:T(8,128)}) custom-call(f32[2,64,4096]{2,1,0:T(8,128)} %get-tuple-element.75._, f32[2,80,2048]{2,1,0:T(8,128)S(1)} %get-tuple-element.71.f2_ref, f32[2,80,512]{2,1,0:T(8,128)S(1)} %get-tuple-element.76.f2e_ref, ...), custom_call_target="tpu_custom_call", output_to_operand_aliasing={{0}: (0, {})} | custom-call | flops 251658240 | tf_op jit(solution)/shard_map/pallas_call | solution.py:24
  (5 shorter events, 0.0 us)
Async XLA Ops:
  0.6 8.9 %slice-start = ((s8[16777216]{0:T(1024)(128)(4,1)}), s8[4194304]{0:T(1024)(128)(4,1)S(1)}, s32[]{:S(2)}) async-start(s8[16777216]{0:T(1024)(128)(4,1)} %bitcast.13), calls=%async_computation | async-start | bytes 8388608
  3.4 6.1 %slice-start.1 = ((s8[16777216]{0:T(1024)(128)(4,1)}), s8[4194304]{0:T(1024)(128)(4,1)S(1)}, s32[]{:S(2)}) async-start(s8[16777216]{0:T(1024)(128)(4,1)} %bitcast.13), calls=%async_computation.1 | async-start | bytes 8388608
  3.5 6.1 %slice-start.2 = ((s8[16777216]{0:T(1024)(128)(4,1)}), s8[4194304]{0:T(1024)(128)(4,1)S(1)}, s32[]{:S(2)}) async-start(s8[16777216]{0:T(1024)(128)(4,1)} %bitcast.13), calls=%async_computation.2 | async-start | bytes 8388608
  3.5 6.1 %slice-start.3 = ((s8[16777216]{0:T(1024)(128)(4,1)}), s8[4194304]{0:T(1024)(128)(4,1)S(1)}, s32[]{:S(2)}) async-start(s8[16777216]{0:T(1024)(128)(4,1)} %bitcast.13), calls=%async_computation.3 | async-start | bytes 8388608
  3.5 7.2 %collective-permute-start.2 = (f32[2,8,128]{2,1,0:T(8,128)S(1)}, f32[2,8,128]{2,1,0:T(8,128)S(1)}, u32[]{:S(2)}, u32[]{:S(2)}) collective-permute-start(f32[2,8,128]{2,1,0:T(8,128)S(1)} %get-tuple-element.46), channel_id=1, source_target_pairs={{0,1},{1,0},{2,3},{3,2},{4,5},{5,4},{6,7},{7,6},{8,9},{9,8},{10,11... | collective-permute-start | bytes 24584 | tf_op jit(solution)/shard_map/ppermute | solution.py:183
  6.5 4.7 %collective-permute-start.3 = (f32[2,8,128]{2,1,0:T(8,128)S(1)}, f32[2,8,128]{2,1,0:T(8,128)S(1)}, u32[]{:S(2)}, u32[]{:S(2)}) collective-permute-start(f32[2,8,128]{2,1,0:T(8,128)S(1)} %get-tuple-element.47), channel_id=1, source_target_pairs={{0,3},{1,2},{2,1},{3,0},{4,7},{5,6},{6,5},{7,4},{8,11},{9,10},{10,... | collective-permute-start | bytes 24584 | tf_op jit(solution)/shard_map/ppermute | solution.py:183
  8.0 13.6 %collective-permute-start = (f32[2,8,3584]{2,1,0:T(8,128)S(1)}, f32[2,8,3584]{2,1,0:T(8,128)S(1)}, u32[]{:S(2)}, u32[]{:S(2)}) collective-permute-start(f32[2,8,3584]{2,1,0:T(8,128)S(1)} %get-tuple-element.42), channel_id=1, source_target_pairs={{0,1},{1,0},{2,3},{3,2},{4,5},{5,4},{6,7},{7,6},{8,9},{9,8},{10,11... | collective-permute-start | bytes 688136 | tf_op jit(solution)/shard_map/ppermute | solution.py:183
  9.5 12.1 %collective-permute-start.1 = (f32[2,8,3584]{2,1,0:T(8,128)S(1)}, f32[2,8,3584]{2,1,0:T(8,128)S(1)}, u32[]{:S(2)}, u32[]{:S(2)}) collective-permute-start(f32[2,8,3584]{2,1,0:T(8,128)S(1)} %get-tuple-element.43), channel_id=1, source_target_pairs={{0,3},{1,2},{2,1},{3,0},{4,7},{5,6},{6,5},{7,4},{8,11},{9,10},{10,... | collective-permute-start | bytes 688136 | tf_op jit(solution)/shard_map/ppermute | solution.py:183
  9.5 1.6 %copy-start.3 = (f32[1,2,64,128]{3,2,1,0:T(8,128)S(1)}, f32[1,2,64,128]{3,2,1,0:T(8,128)}, u32[]{:S(2)}) copy-start(f32[1,2,64,128]{3,2,1,0:T(8,128)} %param.15) | copy-start | bytes 196612
  11.2 3.1 %copy-start.2 = (f32[1,2,64,4096]{3,2,1,0:T(8,128)S(1)}, f32[1,2,64,4096]{3,2,1,0:T(8,128)}, u32[]{:S(2)}) copy-start(f32[1,2,64,4096]{3,2,1,0:T(8,128)} %param.11) | copy-start | bytes 6291460
  11.2 3.1 %copy-start.4 = (f32[1,2,16]{2,1,0:T(2,128)S(1)}, f32[1,2,16]{2,1,0:T(2,128)}, u32[]{:S(2)}) copy-start(f32[1,2,16]{2,1,0:T(2,128)} %pcur_ref.1) | copy-start | bytes 388
  11.2 3.1 %copy-start.5 = (s32[1,16]{1,0:T(1,128)S(1)}, s32[1,16]{1,0:T(1,128)}, u32[]{:S(2)}) copy-start(s32[1,16]{1,0:T(1,128)} %prow_ref.1) | copy-start | bytes 196
  11.2 3.1 %copy-start.6 = (s32[1,16]{1,0:T(1,128)S(1)}, s32[1,16]{1,0:T(1,128)}, u32[]{:S(2)}) copy-start(s32[1,16]{1,0:T(1,128)} %pcol_ref.1) | copy-start | bytes 196
  11.3 1.3 %collective-permute-start.4 = (f32[2,72,128]{2,1,0:T(8,128)S(1)}, f32[2,72,128]{2,1,0:T(8,128)S(1)}, u32[]{:S(2)}, u32[]{:S(2)}) collective-permute-start(f32[2,72,128]{2,1,0:T(8,128)S(1)} %shard_map.126.mult_ref.own_ref), channel_id=1, source_target_pairs={{0,4},{4,0},{8,12},{12,8},{16,20},{20,16},{24,28},{28,24},{1,5},{5... | collective-permute-start | bytes 221192 | tf_op jit(solution)/shard_map/ppermute | solution.py:192
  12.6 6.2 %collective-permute-start.5 = (f32[2,2,72,128]{3,2,1,0:T(8,128)S(1)}, f32[2,2,72,128]{3,2,1,0:T(8,128)S(1)}, u32[]{:S(2)}, u32[]{:S(2)}) collective-permute-start(f32[2,2,72,128]{3,2,1,0:T(8,128)S(1)} %get-tuple-element.65), channel_id=1, source_target_pairs={{0,8},{4,12},{8,0},{12,4},{16,24},{20,28},{24,16},{28,20},{1,9},{5... | collective-permute-start | bytes 442376 | tf_op jit(solution)/shard_map/ppermute | solution.py:216
  15.5 6.1 %copy-start = (f32[1,2,64,4096]{3,2,1,0:T(8,128)S(1)}, f32[1,2,64,4096]{3,2,1,0:T(8,128)}, u32[]{:S(2)}) copy-start(f32[1,2,64,4096]{3,2,1,0:T(8,128)} %param.12) | copy-start | bytes 6291460
  15.5 6.1 %copy-start.1 = (f32[1,2,64,4096]{3,2,1,0:T(8,128)S(1)}, f32[1,2,64,4096]{3,2,1,0:T(8,128)}, u32[]{:S(2)}) copy-start(f32[1,2,64,4096]{3,2,1,0:T(8,128)} %param.13) | copy-start | bytes 6291460
  18.9 6.6 %collective-permute-start.6 = (f32[1,2,72,128]{3,2,1,0:T(8,128)S(1)}, f32[1,2,72,128]{3,2,1,0:T(8,128)S(1)}, u32[]{:S(2)}, u32[]{:S(2)}) collective-permute-start(f32[1,2,72,128]{3,2,1,0:T(8,128)S(1)} %get-tuple-element.68), channel_id=1, source_target_pairs={{0,16},{4,20},{8,24},{12,28},{16,0},{20,4},{24,8},{28,12},{1,17},{... | collective-permute-start | bytes 221192 | tf_op jit(solution)/shard_map/ppermute | solution.py:216
  28.5 8.9 %collective-permute-start.7 = (f32[2,64,128]{2,1,0:T(8,128)S(1)}, f32[2,64,128]{2,1,0:T(8,128)S(1)}, u32[]{:S(2)}, u32[]{:S(2)}) collective-permute-start(f32[2,64,128]{2,1,0:T(8,128)S(1)} %get-tuple-element.73.refs_0_), channel_id=1, source_target_pairs={{0,8},{4,12},{8,16},{12,20},{16,24},{20,28},{24,0},{28,4},{1,9},{5... | collective-permute-start | bytes 196616 | tf_op jit(solution)/shard_map/ppermute | solution.py:188
  30.0 7.4 %collective-permute-start.8 = (f32[2,64,128]{2,1,0:T(8,128)S(1)}, f32[2,64,128]{2,1,0:T(8,128)S(1)}, u32[]{:S(2)}, u32[]{:S(2)}) collective-permute-start(f32[2,64,128]{2,1,0:T(8,128)S(1)} %get-tuple-element.73.refs_0_), channel_id=1, source_target_pairs={{0,16},{4,20},{8,24},{12,28},{16,0},{20,4},{24,8},{28,12},{1,17},{... | collective-permute-start | bytes 196616 | tf_op jit(solution)/shard_map/ppermute | solution.py:188
  32.3 5.0 %collective-permute-start.9 = (f32[2,64,128]{2,1,0:T(8,128)S(1)}, f32[2,64,128]{2,1,0:T(8,128)S(1)}, u32[]{:S(2)}, u32[]{:S(2)}) collective-permute-start(f32[2,64,128]{2,1,0:T(8,128)S(1)} %get-tuple-element.73.refs_0_), channel_id=1, source_target_pairs={{0,24},{4,28},{8,0},{12,4},{16,8},{20,12},{24,16},{28,20},{1,25},{... | collective-permute-start | bytes 196616 | tf_op jit(solution)/shard_map/ppermute | solution.py:188
  37.5 1.7 %collective-permute-start.10 = (f32[2,64,128]{2,1,0:T(8,128)S(1)}, f32[2,64,128]{2,1,0:T(8,128)S(1)}, u32[]{:S(2)}, u32[]{:S(2)}) collective-permute-start(f32[2,64,128]{2,1,0:T(8,128)S(1)} %get-tuple-element.79), channel_id=1, source_target_pairs={{0,4},{4,0},{8,12},{12,8},{16,20},{20,16},{24,28},{28,24},{1,5},{5... | collective-permute-start | bytes 196616 | tf_op jit(solution)/shard_map/ppermute | solution.py:192

commit v6 on v5

--- a/solution.py
+++ b/solution.py
@@ -391,7 +391,7 @@
 def far_kernel(
     count, start_ref, f0e_ref, f1_ref, src_ref, srce_ref, diag_ref, dge_ref, mask_ref, *refs
 ):
-    pieces, w_refs, (f1e_ref, f2s_ref, f2e_ref, f3e_ref, far_ref) = refs[:count], refs[count:-5], refs[-5:]
+    pieces, w_refs, (f2s_ref, f2e_ref, f3e_ref, far_ref, f1e_ref) = refs[:count], refs[count:-5], refs[-5:]
     w = Weights(w_refs)
     size, last = w.size, w.last
     rows = far_ref.shape[1]
@@ -458,23 +458,17 @@
     )
 
 
-def third_kernel(early, _, f2s_ref, f2_ref, f3_ref, src_ref, srce_ref, diag_ref, dge_ref, mask_ref, _after, *refs):
-    w_refs, (out_ref, more_ref, sem) = refs[:-3], refs[-3:]
+def third_kernel(first, f2s_ref, f2_ref, f2e_ref, src_ref, srce_ref, diag_ref, dge_ref, mask_ref, _, *refs):
+    w_refs, f3_ref = refs[:-1], refs[-1]
     w = Weights(w_refs)
     size = w.size
-    first = f3_ref.shape[2] // size
     source, diag = (src_ref, srce_ref), (diag_ref, dge_ref)
-    copies = [block_copy(f3_ref, k, out_ref, k, size, sem.at[k]) for k in range(early, first)]
-    for copy in copies:
-        copy.start()
-    f2 = reader([(f2s_ref.shape[2] // size, f2_ref), (0, f2s_ref)], size)
-    sweep(w, f2, source, diag, mask_ref, first, more_ref.shape[2] // size, more_ref)
-    for copy in copies:
-        copy.wait()
+    f2 = reader([(w.last - 1, f2e_ref), (f2s_ref.shape[2] // size, f2_ref), (0, f2s_ref)], size)
+    sweep(w, f2, source, diag, mask_ref, first, f3_ref.shape[2] // size, f3_ref)
 
 
 def last_kernel(
-    f2_first, _, f2_ref, f2e_ref, near_ref, f3_ref, f3e_ref, src_ref, srce_ref, diag_ref, dge_ref, mask_ref,
+    f2_first, early, _, f2_ref, f2e_ref, f3_ref, more_ref, f3e_ref, src_ref, srce_ref, diag_ref, dge_ref, mask_ref,
     mult_ref, mine_ref, theirs_ref, *refs,
 ):
     w_refs, (out_ref, next_ref, held_ref, new_ref, sem) = refs[:-5], refs[-5:]
@@ -483,18 +477,19 @@
     count = held_ref.shape[0]
     first = last - count
     source, diag = (src_ref, srce_ref), (diag_ref, dge_ref)
-    more = f3_ref.shape[2] // size
-    copies = [block_copy(f3_ref, k, out_ref, first - more + k, size, sem.at[k]) for k in range(more)]
-    copies.append(block_copy(f3e_ref, 0, out_ref, last, size, sem.at[more]))
+    done = f3_ref.shape[2] // size
+    copies = [block_copy(f3_ref, k, out_ref, k, size, sem.at[k]) for k in range(early, done)]
+    copies += [block_copy(more_ref, k - done, out_ref, k, size, sem.at[k]) for k in range(done, first)]
+    copies.append(block_copy(f3e_ref, 0, out_ref, last, size, sem.at[last]))
     for copy in copies:
         copy.start()
-    new_ref[...] = mult_ref[...] + (near_ref[:, :, :IB] - (mine_ref[...] + theirs_ref[...]))
-    copies.append(pltpu.make_async_copy(new_ref, next_ref, sem.at[more + 1]))
+    new_ref[...] = mult_ref[...] + (f3_ref[:, :, :IB] - (mine_ref[...] + theirs_ref[...]))
+    copies.append(pltpu.make_async_copy(new_ref, next_ref, sem.at[last + 1]))
     copies[-1].start()
     f2 = reader([(last - 1, f2e_ref), (f2_first, f2_ref)], size)
     for i in range(count):
         sweep(w, f2, source, diag, mask_ref, first + i, 1, held_ref.at[i])
-        copies.append(block_copy(held_ref.at[i], 0, out_ref, first + i, size, sem.at[more + 2 + i]))
+        copies.append(block_copy(held_ref.at[i], 0, out_ref, first + i, size, sem.at[first + i]))
         copies[-1].start()
     for copy in copies:
         copy.wait()
@@ -589,20 +584,20 @@
     )
     known = (src, srce, diag, dge, mask)
     fill = nb * 3 // 8
-    f1e, f2s, f2e, f3e, far = run(
+    f2s, f2e, f3e, far = run(
         functools.partial(far_kernel, len(incoming)),
         (start, f0e, f1, *known, *incoming),
         [
-            held((2, high, size)),
             held((2, high, fill * size)),
             held((2, high, 2 * size)),
             held((2, rows, size)),
             held((2, rows, IB)),
         ],
         4 + fill,
+        scratch=[held((2, high, size))],
     )
     ends = [to_chip(far, step) if step else far for step in range(chips)]
-    done, tail = nb * 5 // 8, nb // 8
+    done, tail = nb * 9 // 16, nb // 16
     whole = jax.ShapeDtypeStruct((2, rows, width), jnp.float32)
     partly, f2, f3a = run(
         middle_kernel,
@@ -617,24 +612,21 @@
     )
     theirs = swap_cores(theirs)
     more = nb - 1 - tail - done
-    partly, f3b = run(
-        functools.partial(third_kernel, fill - 1),
-        (partly, f2s, f2, f3a, *known, mine),
-        [whole, held((2, rows, more * size))],
+    f3b = run(
+        functools.partial(third_kernel, done),
+        (f2s, f2, f2e, *known, mine),
+        held((2, rows, more * size)),
         more,
-        scratch=[pltpu.SemaphoreType.DMA((done,))],
-        out_specs=[ANY_SPEC, VMEM_SPEC],
-        aliased=True,
     )
     solved, updated = run(
-        functools.partial(last_kernel, fill),
+        functools.partial(last_kernel, fill, fill - 1),
         (partly, f2, f2e, f3a, f3b, f3e, *known, mult, mine, theirs),
         [whole, jax.ShapeDtypeStruct(mult.shape, jnp.float32)],
         tail,
         scratch=[
             pltpu.VMEM((tail, 2, rows, size), jnp.float32),
             pltpu.VMEM(mult.shape, jnp.float32),
-            pltpu.SemaphoreType.DMA((2 + more + tail,)),
+            pltpu.SemaphoreType.DMA((nb + 1,)),
         ],
         out_specs=[ANY_SPEC] * 2,
         aliased=True,

time: 40.9 us -> 40 us (0.978)
  Pallas kernels: 22.9 us -> 21.9 us
    pallas_call x16, Pallas kernels: 22.9 us -> 21.9 us  [call(): pl.pallas_call(kernel, out_shape=outs, in_specs=specs, out_specs=out_spec...]
where the time goes in v6:
time: 40 us; the launch traced here: 39.8 us
  Pallas kernels  21.9 us (55%)
  starting transfers between devices  14.9 us (37%)
  waiting for transfers between devices  1.85 us (5%)
  between operations  1.08 us (3%)
    pallas_call x16, Pallas kernels, call(): pl.pallas_call(kernel, out_shape=outs, in_specs=specs, out_specs=out_spec...  21.9 us
    ppermute x4, starting transfers between devices, swap_edges(): return (lax.ppermute(one, 'tile', first), lax.ppermute(two, 'tile', second))  6.01 us
    ppermute x3, starting transfers between devices, to_chip(): lax.ppermute(cells, 'sub', [(i, (i + 2 * step) % count) for i in range(co...  4.41 us
    ppermute x2, starting transfers between devices, over_bit(): lax.ppermute(cells, 'sub', [(i, i ^ 2 * bit) for i in range(lax.axis_size...  4.32 us
    ppermute x2, waiting for transfers between devices, over_bit(): lax.ppermute(cells, 'sub', [(i, i ^ 2 * bit) for i in range(lax.axis_size...  1.26 us
  transfers between devices with their start and end apart: 11, of which 4 were waited for; matrix products, arithmetic and copies ran while one was open for 0% of the time, Pallas kernels for 38%

profile of v6, /device:TPU:0, one launch (start us, length us, event | category | flops | bytes accessed | tf_op | source)
XLA Modules:
  0.0 39.8 jit_solution(288868354891838077)
XLA Ops:
  0.6 0.0 slice-start
  0.6 2.8 %shard_map.122 = (f32[2,8,128]{2,1,0:T(8,128)S(1)}, f32[2,8,128]{2,1,0:T(8,128)S(1)}, f32[2,8,3584]{2,1,0:T(8,128)S(1)}, f32[2,8,3584]{2,1,0:T(8,128)S(1)}, s32[...) custom-call(f32[2,64,4096]{2,1,0:T(8,128)} %bitcast.24, f32[2,64,4096]{2,1,0:T(8,128)} %bitcast.27, f32[2,64,4096]{2,1,0:T(8,128)} %bitcast.18, ...), custom_call_target="tpu_custom_call" | custom-call | tf_op jit(solution)/shard_map/pallas_call | solution.py:24
  3.4 0.0 slice-start.1
  3.5 0.0 slice-start.2
  3.5 0.0 slice-start.3
  3.5 3.0 %collective-permute-start.2 = (f32[2,8,128]{2,1,0:T(8,128)S(1)}, f32[2,8,128]{2,1,0:T(8,128)S(1)}, u32[]{:S(2)}, u32[]{:S(2)}) collective-permute-start(f32[2,8,128]{2,1,0:T(8,128)S(1)} %get-tuple-element.44), channel_id=1, source_target_pairs={{0,1},{1,0},{2,3},{3,2},{4,5},{5,4},{6,7},{7,6},{8,9},{9,8},{10,11... | collective-permute-start | bytes 24584 | tf_op jit(solution)/shard_map/ppermute | solution.py:183
  6.5 1.5 %collective-permute-start.3 = (f32[2,8,128]{2,1,0:T(8,128)S(1)}, f32[2,8,128]{2,1,0:T(8,128)S(1)}, u32[]{:S(2)}, u32[]{:S(2)}) collective-permute-start(f32[2,8,128]{2,1,0:T(8,128)S(1)} %get-tuple-element.45), channel_id=1, source_target_pairs={{0,3},{1,2},{2,1},{3,0},{4,7},{5,6},{6,5},{7,4},{8,11},{9,10},{10,... | collective-permute-start | bytes 24584 | tf_op jit(solution)/shard_map/ppermute | solution.py:183
  8.0 1.5 %collective-permute-start = (f32[2,8,3584]{2,1,0:T(8,128)S(1)}, f32[2,8,3584]{2,1,0:T(8,128)S(1)}, u32[]{:S(2)}, u32[]{:S(2)}) collective-permute-start(f32[2,8,3584]{2,1,0:T(8,128)S(1)} %get-tuple-element.40), channel_id=1, source_target_pairs={{0,1},{1,0},{2,3},{3,2},{4,5},{5,4},{6,7},{7,6},{8,9},{9,8},{10,11... | collective-permute-start | bytes 688136 | tf_op jit(solution)/shard_map/ppermute | solution.py:183
  9.5 0.0 collective-permute-start.1
  9.5 0.0 slice-done
  9.5 0.0 slice-done.1
  9.5 0.0 slice-done.2
  9.5 0.0 slice-done.3
  9.5 0.0 copy-start.3
  9.6 1.1 %shard_map.125 = (bf16[4,512,512]{2,1,0:T(8,128)(2,1)S(1)}, bf16[4,512,512]{2,1,0:T(8,128)(2,1)S(1)}, f32[8,128]{1,0:T(8,128)S(1)}) custom-call(f32[16,2048,128]{2,1,0:T(8,128)S(1)} %bitcast.15, f32[80,128]{1,0:T(8,128)S(1)} %shard_map.124._.mask_ref), custom_call_target="tpu_custom_call" | custom-call | bytes 8388608 | tf_op jit(solution)/shard_map/pallas_call | solution.py:24
  10.7 0.0 collective-permute-done.2.one_ref
  10.7 0.5 %collective-permute-done.3.two_ref = f32[2,8,128]{2,1,0:T(8,128)S(1)} collective-permute-done((f32[2,8,128]{2,1,0:T(8,128)S(1)}, f32[2,8,128]{2,1,0:T(8,128)S(1)}, u32[]{:S(2)}, u32[]{:S(2)}) %collective-permute-start.3) | collective-permute-done | bytes 8224 | tf_op jit(solution)/shard_map/ppermute | solution.py:183
  11.2 0.0 copy-done.3
  11.2 0.0 copy-start.2
  11.2 0.0 copy-start.4
  11.2 0.0 copy-start.5
  11.2 0.0 copy-start.6
  11.3 0.1 collective-permute-start.4
  11.3 1.1 %shard_map.128 = (bf16[4,512,512]{2,1,0:T(8,128)(2,1)S(1)}, bf16[4,512,512]{2,1,0:T(8,128)(2,1)S(1)}, f32[8,128]{1,0:T(8,128)S(1)}) custom-call(f32[16,2048,128]{2,1,0:T(8,128)S(1)} %bitcast.16, f32[8,128]{1,0:T(8,128)S(1)} %get-tuple-element.47._), custom_call_target="tpu_custom_call" | custom-call | bytes 8388608 | tf_op jit(solution)/shard_map/pallas_call | solution.py:24
  12.5 0.1 collective-permute-done.4.other_ref
  12.6 0.1 shard_map.129
  12.6 1.7 %collective-permute-start.5 = (f32[2,2,72,128]{3,2,1,0:T(8,128)S(1)}, f32[2,2,72,128]{3,2,1,0:T(8,128)S(1)}, u32[]{:S(2)}, u32[]{:S(2)}) collective-permute-start(f32[2,2,72,128]{3,2,1,0:T(8,128)S(1)} %get-tuple-element.63), channel_id=1, source_target_pairs={{0,8},{4,12},{8,0},{12,4},{16,24},{20,28},{24,16},{28,20},{1,9},{5... | collective-permute-start | bytes 442376 | tf_op jit(solution)/shard_map/ppermute | solution.py:216
  14.3 0.0 copy-done.2
  14.3 0.0 copy-done.4
  14.3 0.0 copy-done.5
  14.3 0.0 copy-done.6
  14.3 1.2 %shard_map.127 = (f32[2,64,4096]{2,1,0:T(8,128)S(1)}, f32[2,16,4096]{2,1,0:T(8,128)S(1)}) custom-call(f32[2,64,4096]{2,1,0:T(8,128)S(1)} %bitcast.28, f32[2,72,128]{2,1,0:T(8,128)S(1)} %shard_map.126.mult_ref.own_ref, s32[1,16]{1,0:T(1,128)S(1)} %copy-done.5, s32[1,16]{1,0:T(1,128)S(1)} %copy-done.6, f32[1,2,16]{2,1,0:T(2,128)S(1)} %copy-done.4), custom_call_target="tpu_custom_call" | custom-call | bytes 8388608 | tf_op jit(solution)/shard_map/pallas_call | solution.py:24
  15.5 0.0 copy-start
  15.5 0.0 copy-start.1
  15.5 2.2 %shard_map.130 = (bf16[8,512,512]{2,1,0:T(8,128)(2,1)S(1)}, bf16[8,512,512]{2,1,0:T(8,128)(2,1)S(1)}, f32[8,128]{1,0:T(8,128)S(1)}) custom-call(f32[16,2048,128]{2,1,0:T(8,128)S(1)} %bitcast.17, f32[2,2,72,128]{3,2,1,0:T(8,128)S(1)} %get-tuple-element.56._.keep_ref), custom_call_target="tpu_custom_call" | custom-call | bytes 16777216 | tf_op jit(solution)/shard_map/pallas_call | solution.py:24
  17.8 1.1 %collective-permute-done.5.got_ref = f32[2,2,72,128]{3,2,1,0:T(8,128)S(1)} collective-permute-done((f32[2,2,72,128]{3,2,1,0:T(8,128)S(1)}, f32[2,2,72,128]{3,2,1,0:T(8,128)S(1)}, u32[]{:S(2)}, u32[]{:S(2)}) %collective-permute-start.5) | collective-permute-done | bytes 147488 | tf_op jit(solution)/shard_map/ppermute | solution.py:216
  18.9 2.7 %collective-permute-start.6 = (f32[1,2,72,128]{3,2,1,0:T(8,128)S(1)}, f32[1,2,72,128]{3,2,1,0:T(8,128)S(1)}, u32[]{:S(2)}, u32[]{:S(2)}) collective-permute-start(f32[1,2,72,128]{3,2,1,0:T(8,128)S(1)} %get-tuple-element.66), channel_id=1, source_target_pairs={{0,16},{4,20},{8,24},{12,28},{16,0},{20,4},{24,8},{28,12},{1,17},{... | collective-permute-start | bytes 221192 | tf_op jit(solution)/shard_map/ppermute | solution.py:216
  21.6 0.0 collective-permute-done.one_ref
  21.6 0.0 collective-permute-done.1.two_ref
  21.6 0.0 copy-done
  21.6 0.0 copy-done.1
  21.6 3.8 %shard_map.131 = (f32[2,16,4096]{2,1,0:T(8,128)S(1)}, f32[2,16,4096]{2,1,0:T(8,128)S(1)}, f32[2,16,4096]{2,1,0:T(8,128)S(1)}, f32[2,80,3840]{2,1,0:T(8,128)S(1)}) custom-call(f32[2,64,4096]{2,1,0:T(8,128)S(1)} %bitcast.25, f32[2,64,4096]{2,1,0:T(8,128)S(1)} %bitcast.19, f32[2,8,3584]{2,1,0:T(8,128)S(1)} %collective-permute-done.one_ref, ...), custom_call_target="tpu_custom_call" | custom-call | flops 1887436800 | tf_op jit(solution)/shard_map/pallas_call | solution.py:24
  25.4 0.1 collective-permute-done.6
  25.5 2.5 %shard_map.133 = (f32[2,80,1536]{2,1,0:T(8,128)S(1)}, f32[2,80,512]{2,1,0:T(8,128)S(1)}, f32[2,64,256]{2,1,0:T(8,128)S(1)}, f32[2,64,128]{2,1,0:T(8,128)S(1)}) custom-call(f32[2,64,4096]{2,1,0:T(8,128)S(1)} %bitcast.26, f32[2,16,4096]{2,1,0:T(8,128)S(1)} %get-tuple-element.60.f0e_ref, f32[2,80,3840]{2,1,0:T(8,128)S(1)} %get-tuple-element.59.f1_ref, ...), custom_call_target="tpu_custom_call" | custom-call | flops 1258291200 | tf_op jit(solution)/shard_map/pallas_call | solution.py:24
  28.0 1.5 %collective-permute-start.7 = (f32[2,64,128]{2,1,0:T(8,128)S(1)}, f32[2,64,128]{2,1,0:T(8,128)S(1)}, u32[]{:S(2)}, u32[]{:S(2)}) collective-permute-start(f32[2,64,128]{2,1,0:T(8,128)S(1)} %get-tuple-element.72.refs_0_), channel_id=1, source_target_pairs={{0,8},{4,12},{8,16},{12,20},{16,24},{20,28},{24,0},{28,4},{1,9},{5... | collective-permute-start | bytes 196616 | tf_op jit(solution)/shard_map/ppermute | solution.py:188
  29.5 2.4 %collective-permute-start.8 = (f32[2,64,128]{2,1,0:T(8,128)S(1)}, f32[2,64,128]{2,1,0:T(8,128)S(1)}, u32[]{:S(2)}, u32[]{:S(2)}) collective-permute-start(f32[2,64,128]{2,1,0:T(8,128)S(1)} %get-tuple-element.72.refs_0_), channel_id=1, source_target_pairs={{0,16},{4,20},{8,24},{12,28},{16,0},{20,4},{24,8},{28,12},{1,17},{... | collective-permute-start | bytes 196616 | tf_op jit(solution)/shard_map/ppermute | solution.py:188
  31.9 0.5 %collective-permute-start.9 = (f32[2,64,128]{2,1,0:T(8,128)S(1)}, f32[2,64,128]{2,1,0:T(8,128)S(1)}, u32[]{:S(2)}, u32[]{:S(2)}) collective-permute-start(f32[2,64,128]{2,1,0:T(8,128)S(1)} %get-tuple-element.72.refs_0_), channel_id=1, source_target_pairs={{0,24},{4,28},{8,0},{12,4},{16,8},{20,12},{24,16},{28,20},{1,25},{... | collective-permute-start | bytes 196616 | tf_op jit(solution)/shard_map/ppermute | solution.py:188
  32.4 4.3 %shard_map.134 = (f32[2,64,4096]{2,1,0:T(8,128)}, f32[2,80,2048]{2,1,0:T(8,128)S(1)}, f32[2,64,2304]{2,1,0:T(8,128)S(1)}) custom-call(f32[2,80,3840]{2,1,0:T(8,128)S(1)} %get-tuple-element.59.f1_ref, f32[2,80,1536]{2,1,0:T(8,128)S(1)} %get-tuple-element.67.f2s_ref, f32[2,64,4096]{2,1,0:T(8,128)S(1)} %get-tuple-element.48.src_ref, ...), custom_call_target="tpu_custom_call" | custom-call | flops 2139095040 | tf_op jit(solution)/shard_map/pallas_call | solution.py:24
  36.7 0.0 collective-permute-done.7.refs_1_
  36.7 0.0 collective-permute-done.8.refs_2_
  36.7 0.0 collective-permute-done.9.refs_3_
  36.7 0.1 shard_map.135
  36.8 0.1 collective-permute-start.10
  36.9 1.3 %shard_map.136.more_ref = f32[2,64,1280]{2,1,0:T(8,128)S(1)} custom-call(f32[2,80,1536]{2,1,0:T(8,128)S(1)} %get-tuple-element.67.f2s_ref, f32[2,80,2048]{2,1,0:T(8,128)S(1)} %get-tuple-element.69.f2_ref, f32[2,80,512]{2,1,0:T(8,128)S(1)} %get-tuple-element.70.f2e_ref, f32[2,64,4096]{2,1,0:T(8,128)S(1)} %get-tuple-element.48.src_ref, ...), custom_call_target="tpu_custom_call" | custom-call | flops 629145600 | tf_op jit(solution)/shard_map/pallas_call | solution.py:24
  38.2 0.0 collective-permute-done.10.theirs_ref
  38.2 1.4 %shard_map.137 = (f32[2,64,4096]{2,1,0:T(8,128)}, f32[2,64,128]{2,1,0:T(8,128)}) custom-call(f32[2,64,4096]{2,1,0:T(8,128)} %get-tuple-element.68._, f32[2,80,2048]{2,1,0:T(8,128)S(1)} %get-tuple-element.69.f2_ref, f32[2,80,512]{2,1,0:T(8,128)S(1)} %get-tuple-element.70.f2e_ref, ...), custom_call_target="tpu_custom_call", output_to_operand_aliasing={{0}: (0, {})} | custom-call | flops 125829120 | tf_op jit(solution)/shard_map/pallas_call | solution.py:24
  (5 shorter events, 0.0 us)
Async XLA Ops:
  0.6 8.9 %slice-start = ((s8[16777216]{0:T(1024)(128)(4,1)}), s8[4194304]{0:T(1024)(128)(4,1)S(1)}, s32[]{:S(2)}) async-start(s8[16777216]{0:T(1024)(128)(4,1)} %bitcast.13), calls=%async_computation | async-start | bytes 8388608
  3.4 6.1 %slice-start.1 = ((s8[16777216]{0:T(1024)(128)(4,1)}), s8[4194304]{0:T(1024)(128)(4,1)S(1)}, s32[]{:S(2)}) async-start(s8[16777216]{0:T(1024)(128)(4,1)} %bitcast.13), calls=%async_computation.1 | async-start | bytes 8388608
  3.5 6.1 %slice-start.2 = ((s8[16777216]{0:T(1024)(128)(4,1)}), s8[4194304]{0:T(1024)(128)(4,1)S(1)}, s32[]{:S(2)}) async-start(s8[16777216]{0:T(1024)(128)(4,1)} %bitcast.13), calls=%async_computation.2 | async-start | bytes 8388608
  3.5 6.1 %slice-start.3 = ((s8[16777216]{0:T(1024)(128)(4,1)}), s8[4194304]{0:T(1024)(128)(4,1)S(1)}, s32[]{:S(2)}) async-start(s8[16777216]{0:T(1024)(128)(4,1)} %bitcast.13), calls=%async_computation.3 | async-start | bytes 8388608
  3.5 7.2 %collective-permute-start.2 = (f32[2,8,128]{2,1,0:T(8,128)S(1)}, f32[2,8,128]{2,1,0:T(8,128)S(1)}, u32[]{:S(2)}, u32[]{:S(2)}) collective-permute-start(f32[2,8,128]{2,1,0:T(8,128)S(1)} %get-tuple-element.44), channel_id=1, source_target_pairs={{0,1},{1,0},{2,3},{3,2},{4,5},{5,4},{6,7},{7,6},{8,9},{9,8},{10,11... | collective-permute-start | bytes 24584 | tf_op jit(solution)/shard_map/ppermute | solution.py:183
  6.5 4.7 %collective-permute-start.3 = (f32[2,8,128]{2,1,0:T(8,128)S(1)}, f32[2,8,128]{2,1,0:T(8,128)S(1)}, u32[]{:S(2)}, u32[]{:S(2)}) collective-permute-start(f32[2,8,128]{2,1,0:T(8,128)S(1)} %get-tuple-element.45), channel_id=1, source_target_pairs={{0,3},{1,2},{2,1},{3,0},{4,7},{5,6},{6,5},{7,4},{8,11},{9,10},{10,... | collective-permute-start | bytes 24584 | tf_op jit(solution)/shard_map/ppermute | solution.py:183
  8.0 13.6 %collective-permute-start = (f32[2,8,3584]{2,1,0:T(8,128)S(1)}, f32[2,8,3584]{2,1,0:T(8,128)S(1)}, u32[]{:S(2)}, u32[]{:S(2)}) collective-permute-start(f32[2,8,3584]{2,1,0:T(8,128)S(1)} %get-tuple-element.40), channel_id=1, source_target_pairs={{0,1},{1,0},{2,3},{3,2},{4,5},{5,4},{6,7},{7,6},{8,9},{9,8},{10,11... | collective-permute-start | bytes 688136 | tf_op jit(solution)/shard_map/ppermute | solution.py:183
  9.5 12.1 %collective-permute-start.1 = (f32[2,8,3584]{2,1,0:T(8,128)S(1)}, f32[2,8,3584]{2,1,0:T(8,128)S(1)}, u32[]{:S(2)}, u32[]{:S(2)}) collective-permute-start(f32[2,8,3584]{2,1,0:T(8,128)S(1)} %get-tuple-element.41), channel_id=1, source_target_pairs={{0,3},{1,2},{2,1},{3,0},{4,7},{5,6},{6,5},{7,4},{8,11},{9,10},{10,... | collective-permute-start | bytes 688136 | tf_op jit(solution)/shard_map/ppermute | solution.py:183
  9.5 1.6 %copy-start.3 = (f32[1,2,64,128]{3,2,1,0:T(8,128)S(1)}, f32[1,2,64,128]{3,2,1,0:T(8,128)}, u32[]{:S(2)}) copy-start(f32[1,2,64,128]{3,2,1,0:T(8,128)} %param.15) | copy-start | bytes 196612
  11.2 3.1 %copy-start.2 = (f32[1,2,64,4096]{3,2,1,0:T(8,128)S(1)}, f32[1,2,64,4096]{3,2,1,0:T(8,128)}, u32[]{:S(2)}) copy-start(f32[1,2,64,4096]{3,2,1,0:T(8,128)} %param.11) | copy-start | bytes 6291460
  11.2 3.1 %copy-start.4 = (f32[1,2,16]{2,1,0:T(2,128)S(1)}, f32[1,2,16]{2,1,0:T(2,128)}, u32[]{:S(2)}) copy-start(f32[1,2,16]{2,1,0:T(2,128)} %pcur_ref.1) | copy-start | bytes 388
  11.2 3.1 %copy-start.5 = (s32[1,16]{1,0:T(1,128)S(1)}, s32[1,16]{1,0:T(1,128)}, u32[]{:S(2)}) copy-start(s32[1,16]{1,0:T(1,128)} %prow_ref.1) | copy-start | bytes 196
  11.2 3.1 %copy-start.6 = (s32[1,16]{1,0:T(1,128)S(1)}, s32[1,16]{1,0:T(1,128)}, u32[]{:S(2)}) copy-start(s32[1,16]{1,0:T(1,128)} %pcol_ref.1) | copy-start | bytes 196
  11.3 1.3 %collective-permute-start.4 = (f32[2,72,128]{2,1,0:T(8,128)S(1)}, f32[2,72,128]{2,1,0:T(8,128)S(1)}, u32[]{:S(2)}, u32[]{:S(2)}) collective-permute-start(f32[2,72,128]{2,1,0:T(8,128)S(1)} %shard_map.126.mult_ref.own_ref), channel_id=1, source_target_pairs={{0,4},{4,0},{8,12},{12,8},{16,20},{20,16},{24,28},{28,24},{1,5},{5... | collective-permute-start | bytes 221192 | tf_op jit(solution)/shard_map/ppermute | solution.py:192
  12.6 6.2 %collective-permute-start.5 = (f32[2,2,72,128]{3,2,1,0:T(8,128)S(1)}, f32[2,2,72,128]{3,2,1,0:T(8,128)S(1)}, u32[]{:S(2)}, u32[]{:S(2)}) collective-permute-start(f32[2,2,72,128]{3,2,1,0:T(8,128)S(1)} %get-tuple-element.63), channel_id=1, source_target_pairs={{0,8},{4,12},{8,0},{12,4},{16,24},{20,28},{24,16},{28,20},{1,9},{5... | collective-permute-start | bytes 442376 | tf_op jit(solution)/shard_map/ppermute | solution.py:216
  15.5 6.1 %copy-start = (f32[1,2,64,4096]{3,2,1,0:T(8,128)S(1)}, f32[1,2,64,4096]{3,2,1,0:T(8,128)}, u32[]{:S(2)}) copy-start(f32[1,2,64,4096]{3,2,1,0:T(8,128)} %param.12) | copy-start | bytes 6291460
  15.5 6.1 %copy-start.1 = (f32[1,2,64,4096]{3,2,1,0:T(8,128)S(1)}, f32[1,2,64,4096]{3,2,1,0:T(8,128)}, u32[]{:S(2)}) copy-start(f32[1,2,64,4096]{3,2,1,0:T(8,128)} %param.13) | copy-start | bytes 6291460
  18.9 6.6 %collective-permute-start.6 = (f32[1,2,72,128]{3,2,1,0:T(8,128)S(1)}, f32[1,2,72,128]{3,2,1,0:T(8,128)S(1)}, u32[]{:S(2)}, u32[]{:S(2)}) collective-permute-start(f32[1,2,72,128]{3,2,1,0:T(8,128)S(1)} %get-tuple-element.66), channel_id=1, source_target_pairs={{0,16},{4,20},{8,24},{12,28},{16,0},{20,4},{24,8},{28,12},{1,17},{... | collective-permute-start | bytes 221192 | tf_op jit(solution)/shard_map/ppermute | solution.py:216
  28.0 8.7 %collective-permute-start.7 = (f32[2,64,128]{2,1,0:T(8,128)S(1)}, f32[2,64,128]{2,1,0:T(8,128)S(1)}, u32[]{:S(2)}, u32[]{:S(2)}) collective-permute-start(f32[2,64,128]{2,1,0:T(8,128)S(1)} %get-tuple-element.72.refs_0_), channel_id=1, source_target_pairs={{0,8},{4,12},{8,16},{12,20},{16,24},{20,28},{24,0},{28,4},{1,9},{5... | collective-permute-start | bytes 196616 | tf_op jit(solution)/shard_map/ppermute | solution.py:188
  29.5 7.2 %collective-permute-start.8 = (f32[2,64,128]{2,1,0:T(8,128)S(1)}, f32[2,64,128]{2,1,0:T(8,128)S(1)}, u32[]{:S(2)}, u32[]{:S(2)}) collective-permute-start(f32[2,64,128]{2,1,0:T(8,128)S(1)} %get-tuple-element.72.refs_0_), channel_id=1, source_target_pairs={{0,16},{4,20},{8,24},{12,28},{16,0},{20,4},{24,8},{28,12},{1,17},{... | collective-permute-start | bytes 196616 | tf_op jit(solution)/shard_map/ppermute | solution.py:188
  31.9 4.8 %collective-permute-start.9 = (f32[2,64,128]{2,1,0:T(8,128)S(1)}, f32[2,64,128]{2,1,0:T(8,128)S(1)}, u32[]{:S(2)}, u32[]{:S(2)}) collective-permute-start(f32[2,64,128]{2,1,0:T(8,128)S(1)} %get-tuple-element.72.refs_0_), channel_id=1, source_target_pairs={{0,24},{4,28},{8,0},{12,4},{16,8},{20,12},{24,16},{28,20},{1,25},{... | collective-permute-start | bytes 196616 | tf_op jit(solution)/shard_map/ppermute | solution.py:188
  36.8 1.4 %collective-permute-start.10 = (f32[2,64,128]{2,1,0:T(8,128)S(1)}, f32[2,64,128]{2,1,0:T(8,128)S(1)}, u32[]{:S(2)}, u32[]{:S(2)}) collective-permute-start(f32[2,64,128]{2,1,0:T(8,128)S(1)} %get-tuple-element.75), channel_id=1, source_target_pairs={{0,4},{4,0},{8,12},{12,8},{16,20},{20,16},{24,28},{28,24},{1,5},{5... | collective-permute-start | bytes 196616 | tf_op jit(solution)/shard_map/ppermute | solution.py:192

commit v7 on v6

--- a/solution.py
+++ b/solution.py
@@ -12,7 +12,7 @@
 SWEEPS = 3
 LANES = 128
 PAD = 8
-CARRY = 4 * 10**10, 10**10
+CARRY = 4 * 10**10, 5 * 10**9, 4 * 10**10
 MIB = 1 << 20
 
 VMEM_SPEC = pl.BlockSpec(memory_space=pltpu.VMEM)
@@ -88,24 +88,19 @@
     return (high, low), token
 
 
+def tiles_kernel(mult_ref, m1_ref, m2_ref):
+    rows = mult_ref.shape[1]
+    even = lax.rem(lax.axis_index("tile"), 2) == 0
+    top, bottom = mult_ref[:, :PAD], mult_ref[:, rows - PAD :]
+    m1_ref[...] = jnp.where(even, bottom, top)
+    m2_ref[...] = jnp.where(even, top, bottom)
+
+
 def edges_kernel(
-    start_hbm, load_hbm, diag_hbm, mult_ref, peer_ref, len_ref, active_ref,
-    m1_ref, m2_ref, one_ref, two_ref, peers_ref, mask_ref, buf, sem,
+    start_ref, load_ref, diag_ref, _, peer_ref, len_ref, active_ref, one_ref, two_ref, peers_ref, mask_ref
 ):
-    rows = start_hbm.shape[1]
+    _, rows, width = start_ref.shape
     even = lax.rem(lax.axis_index("tile"), 2) == 0
-    ends = (pl.ds(0, PAD), pl.ds(rows - PAD, PAD))
-    copies = [
-        pltpu.make_async_copy(ref.at[:, ends[e]], buf.at[i, e], sem.at[i, e])
-        for i, ref in enumerate((start_hbm, load_hbm, diag_hbm))
-        for e in range(2)
-    ]
-    for copy in copies:
-        copy.start()
-    for c in range(2):
-        top, bottom = mult_ref[c, ends[0]], mult_ref[c, ends[1]]
-        m1_ref[c] = jnp.where(even, bottom, top)
-        m2_ref[c] = jnp.where(even, top, bottom)
     me = lax.axis_index("sub")
     first = lax.axis_index("tile") * rows
     at = lax.broadcasted_iota(jnp.int32, peers_ref.shape[1:], 0)
@@ -114,16 +109,18 @@
     peers_ref[1] = line_peers(peer_ref, len_ref, me + 1 - 2 * lax.rem(me, 2), lines)
     at = lax.broadcasted_iota(jnp.int32, mask_ref.shape, 0) + (first - PAD)
     mask_ref[...] = jnp.where((at >= 0) & (at < active_ref[me]), 1.0, 0.0)
-    row = lax.broadcasted_iota(jnp.int32, (PAD, start_hbm.shape[2]), 0)
-    for copy in copies:
-        copy.wait()
+    row = lax.broadcasted_iota(jnp.int32, (PAD, width), 0)
+    ends = (slice(0, PAD), slice(rows - PAD, rows))
 
     def lines_of(c, e, turns):
-        field, load, diag = (pltpu.roll(buf[i, e, c], t, 0) if t else buf[i, e, c] for i, t in enumerate(turns))
-        return jnp.where(row < 3, field, jnp.where(row < 5, load, diag))
-
-    for c in range(2):
-        top, bottom = pack_rows(lines_of(c, 0, (0, 3, 5))), pack_rows(lines_of(c, 1, (3, 5, 7)))
+        field, load, diag = (
+            pltpu.roll(ref[c, ends[e]], t, 0) if t else ref[c, ends[e]]
+            for ref, t in zip((start_ref, load_ref, diag_ref), turns)
+        )
+        return pack_rows(jnp.where(row < 3, field, jnp.where(row < 5, load, diag)))
+
+    for c in range(2):
+        top, bottom = lines_of(c, 0, (0, 3, 5)), lines_of(c, 1, (3, 5, 7))
         one_ref[c] = jnp.where(even, bottom, top)
         two_ref[c] = jnp.where(even, top, bottom)
 
@@ -515,39 +512,48 @@
 
     count = lax.axis_size("sub")
 
-    m1, m2, one, two, peers, mask = call(
+    m1, m2 = call(
+        tiles_kernel,
+        (mult,),
+        [VMEM_SPEC],
+        [held((2, PAD, IB))] * 2,
+        MIB,
+        flops=CARRY[0],
+        moved=10**6,
+    )
+    ends = (m1, m2)
+    m1, m2 = swap_edges(m1, m2)
+    one, two, peers, mask = call(
         edges_kernel,
-        (start, load, diag, mult, contact_peer, contact_len, active_rows),
-        [ANY_SPEC] * 3 + [VMEM_SPEC] + [SMEM_SPEC] * 3,
-        [held((2, PAD, IB))] * 2
-        + [held((2, PAD, width // PAD * (PAD - 1)))] * 2
+        (start, load, diag, ends[0], contact_peer, contact_len, active_rows),
+        [VMEM_SPEC] * 4 + [SMEM_SPEC] * 3,
+        [held((2, PAD, width // PAD * (PAD - 1)))] * 2
         + [held((2, rows + PAD, LANES), jnp.int32), held((high, LANES))],
-        56 * MIB,
-        [pltpu.VMEM((3, 2, 2, PAD, width), jnp.float32), pltpu.SemaphoreType.DMA((3, 2))],
-    )
-    m1, m2 = passed(CARRY[0], m1, m2)
-    m1, m2 = swap_edges(m1, m2)
-    one, two = swap_edges(one, two)
-    (mask,) = passed(CARRY[1], mask)
+        4 * MIB,
+        flops=CARRY[2],
+        moved=10**6,
+    )
+    got_one, got_two = swap_edges(one, two)
     flat = flat_weights(block_inverse[0])
     chips = count // 2
     quarter = nb // 4
-    w1, token = split_weights(flat, size, 0, quarter, mask)
     lines_mult = call(
         lines_kernel,
-        (mult, m1, m2, token),
+        (mult, m1, m2, one),
         [VMEM_SPEC] * 4,
         held((2, rows + PAD, IB)),
         MIB,
     )
     other = swap_cores(lines_mult)
-    w2, token = split_weights(flat, size, quarter, quarter, token)
+    mask, after = passed(CARRY[1], mask, lines_mult)
+    w1, token = split_weights(flat, size, 0, quarter, after)
     half = held((chips // 2, *lines_mult.shape))
     keep, send = call(
         merge_kernel, (peers, lines_mult, other, token), [VMEM_SPEC] * 4, [half] * 2, 2 * MIB
     )
     got = over_bit(send, 1)
-    w3, token = split_weights(flat, size, 2 * quarter, nb - 2 * quarter, keep)
+    w2, token = split_weights(flat, size, quarter, quarter, keep)
+    w3, token = split_weights(flat, size, 2 * quarter, nb - 2 * quarter, token)
     weights = (*w1, *w2, *w3)
     step = 6 * high * (2 * size) ** 2
     some = held((2, 2 * PAD, width))
@@ -578,7 +584,7 @@
     incoming = [keep[0], got[0]]
     srce, dge, f0e, f1 = run(
         first_kernel,
-        (start, diag, one, two, src, add, mask),
+        (start, diag, got_one, got_two, src, add, mask),
         [some, some, some, held((2, high, (nb - 1) * size))],
         nb - 1,
     )

time: 40 us -> 39.6 us (0.990)
  starting transfers between devices: 14.9 us -> 17.1 us
  waiting for transfers between devices: 1.85 us -> 0.03 us
  Pallas kernels: 21.9 us -> 20.2 us
  local copies, waits for them, and re-layouts: 0.07 us -> 0.91 us
    pallas_call x16, Pallas kernels: 21.9 us -> 20.2 us  [call(): pl.pallas_call(kernel, out_shape=outs, in_specs=specs, out_specs=out_spec...]
    ppermute x2, waiting for transfers between devices: 1.26 us -> 0.01 us  [over_bit(): lax.ppermute(cells, 'sub', [(i, i ^ 2 * bit) for i in range(lax.axis_size...]
    ppermute x4, starting transfers between devices: 6.01 us -> 7.24 us  [swap_edges(): return (lax.ppermute(one, 'tile', first), lax.ppermute(two, 'tile', second))]
    ppermute x2, starting transfers between devices: 4.32 us -> 5.18 us  [over_bit(): lax.ppermute(cells, 'sub', [(i, i ^ 2 * bit) for i in range(lax.axis_size...]
    unnamed x22 -> x30, local copies, waits for them, and re-layouts: 0.07 us -> 0.91 us
    ppermute x4, waiting for transfers between devices: 0.48 us -> 0.01 us  [swap_edges(): return (lax.ppermute(one, 'tile', first), lax.ppermute(two, 'tile', second))]
  transfers between devices with their start and end apart: 11 -> 11, of which waited for: 4 -> 0; matrix products, arithmetic and copies ran while one was open for 0% -> 0% of each run, Pallas kernels for 38% -> 41%
where the time goes in v7:
time: 39.6 us; the launch traced here: 39.4 us
  Pallas kernels  20.2 us (51%)
  starting transfers between devices  17.1 us (43%)
  between operations  1.13 us (3%)
  local copies, waits for them, and re-layouts  0.91 us (2%)
    pallas_call x16, Pallas kernels, call(): pl.pallas_call(kernel, out_shape=outs, in_specs=specs, out_specs=out_spec...  20.2 us
    ppermute x4, starting transfers between devices, swap_edges(): return (lax.ppermute(one, 'tile', first), lax.ppermute(two, 'tile', second))  7.24 us
    ppermute x2, starting transfers between devices, over_bit(): lax.ppermute(cells, 'sub', [(i, i ^ 2 * bit) for i in range(lax.axis_size...  5.18 us
    ppermute x3, starting transfers between devices, to_chip(): lax.ppermute(cells, 'sub', [(i, (i + 2 * step) % count) for i in range(co...  4.56 us
    unnamed x30, local copies, waits for them, and re-layouts  0.91 us
  transfers between devices with their start and end apart: 11, of which 0 were waited for; matrix products, arithmetic and copies ran while one was open for 0% of the time, Pallas kernels for 41%

profile of v7, /device:TPU:0, one launch (start us, length us, event | category | flops | bytes accessed | tf_op | source)
XLA Modules:
  0.0 39.4 jit_solution(11207827528752545709)
XLA Ops:
  0.6 0.0 copy-start.3
  0.6 0.8 %copy-done.3 = f32[1,2,64,128]{3,2,1,0:T(8,128)S(1)} copy-done((f32[1,2,64,128]{3,2,1,0:T(8,128)S(1)}, f32[1,2,64,128]{3,2,1,0:T(8,128)}, u32[]{:S(2)}) %copy-start.3) | copy-done | bytes 65560
  1.5 0.0 copy-start
  1.5 0.0 copy-start.1
  1.5 0.0 copy-start.2
  1.5 0.0 copy-start.8
  1.5 0.0 copy-start.9
  1.5 0.0 copy-start.10
  1.5 0.0 slice-start
  1.5 0.0 slice-start.1
  1.6 3.0 %collective-permute-start.2 = (f32[2,8,128]{2,1,0:T(8,128)S(1)}, f32[2,8,128]{2,1,0:T(8,128)S(1)}, u32[]{:S(2)}, u32[]{:S(2)}) collective-permute-start(f32[2,8,128]{2,1,0:T(8,128)S(1)} %get-tuple-element.40._), channel_id=1, source_target_pairs={{0,1},{1,0},{2,3},{3,2},{4,5},{5,4},{6,7},{7,6},{8,9},{9,8},{10,11... | collective-permute-start | bytes 24584 | tf_op jit(solution)/shard_map/ppermute | solution.py:180
  4.6 1.5 %collective-permute-start.3 = (f32[2,8,128]{2,1,0:T(8,128)S(1)}, f32[2,8,128]{2,1,0:T(8,128)S(1)}, u32[]{:S(2)}, u32[]{:S(2)}) collective-permute-start(f32[2,8,128]{2,1,0:T(8,128)S(1)} %get-tuple-element.43), channel_id=1, source_target_pairs={{0,3},{1,2},{2,1},{3,0},{4,7},{5,6},{6,5},{7,4},{8,11},{9,10},{10,... | collective-permute-start | bytes 24584 | tf_op jit(solution)/shard_map/ppermute | solution.py:180
  6.0 0.0 copy-done
  6.1 0.0 copy-done.1
  6.1 0.0 copy-done.2
  6.1 0.0 copy-done.8
  6.1 0.0 copy-done.9
  6.1 0.0 copy-done.10
  6.1 0.0 copy-start.4
  6.1 0.0 slice-start.2
  6.1 0.0 slice-start.3
  6.1 0.9 %shard_map.123 = (f32[2,8,3584]{2,1,0:T(8,128)S(1)}, f32[2,8,3584]{2,1,0:T(8,128)S(1)}, s32[2,72,128]{2,1,0:T(8,128)S(1)}, f32[80,128]{1,0:T(8,128)S(1)}) custom-call(f32[2,64,4096]{2,1,0:T(8,128)S(1)} %bitcast.24, f32[2,64,4096]{2,1,0:T(8,128)S(1)} %bitcast.27, f32[2,64,4096]{2,1,0:T(8,128)S(1)} %bitcast.18, f32[2,8,128]{2,1,0:T(8,128)S(1)} %get-tuple-element.40._, ...), custom_call_target="tpu_custom_call" | custom-call | flops 40000000000 | bytes 1000000 | tf_op jit(solution)/shard_map/pallas_call | solution.py:24
  7.0 1.6 %collective-permute-start = (f32[2,8,3584]{2,1,0:T(8,128)S(1)}, f32[2,8,3584]{2,1,0:T(8,128)S(1)}, u32[]{:S(2)}, u32[]{:S(2)}) collective-permute-start(f32[2,8,3584]{2,1,0:T(8,128)S(1)} %get-tuple-element.41._), channel_id=1, source_target_pairs={{0,1},{1,0},{2,3},{3,2},{4,5},{5,4},{6,7},{7,6},{8,9},{9,8},{10,11... | collective-permute-start | bytes 688136 | tf_op jit(solution)/shard_map/ppermute | solution.py:180
  8.6 1.2 %collective-permute-start.1 = (f32[2,8,3584]{2,1,0:T(8,128)S(1)}, f32[2,8,3584]{2,1,0:T(8,128)S(1)}, u32[]{:S(2)}, u32[]{:S(2)}) collective-permute-start(f32[2,8,3584]{2,1,0:T(8,128)S(1)} %get-tuple-element.42), channel_id=1, source_target_pairs={{0,3},{1,2},{2,1},{3,0},{4,7},{5,6},{6,5},{7,4},{8,11},{9,10},{10,... | collective-permute-start | bytes 688136 | tf_op jit(solution)/shard_map/ppermute | solution.py:180
  9.8 0.0 collective-permute-done.2.one_ref
  9.8 0.0 collective-permute-done.3.two_ref
  9.8 0.0 copy-done.4
  9.8 0.1 collective-permute-start.4
  9.9 0.0 slice-done
  9.9 0.0 slice-done.1
  9.9 0.0 slice-done.2
  9.9 0.0 slice-done.3
  10.0 0.0 copy-start.5
  10.0 0.0 copy-start.6
  10.0 0.0 copy-start.7
  10.0 1.1 %shard_map.127 = (bf16[4,512,512]{2,1,0:T(8,128)(2,1)S(1)}, bf16[4,512,512]{2,1,0:T(8,128)(2,1)S(1)}, f32[8,128]{1,0:T(8,128)S(1)}) custom-call(f32[16,2048,128]{2,1,0:T(8,128)S(1)} %bitcast.15, f32[2,72,128]{2,1,0:T(8,128)S(1)} %get-tuple-element.48._), custom_call_target="tpu_custom_call" | custom-call | bytes 8388608 | tf_op jit(solution)/shard_map/pallas_call | solution.py:24
  11.2 0.0 collective-permute-done.4.other_ref
  11.2 0.1 shard_map.128
  11.2 2.5 %collective-permute-start.5 = (f32[2,2,72,128]{3,2,1,0:T(8,128)S(1)}, f32[2,2,72,128]{3,2,1,0:T(8,128)S(1)}, u32[]{:S(2)}, u32[]{:S(2)}) collective-permute-start(f32[2,2,72,128]{3,2,1,0:T(8,128)S(1)} %get-tuple-element.63), channel_id=1, source_target_pairs={{0,8},{4,12},{8,0},{12,4},{16,24},{20,28},{24,16},{28,20},{1,9},{5... | collective-permute-start | bytes 442376 | tf_op jit(solution)/shard_map/ppermute | solution.py:213
  13.7 0.0 copy-done.5
  13.7 0.0 copy-done.6
  13.8 0.0 copy-done.7
  13.8 1.2 %shard_map.125 = (f32[2,64,4096]{2,1,0:T(8,128)S(1)}, f32[2,16,4096]{2,1,0:T(8,128)S(1)}) custom-call(f32[2,64,4096]{2,1,0:T(8,128)S(1)} %bitcast.28, f32[2,72,128]{2,1,0:T(8,128)S(1)} %shard_map.124.mult_ref.refs_1_.own_ref, s32[1,16]{1,0:T(1,128)S(1)} %copy-done.6, s32[1,16]{1,0:T(1,128)S(1)} %copy-done.7, f32[1,2,16]{2,1,0:T(2,128)S(1)} %copy-done.5), custom_call_target="tpu_custom_call" | custom-call | bytes 8388608 | tf_op jit(solution)/shard_map/pallas_call | solution.py:24
  14.9 1.1 %shard_map.129 = (bf16[4,512,512]{2,1,0:T(8,128)(2,1)S(1)}, bf16[4,512,512]{2,1,0:T(8,128)(2,1)S(1)}, f32[8,128]{1,0:T(8,128)S(1)}) custom-call(f32[16,2048,128]{2,1,0:T(8,128)S(1)} %bitcast.16, f32[2,2,72,128]{3,2,1,0:T(8,128)S(1)} %get-tuple-element.53._.keep_ref), custom_call_target="tpu_custom_call" | custom-call | bytes 8388608 | tf_op jit(solution)/shard_map/pallas_call | solution.py:24
  16.1 2.2 %shard_map.130 = (bf16[8,512,512]{2,1,0:T(8,128)(2,1)S(1)}, bf16[8,512,512]{2,1,0:T(8,128)(2,1)S(1)}, f32[8,128]{1,0:T(8,128)S(1)}) custom-call(f32[16,2048,128]{2,1,0:T(8,128)S(1)} %bitcast.17, f32[8,128]{1,0:T(8,128)S(1)} %get-tuple-element.56._), custom_call_target="tpu_custom_call" | custom-call | bytes 16777216 | tf_op jit(solution)/shard_map/pallas_call | solution.py:24
  18.3 0.0 collective-permute-done.5.got_ref
  18.4 2.7 %collective-permute-start.6 = (f32[1,2,72,128]{3,2,1,0:T(8,128)S(1)}, f32[1,2,72,128]{3,2,1,0:T(8,128)S(1)}, u32[]{:S(2)}, u32[]{:S(2)}) collective-permute-start(f32[1,2,72,128]{3,2,1,0:T(8,128)S(1)} %get-tuple-element.66), channel_id=1, source_target_pairs={{0,16},{4,20},{8,24},{12,28},{16,0},{20,4},{24,8},{28,12},{1,17},{... | collective-permute-start | bytes 221192 | tf_op jit(solution)/shard_map/ppermute | solution.py:213
  21.0 0.0 collective-permute-done.one_ref
  21.0 0.0 collective-permute-done.1.two_ref
  21.0 3.9 %shard_map.131 = (f32[2,16,4096]{2,1,0:T(8,128)S(1)}, f32[2,16,4096]{2,1,0:T(8,128)S(1)}, f32[2,16,4096]{2,1,0:T(8,128)S(1)}, f32[2,80,3840]{2,1,0:T(8,128)S(1)}) custom-call(f32[2,64,4096]{2,1,0:T(8,128)S(1)} %bitcast.25, f32[2,64,4096]{2,1,0:T(8,128)S(1)} %bitcast.19, f32[2,8,3584]{2,1,0:T(8,128)S(1)} %collective-permute-done.one_ref, ...), custom_call_target="tpu_custom_call" | custom-call | flops 1887436800 | tf_op jit(solution)/shard_map/pallas_call | solution.py:24
  24.9 0.0 collective-permute-done.6
  24.9 2.5 %shard_map.133 = (f32[2,80,1536]{2,1,0:T(8,128)S(1)}, f32[2,80,512]{2,1,0:T(8,128)S(1)}, f32[2,64,256]{2,1,0:T(8,128)S(1)}, f32[2,64,128]{2,1,0:T(8,128)S(1)}) custom-call(f32[2,64,4096]{2,1,0:T(8,128)S(1)} %bitcast.26, f32[2,16,4096]{2,1,0:T(8,128)S(1)} %get-tuple-element.60.f0e_ref, f32[2,80,3840]{2,1,0:T(8,128)S(1)} %get-tuple-element.59.f1_ref, ...), custom_call_target="tpu_custom_call" | custom-call | flops 1258291200 | tf_op jit(solution)/shard_map/pallas_call | solution.py:24
  27.5 1.0 %collective-permute-start.7 = (f32[2,64,128]{2,1,0:T(8,128)S(1)}, f32[2,64,128]{2,1,0:T(8,128)S(1)}, u32[]{:S(2)}, u32[]{:S(2)}) collective-permute-start(f32[2,64,128]{2,1,0:T(8,128)S(1)} %get-tuple-element.72.refs_0_), channel_id=1, source_target_pairs={{0,8},{4,12},{8,16},{12,20},{16,24},{20,28},{24,0},{28,4},{1,9},{5... | collective-permute-start | bytes 196616 | tf_op jit(solution)/shard_map/ppermute | solution.py:185
  28.5 2.2 %collective-permute-start.8 = (f32[2,64,128]{2,1,0:T(8,128)S(1)}, f32[2,64,128]{2,1,0:T(8,128)S(1)}, u32[]{:S(2)}, u32[]{:S(2)}) collective-permute-start(f32[2,64,128]{2,1,0:T(8,128)S(1)} %get-tuple-element.72.refs_0_), channel_id=1, source_target_pairs={{0,16},{4,20},{8,24},{12,28},{16,0},{20,4},{24,8},{28,12},{1,17},{... | collective-permute-start | bytes 196616 | tf_op jit(solution)/shard_map/ppermute | solution.py:185
  30.7 1.3 %collective-permute-start.9 = (f32[2,64,128]{2,1,0:T(8,128)S(1)}, f32[2,64,128]{2,1,0:T(8,128)S(1)}, u32[]{:S(2)}, u32[]{:S(2)}) collective-permute-start(f32[2,64,128]{2,1,0:T(8,128)S(1)} %get-tuple-element.72.refs_0_), channel_id=1, source_target_pairs={{0,24},{4,28},{8,0},{12,4},{16,8},{20,12},{24,16},{28,20},{1,25},{... | collective-permute-start | bytes 196616 | tf_op jit(solution)/shard_map/ppermute | solution.py:185
  32.0 4.3 %shard_map.134 = (f32[2,64,4096]{2,1,0:T(8,128)}, f32[2,80,2048]{2,1,0:T(8,128)S(1)}, f32[2,64,2304]{2,1,0:T(8,128)S(1)}) custom-call(f32[2,80,3840]{2,1,0:T(8,128)S(1)} %get-tuple-element.59.f1_ref, f32[2,80,1536]{2,1,0:T(8,128)S(1)} %get-tuple-element.67.f2s_ref, f32[2,64,4096]{2,1,0:T(8,128)S(1)} %get-tuple-element.44.src_ref, ...), custom_call_target="tpu_custom_call" | custom-call | flops 2139095040 | tf_op jit(solution)/shard_map/pallas_call | solution.py:24
  36.3 0.0 collective-permute-done.7.refs_1_
  36.3 0.0 collective-permute-done.8.refs_2_
  36.3 0.0 collective-permute-done.9.refs_3_
  36.3 0.1 shard_map.135
  36.4 0.1 collective-permute-start.10
  36.5 1.3 %shard_map.136.more_ref = f32[2,64,1280]{2,1,0:T(8,128)S(1)} custom-call(f32[2,80,1536]{2,1,0:T(8,128)S(1)} %get-tuple-element.67.f2s_ref, f32[2,80,2048]{2,1,0:T(8,128)S(1)} %get-tuple-element.69.f2_ref, f32[2,80,512]{2,1,0:T(8,128)S(1)} %get-tuple-element.70.f2e_ref, f32[2,64,4096]{2,1,0:T(8,128)S(1)} %get-tuple-element.44.src_ref, ...), custom_call_target="tpu_custom_call" | custom-call | flops 629145600 | tf_op jit(solution)/shard_map/pallas_call | solution.py:24
  37.8 0.0 collective-permute-done.10.theirs_ref
  37.8 1.4 %shard_map.137 = (f32[2,64,4096]{2,1,0:T(8,128)}, f32[2,64,128]{2,1,0:T(8,128)}) custom-call(f32[2,64,4096]{2,1,0:T(8,128)} %get-tuple-element.68._, f32[2,80,2048]{2,1,0:T(8,128)S(1)} %get-tuple-element.69.f2_ref, f32[2,80,512]{2,1,0:T(8,128)S(1)} %get-tuple-element.70.f2e_ref, ...), custom_call_target="tpu_custom_call", output_to_operand_aliasing={{0}: (0, {})} | custom-call | flops 125829120 | tf_op jit(solution)/shard_map/pallas_call | solution.py:24
  (5 shorter events, 0.1 us)
Async XLA Ops:
  0.6 0.8 %copy-start.3 = (f32[1,2,64,128]{3,2,1,0:T(8,128)S(1)}, f32[1,2,64,128]{3,2,1,0:T(8,128)}, u32[]{:S(2)}) copy-start(f32[1,2,64,128]{3,2,1,0:T(8,128)} %param.15) | copy-start | bytes 196612
  1.5 4.6 %copy-start = (f32[1,2,64,4096]{3,2,1,0:T(8,128)S(1)}, f32[1,2,64,4096]{3,2,1,0:T(8,128)}, u32[]{:S(2)}) copy-start(f32[1,2,64,4096]{3,2,1,0:T(8,128)} %param.12) | copy-start | bytes 6291460
  1.5 4.6 %copy-start.1 = (f32[1,2,64,4096]{3,2,1,0:T(8,128)S(1)}, f32[1,2,64,4096]{3,2,1,0:T(8,128)}, u32[]{:S(2)}) copy-start(f32[1,2,64,4096]{3,2,1,0:T(8,128)} %param.13) | copy-start | bytes 6291460
  1.5 4.6 %copy-start.2 = (f32[1,2,64,4096]{3,2,1,0:T(8,128)S(1)}, f32[1,2,64,4096]{3,2,1,0:T(8,128)}, u32[]{:S(2)}) copy-start(f32[1,2,64,4096]{3,2,1,0:T(8,128)} %param.11) | copy-start | bytes 6291460
  1.5 4.6 %copy-start.8 = (s32[8,8]{1,0:T(8,128)S(1)}, s32[8,8]{1,0:T(8,128)}, u32[]{:S(2)}) copy-start(s32[8,8]{1,0:T(8,128)} %peer_ref.1) | copy-start | bytes 772
  1.5 4.6 %copy-start.9 = (s32[8,8]{1,0:T(8,128)S(1)}, s32[8,8]{1,0:T(8,128)}, u32[]{:S(2)}) copy-start(s32[8,8]{1,0:T(8,128)} %len_ref.1) | copy-start | bytes 772
  1.5 4.6 %copy-start.10 = (s32[8]{0:T(128)S(1)}, s32[8]{0:T(128)}, u32[]{:S(2)}) copy-start(s32[8]{0:T(128)} %active_ref.1) | copy-start | bytes 100
  1.5 8.4 %slice-start = ((s8[16777216]{0:T(1024)(128)(4,1)}), s8[4194304]{0:T(1024)(128)(4,1)S(1)}, s32[]{:S(2)}) async-start(s8[16777216]{0:T(1024)(128)(4,1)} %bitcast.13), calls=%async_computation | async-start | bytes 8388608
  1.5 8.4 %slice-start.1 = ((s8[16777216]{0:T(1024)(128)(4,1)}), s8[4194304]{0:T(1024)(128)(4,1)S(1)}, s32[]{:S(2)}) async-start(s8[16777216]{0:T(1024)(128)(4,1)} %bitcast.13), calls=%async_computation.1 | async-start | bytes 8388608
  1.6 8.2 %collective-permute-start.2 = (f32[2,8,128]{2,1,0:T(8,128)S(1)}, f32[2,8,128]{2,1,0:T(8,128)S(1)}, u32[]{:S(2)}, u32[]{:S(2)}) collective-permute-start(f32[2,8,128]{2,1,0:T(8,128)S(1)} %get-tuple-element.40._), channel_id=1, source_target_pairs={{0,1},{1,0},{2,3},{3,2},{4,5},{5,4},{6,7},{7,6},{8,9},{9,8},{10,11... | collective-permute-start | bytes 24584 | tf_op jit(solution)/shard_map/ppermute | solution.py:180
  4.6 5.2 %collective-permute-start.3 = (f32[2,8,128]{2,1,0:T(8,128)S(1)}, f32[2,8,128]{2,1,0:T(8,128)S(1)}, u32[]{:S(2)}, u32[]{:S(2)}) collective-permute-start(f32[2,8,128]{2,1,0:T(8,128)S(1)} %get-tuple-element.43), channel_id=1, source_target_pairs={{0,3},{1,2},{2,1},{3,0},{4,7},{5,6},{6,5},{7,4},{8,11},{9,10},{10,... | collective-permute-start | bytes 24584 | tf_op jit(solution)/shard_map/ppermute | solution.py:180
  6.1 3.7 %copy-start.4 = (f32[1,2,64,128]{3,2,1,0:T(8,128)S(1)}, f32[1,2,64,128]{3,2,1,0:T(8,128)}, u32[]{:S(2)}) copy-start(f32[1,2,64,128]{3,2,1,0:T(8,128)} %param.15) | copy-start | bytes 196612
  6.1 3.8 %slice-start.2 = ((s8[16777216]{0:T(1024)(128)(4,1)}), s8[4194304]{0:T(1024)(128)(4,1)S(1)}, s32[]{:S(2)}) async-start(s8[16777216]{0:T(1024)(128)(4,1)} %bitcast.13), calls=%async_computation.2 | async-start | bytes 8388608
  6.1 3.8 %slice-start.3 = ((s8[16777216]{0:T(1024)(128)(4,1)}), s8[4194304]{0:T(1024)(128)(4,1)S(1)}, s32[]{:S(2)}) async-start(s8[16777216]{0:T(1024)(128)(4,1)} %bitcast.13), calls=%async_computation.3 | async-start | bytes 8388608
  7.0 14.0 %collective-permute-start = (f32[2,8,3584]{2,1,0:T(8,128)S(1)}, f32[2,8,3584]{2,1,0:T(8,128)S(1)}, u32[]{:S(2)}, u32[]{:S(2)}) collective-permute-start(f32[2,8,3584]{2,1,0:T(8,128)S(1)} %get-tuple-element.41._), channel_id=1, source_target_pairs={{0,1},{1,0},{2,3},{3,2},{4,5},{5,4},{6,7},{7,6},{8,9},{9,8},{10,11... | collective-permute-start | bytes 688136 | tf_op jit(solution)/shard_map/ppermute | solution.py:180
  8.6 12.4 %collective-permute-start.1 = (f32[2,8,3584]{2,1,0:T(8,128)S(1)}, f32[2,8,3584]{2,1,0:T(8,128)S(1)}, u32[]{:S(2)}, u32[]{:S(2)}) collective-permute-start(f32[2,8,3584]{2,1,0:T(8,128)S(1)} %get-tuple-element.42), channel_id=1, source_target_pairs={{0,3},{1,2},{2,1},{3,0},{4,7},{5,6},{6,5},{7,4},{8,11},{9,10},{10,... | collective-permute-start | bytes 688136 | tf_op jit(solution)/shard_map/ppermute | solution.py:180
  9.8 1.3 %collective-permute-start.4 = (f32[2,72,128]{2,1,0:T(8,128)S(1)}, f32[2,72,128]{2,1,0:T(8,128)S(1)}, u32[]{:S(2)}, u32[]{:S(2)}) collective-permute-start(f32[2,72,128]{2,1,0:T(8,128)S(1)} %shard_map.124.mult_ref.refs_1_.own_ref), channel_id=1, source_target_pairs={{0,4},{4,0},{8,12},{12,8},{16,20},{20,16},{24,28},{28,24},{1,5},{5... | collective-permute-start | bytes 221192 | tf_op jit(solution)/shard_map/ppermute | solution.py:189
  10.0 3.8 %copy-start.5 = (f32[1,2,16]{2,1,0:T(2,128)S(1)}, f32[1,2,16]{2,1,0:T(2,128)}, u32[]{:S(2)}) copy-start(f32[1,2,16]{2,1,0:T(2,128)} %pcur_ref.1) | copy-start | bytes 388
  10.0 3.8 %copy-start.6 = (s32[1,16]{1,0:T(1,128)S(1)}, s32[1,16]{1,0:T(1,128)}, u32[]{:S(2)}) copy-start(s32[1,16]{1,0:T(1,128)} %prow_ref.1) | copy-start | bytes 196
  10.0 3.8 %copy-start.7 = (s32[1,16]{1,0:T(1,128)S(1)}, s32[1,16]{1,0:T(1,128)}, u32[]{:S(2)}) copy-start(s32[1,16]{1,0:T(1,128)} %pcol_ref.1) | copy-start | bytes 196
  11.2 7.1 %collective-permute-start.5 = (f32[2,2,72,128]{3,2,1,0:T(8,128)S(1)}, f32[2,2,72,128]{3,2,1,0:T(8,128)S(1)}, u32[]{:S(2)}, u32[]{:S(2)}) collective-permute-start(f32[2,2,72,128]{3,2,1,0:T(8,128)S(1)} %get-tuple-element.63), channel_id=1, source_target_pairs={{0,8},{4,12},{8,0},{12,4},{16,24},{20,28},{24,16},{28,20},{1,9},{5... | collective-permute-start | bytes 442376 | tf_op jit(solution)/shard_map/ppermute | solution.py:213
  18.4 6.6 %collective-permute-start.6 = (f32[1,2,72,128]{3,2,1,0:T(8,128)S(1)}, f32[1,2,72,128]{3,2,1,0:T(8,128)S(1)}, u32[]{:S(2)}, u32[]{:S(2)}) collective-permute-start(f32[1,2,72,128]{3,2,1,0:T(8,128)S(1)} %get-tuple-element.66), channel_id=1, source_target_pairs={{0,16},{4,20},{8,24},{12,28},{16,0},{20,4},{24,8},{28,12},{1,17},{... | collective-permute-start | bytes 221192 | tf_op jit(solution)/shard_map/ppermute | solution.py:213
  27.5 8.8 %collective-permute-start.7 = (f32[2,64,128]{2,1,0:T(8,128)S(1)}, f32[2,64,128]{2,1,0:T(8,128)S(1)}, u32[]{:S(2)}, u32[]{:S(2)}) collective-permute-start(f32[2,64,128]{2,1,0:T(8,128)S(1)} %get-tuple-element.72.refs_0_), channel_id=1, source_target_pairs={{0,8},{4,12},{8,16},{12,20},{16,24},{20,28},{24,0},{28,4},{1,9},{5... | collective-permute-start | bytes 196616 | tf_op jit(solution)/shard_map/ppermute | solution.py:185
  28.5 7.8 %collective-permute-start.8 = (f32[2,64,128]{2,1,0:T(8,128)S(1)}, f32[2,64,128]{2,1,0:T(8,128)S(1)}, u32[]{:S(2)}, u32[]{:S(2)}) collective-permute-start(f32[2,64,128]{2,1,0:T(8,128)S(1)} %get-tuple-element.72.refs_0_), channel_id=1, source_target_pairs={{0,16},{4,20},{8,24},{12,28},{16,0},{20,4},{24,8},{28,12},{1,17},{... | collective-permute-start | bytes 196616 | tf_op jit(solution)/shard_map/ppermute | solution.py:185
  30.7 5.7 %collective-permute-start.9 = (f32[2,64,128]{2,1,0:T(8,128)S(1)}, f32[2,64,128]{2,1,0:T(8,128)S(1)}, u32[]{:S(2)}, u32[]{:S(2)}) collective-permute-start(f32[2,64,128]{2,1,0:T(8,128)S(1)} %get-tuple-element.72.refs_0_), channel_id=1, source_target_pairs={{0,24},{4,28},{8,0},{12,4},{16,8},{20,12},{24,16},{28,20},{1,25},{... | collective-permute-start | bytes 196616 | tf_op jit(solution)/shard_map/ppermute | solution.py:185
  36.4 1.4 %collective-permute-start.10 = (f32[2,64,128]{2,1,0:T(8,128)S(1)}, f32[2,64,128]{2,1,0:T(8,128)S(1)}, u32[]{:S(2)}, u32[]{:S(2)}) collective-permute-start(f32[2,64,128]{2,1,0:T(8,128)S(1)} %get-tuple-element.75), channel_id=1, source_target_pairs={{0,4},{4,0},{8,12},{12,8},{16,20},{20,16},{24,28},{28,24},{1,5},{5... | collective-permute-start | bytes 196616 | tf_op jit(solution)/shard_map/ppermute | solution.py:189

commit v8 on v7

--- a/solution.py
+++ b/solution.py
@@ -279,8 +279,8 @@
         mid, wide = tiles_of(field, c, k, size, last)
         rows, width = wide.shape
         beside = (
-            pltpu.roll(wide, 1, 1)[:, LANES : LANES + size]
-            + pltpu.roll(wide, width - 1, 1)[:, LANES : LANES + size]
+            pltpu.roll(wide[:, : width - LANES], 1, 1)[:, LANES:]
+            + pltpu.roll(wide[:, LANES:], width - LANES - 1, 1)[:, :size]
         )
         beside = beside + (pltpu.roll(mid, 1, 0) + pltpu.roll(mid, rows - 1, 0))
         mids.append(mid)
@@ -552,9 +552,8 @@
         merge_kernel, (peers, lines_mult, other, token), [VMEM_SPEC] * 4, [half] * 2, 2 * MIB
     )
     got = over_bit(send, 1)
-    w2, token = split_weights(flat, size, quarter, quarter, keep)
-    w3, token = split_weights(flat, size, 2 * quarter, nb - 2 * quarter, token)
-    weights = (*w1, *w2, *w3)
+    w2, token = split_weights(flat, size, quarter, nb - quarter, keep)
+    weights = (*w1, *w2)
     step = 6 * high * (2 * size) ** 2
     some = held((2, 2 * PAD, width))
 

time: 39.6 us -> 39.3 us (level)
  Pallas kernels: 20.2 us -> 19.8 us
    pallas_call x16 -> x15, Pallas kernels: 20.2 us -> 19.8 us  [call(): pl.pallas_call(kernel, out_shape=outs, in_specs=specs, out_specs=out_spec...]
where the time goes in v8:
time: 39.3 us; the launch traced here: 39.1 us
  Pallas kernels  19.8 us (50%)
  starting transfers between devices  17.2 us (44%)
  between operations  1.12 us (3%)
  local copies, waits for them, and re-layouts  0.91 us (2%)
    pallas_call x15, Pallas kernels, call(): pl.pallas_call(kernel, out_shape=outs, in_specs=specs, out_specs=out_spec...  19.8 us
    ppermute x4, starting transfers between devices, swap_edges(): return (lax.ppermute(one, 'tile', first), lax.ppermute(two, 'tile', second))  7.24 us
    ppermute x2, starting transfers between devices, over_bit(): lax.ppermute(cells, 'sub', [(i, i ^ 2 * bit) for i in range(lax.axis_size...  5.13 us
    ppermute x3, starting transfers between devices, to_chip(): lax.ppermute(cells, 'sub', [(i, (i + 2 * step) % count) for i in range(co...  4.68 us
    unnamed x30, local copies, waits for them, and re-layouts  0.91 us
  transfers between devices with their start and end apart: 11, of which 0 were waited for; matrix products, arithmetic and copies ran while one was open for 0% of the time, Pallas kernels for 41%

profile of v8, /device:TPU:0, one launch (start us, length us, event | category | flops | bytes accessed | tf_op | source)
XLA Modules:
  0.0 39.1 jit_solution(15759442489334297310)
XLA Ops:
  0.6 0.0 copy-start.3
  0.6 0.8 %copy-done.3 = f32[1,2,64,128]{3,2,1,0:T(8,128)S(1)} copy-done((f32[1,2,64,128]{3,2,1,0:T(8,128)S(1)}, f32[1,2,64,128]{3,2,1,0:T(8,128)}, u32[]{:S(2)}) %copy-start.3) | copy-done | bytes 65560
  1.5 0.0 copy-start
  1.5 0.0 copy-start.1
  1.5 0.0 copy-start.2
  1.5 0.0 copy-start.8
  1.5 0.0 copy-start.9
  1.5 0.0 copy-start.10
  1.5 0.0 slice-start
  1.5 0.0 slice-start.1
  1.6 3.0 %collective-permute-start.2 = (f32[2,8,128]{2,1,0:T(8,128)S(1)}, f32[2,8,128]{2,1,0:T(8,128)S(1)}, u32[]{:S(2)}, u32[]{:S(2)}) collective-permute-start(f32[2,8,128]{2,1,0:T(8,128)S(1)} %get-tuple-element.37._), channel_id=1, source_target_pairs={{0,1},{1,0},{2,3},{3,2},{4,5},{5,4},{6,7},{7,6},{8,9},{9,8},{10,11... | collective-permute-start | bytes 24584 | tf_op jit(solution)/shard_map/ppermute | solution.py:180
  4.6 1.5 %collective-permute-start.3 = (f32[2,8,128]{2,1,0:T(8,128)S(1)}, f32[2,8,128]{2,1,0:T(8,128)S(1)}, u32[]{:S(2)}, u32[]{:S(2)}) collective-permute-start(f32[2,8,128]{2,1,0:T(8,128)S(1)} %get-tuple-element.40), channel_id=1, source_target_pairs={{0,3},{1,2},{2,1},{3,0},{4,7},{5,6},{6,5},{7,4},{8,11},{9,10},{10,... | collective-permute-start | bytes 24584 | tf_op jit(solution)/shard_map/ppermute | solution.py:180
  6.0 0.0 copy-done
  6.1 0.0 copy-done.1
  6.1 0.0 copy-done.2
  6.1 0.0 copy-done.8
  6.1 0.0 copy-done.9
  6.1 0.0 copy-done.10
  6.1 0.0 copy-start.4
  6.1 0.0 slice-start.2
  6.1 0.0 slice-start.3
  6.1 0.9 %shard_map.123 = (f32[2,8,3584]{2,1,0:T(8,128)S(1)}, f32[2,8,3584]{2,1,0:T(8,128)S(1)}, s32[2,72,128]{2,1,0:T(8,128)S(1)}, f32[80,128]{1,0:T(8,128)S(1)}) custom-call(f32[2,64,4096]{2,1,0:T(8,128)S(1)} %bitcast.23, f32[2,64,4096]{2,1,0:T(8,128)S(1)} %bitcast.26, f32[2,64,4096]{2,1,0:T(8,128)S(1)} %bitcast.17, f32[2,8,128]{2,1,0:T(8,128)S(1)} %get-tuple-element.37._, ...), custom_call_target="tpu_custom_call" | custom-call | flops 40000000000 | bytes 1000000 | tf_op jit(solution)/shard_map/pallas_call | solution.py:24
  7.0 1.6 %collective-permute-start = (f32[2,8,3584]{2,1,0:T(8,128)S(1)}, f32[2,8,3584]{2,1,0:T(8,128)S(1)}, u32[]{:S(2)}, u32[]{:S(2)}) collective-permute-start(f32[2,8,3584]{2,1,0:T(8,128)S(1)} %get-tuple-element.38._), channel_id=1, source_target_pairs={{0,1},{1,0},{2,3},{3,2},{4,5},{5,4},{6,7},{7,6},{8,9},{9,8},{10,11... | collective-permute-start | bytes 688136 | tf_op jit(solution)/shard_map/ppermute | solution.py:180
  8.6 1.2 %collective-permute-start.1 = (f32[2,8,3584]{2,1,0:T(8,128)S(1)}, f32[2,8,3584]{2,1,0:T(8,128)S(1)}, u32[]{:S(2)}, u32[]{:S(2)}) collective-permute-start(f32[2,8,3584]{2,1,0:T(8,128)S(1)} %get-tuple-element.39), channel_id=1, source_target_pairs={{0,3},{1,2},{2,1},{3,0},{4,7},{5,6},{6,5},{7,4},{8,11},{9,10},{10,... | collective-permute-start | bytes 688136 | tf_op jit(solution)/shard_map/ppermute | solution.py:180
  9.8 0.0 collective-permute-done.2.one_ref
  9.8 0.0 collective-permute-done.3.two_ref
  9.8 0.0 copy-done.4
  9.8 0.1 collective-permute-start.4
  9.9 0.0 slice-done
  9.9 0.0 slice-done.1
  9.9 0.0 slice-done.2
  9.9 0.0 slice-done.3
  10.0 0.0 copy-start.5
  10.0 0.0 copy-start.6
  10.0 0.0 copy-start.7
  10.0 1.1 %shard_map.127 = (bf16[4,512,512]{2,1,0:T(8,128)(2,1)S(1)}, bf16[4,512,512]{2,1,0:T(8,128)(2,1)S(1)}, f32[8,128]{1,0:T(8,128)S(1)}) custom-call(f32[16,2048,128]{2,1,0:T(8,128)S(1)} %bitcast.15, f32[2,72,128]{2,1,0:T(8,128)S(1)} %get-tuple-element.45._), custom_call_target="tpu_custom_call" | custom-call | bytes 8388608 | tf_op jit(solution)/shard_map/pallas_call | solution.py:24
  11.2 0.0 collective-permute-done.4.other_ref
  11.2 0.1 shard_map.128
  11.2 2.5 %collective-permute-start.5 = (f32[2,2,72,128]{3,2,1,0:T(8,128)S(1)}, f32[2,2,72,128]{3,2,1,0:T(8,128)S(1)}, u32[]{:S(2)}, u32[]{:S(2)}) collective-permute-start(f32[2,2,72,128]{3,2,1,0:T(8,128)S(1)} %get-tuple-element.57), channel_id=1, source_target_pairs={{0,8},{4,12},{8,0},{12,4},{16,24},{20,28},{24,16},{28,20},{1,9},{5... | collective-permute-start | bytes 442376 | tf_op jit(solution)/shard_map/ppermute | solution.py:213
  13.7 0.0 copy-done.5
  13.7 0.0 copy-done.6
  13.8 0.0 copy-done.7
  13.8 1.2 %shard_map.125 = (f32[2,64,4096]{2,1,0:T(8,128)S(1)}, f32[2,16,4096]{2,1,0:T(8,128)S(1)}) custom-call(f32[2,64,4096]{2,1,0:T(8,128)S(1)} %bitcast.27, f32[2,72,128]{2,1,0:T(8,128)S(1)} %shard_map.124.mult_ref.refs_1_.own_ref, s32[1,16]{1,0:T(1,128)S(1)} %copy-done.6, s32[1,16]{1,0:T(1,128)S(1)} %copy-done.7, f32[1,2,16]{2,1,0:T(2,128)S(1)} %copy-done.5), custom_call_target="tpu_custom_call" | custom-call | bytes 8388608 | tf_op jit(solution)/shard_map/pallas_call | solution.py:24
  15.0 3.3 %shard_map.129 = (bf16[12,512,512]{2,1,0:T(8,128)(2,1)S(1)}, bf16[12,512,512]{2,1,0:T(8,128)(2,1)S(1)}, f32[8,128]{1,0:T(8,128)S(1)}) custom-call(f32[16,2048,128]{2,1,0:T(8,128)S(1)} %bitcast.16, f32[2,2,72,128]{3,2,1,0:T(8,128)S(1)} %get-tuple-element.50._.keep_ref), custom_call_target="tpu_custom_call" | custom-call | bytes 25165824 | tf_op jit(solution)/shard_map/pallas_call | solution.py:24
  18.3 0.0 collective-permute-done.5.got_ref
  18.3 2.6 %collective-permute-start.6 = (f32[1,2,72,128]{3,2,1,0:T(8,128)S(1)}, f32[1,2,72,128]{3,2,1,0:T(8,128)S(1)}, u32[]{:S(2)}, u32[]{:S(2)}) collective-permute-start(f32[1,2,72,128]{3,2,1,0:T(8,128)S(1)} %get-tuple-element.60), channel_id=1, source_target_pairs={{0,16},{4,20},{8,24},{12,28},{16,0},{20,4},{24,8},{28,12},{1,17},{... | collective-permute-start | bytes 221192 | tf_op jit(solution)/shard_map/ppermute | solution.py:213
  20.9 0.0 collective-permute-done.one_ref
  20.9 0.0 collective-permute-done.1.two_ref
  20.9 3.6 %shard_map.130 = (f32[2,16,4096]{2,1,0:T(8,128)S(1)}, f32[2,16,4096]{2,1,0:T(8,128)S(1)}, f32[2,16,4096]{2,1,0:T(8,128)S(1)}, f32[2,80,3840]{2,1,0:T(8,128)S(1)}) custom-call(f32[2,64,4096]{2,1,0:T(8,128)S(1)} %bitcast.24, f32[2,64,4096]{2,1,0:T(8,128)S(1)} %bitcast.18, f32[2,8,3584]{2,1,0:T(8,128)S(1)} %collective-permute-done.one_ref, ...), custom_call_target="tpu_custom_call" | custom-call | flops 1887436800 | tf_op jit(solution)/shard_map/pallas_call | solution.py:24
  24.6 0.0 collective-permute-done.6
  24.6 2.5 %shard_map.132 = (f32[2,80,1536]{2,1,0:T(8,128)S(1)}, f32[2,80,512]{2,1,0:T(8,128)S(1)}, f32[2,64,256]{2,1,0:T(8,128)S(1)}, f32[2,64,128]{2,1,0:T(8,128)S(1)}) custom-call(f32[2,64,4096]{2,1,0:T(8,128)S(1)} %bitcast.25, f32[2,16,4096]{2,1,0:T(8,128)S(1)} %get-tuple-element.54.f0e_ref, f32[2,80,3840]{2,1,0:T(8,128)S(1)} %get-tuple-element.53.f1_ref, ...), custom_call_target="tpu_custom_call" | custom-call | flops 1258291200 | tf_op jit(solution)/shard_map/pallas_call | solution.py:24
  27.1 1.1 %collective-permute-start.7 = (f32[2,64,128]{2,1,0:T(8,128)S(1)}, f32[2,64,128]{2,1,0:T(8,128)S(1)}, u32[]{:S(2)}, u32[]{:S(2)}) collective-permute-start(f32[2,64,128]{2,1,0:T(8,128)S(1)} %get-tuple-element.66.refs_0_), channel_id=1, source_target_pairs={{0,8},{4,12},{8,16},{12,20},{16,24},{20,28},{24,0},{28,4},{1,9},{5... | collective-permute-start | bytes 196616 | tf_op jit(solution)/shard_map/ppermute | solution.py:185
  28.2 2.4 %collective-permute-start.8 = (f32[2,64,128]{2,1,0:T(8,128)S(1)}, f32[2,64,128]{2,1,0:T(8,128)S(1)}, u32[]{:S(2)}, u32[]{:S(2)}) collective-permute-start(f32[2,64,128]{2,1,0:T(8,128)S(1)} %get-tuple-element.66.refs_0_), channel_id=1, source_target_pairs={{0,16},{4,20},{8,24},{12,28},{16,0},{20,4},{24,8},{28,12},{1,17},{... | collective-permute-start | bytes 196616 | tf_op jit(solution)/shard_map/ppermute | solution.py:185
  30.6 1.2 %collective-permute-start.9 = (f32[2,64,128]{2,1,0:T(8,128)S(1)}, f32[2,64,128]{2,1,0:T(8,128)S(1)}, u32[]{:S(2)}, u32[]{:S(2)}) collective-permute-start(f32[2,64,128]{2,1,0:T(8,128)S(1)} %get-tuple-element.66.refs_0_), channel_id=1, source_target_pairs={{0,24},{4,28},{8,0},{12,4},{16,8},{20,12},{24,16},{28,20},{1,25},{... | collective-permute-start | bytes 196616 | tf_op jit(solution)/shard_map/ppermute | solution.py:185
  31.8 4.3 %shard_map.133 = (f32[2,64,4096]{2,1,0:T(8,128)}, f32[2,80,2048]{2,1,0:T(8,128)S(1)}, f32[2,64,2304]{2,1,0:T(8,128)S(1)}) custom-call(f32[2,80,3840]{2,1,0:T(8,128)S(1)} %get-tuple-element.53.f1_ref, f32[2,80,1536]{2,1,0:T(8,128)S(1)} %get-tuple-element.61.f2s_ref, f32[2,64,4096]{2,1,0:T(8,128)S(1)} %get-tuple-element.41.src_ref, ...), custom_call_target="tpu_custom_call" | custom-call | flops 2139095040 | tf_op jit(solution)/shard_map/pallas_call | solution.py:24
  36.0 0.0 collective-permute-done.7.refs_1_
  36.0 0.0 collective-permute-done.8.refs_2_
  36.0 0.0 collective-permute-done.9.refs_3_
  36.1 0.1 shard_map.134
  36.1 0.1 collective-permute-start.10
  36.2 1.3 %shard_map.135.more_ref = f32[2,64,1280]{2,1,0:T(8,128)S(1)} custom-call(f32[2,80,1536]{2,1,0:T(8,128)S(1)} %get-tuple-element.61.f2s_ref, f32[2,80,2048]{2,1,0:T(8,128)S(1)} %get-tuple-element.63.f2_ref, f32[2,80,512]{2,1,0:T(8,128)S(1)} %get-tuple-element.64.f2e_ref, f32[2,64,4096]{2,1,0:T(8,128)S(1)} %get-tuple-element.41.src_ref, ...), custom_call_target="tpu_custom_call" | custom-call | flops 629145600 | tf_op jit(solution)/shard_map/pallas_call | solution.py:24
  37.5 0.0 collective-permute-done.10.theirs_ref
  37.6 1.4 %shard_map.136 = (f32[2,64,4096]{2,1,0:T(8,128)}, f32[2,64,128]{2,1,0:T(8,128)}) custom-call(f32[2,64,4096]{2,1,0:T(8,128)} %get-tuple-element.62._, f32[2,80,2048]{2,1,0:T(8,128)S(1)} %get-tuple-element.63.f2_ref, f32[2,80,512]{2,1,0:T(8,128)S(1)} %get-tuple-element.64.f2e_ref, ...), custom_call_target="tpu_custom_call", output_to_operand_aliasing={{0}: (0, {})} | custom-call | flops 125829120 | tf_op jit(solution)/shard_map/pallas_call | solution.py:24
  (5 shorter events, 0.1 us)
Async XLA Ops:
  0.6 0.8 %copy-start.3 = (f32[1,2,64,128]{3,2,1,0:T(8,128)S(1)}, f32[1,2,64,128]{3,2,1,0:T(8,128)}, u32[]{:S(2)}) copy-start(f32[1,2,64,128]{3,2,1,0:T(8,128)} %param.15) | copy-start | bytes 196612
  1.5 4.6 %copy-start = (f32[1,2,64,4096]{3,2,1,0:T(8,128)S(1)}, f32[1,2,64,4096]{3,2,1,0:T(8,128)}, u32[]{:S(2)}) copy-start(f32[1,2,64,4096]{3,2,1,0:T(8,128)} %param.12) | copy-start | bytes 6291460
  1.5 4.6 %copy-start.1 = (f32[1,2,64,4096]{3,2,1,0:T(8,128)S(1)}, f32[1,2,64,4096]{3,2,1,0:T(8,128)}, u32[]{:S(2)}) copy-start(f32[1,2,64,4096]{3,2,1,0:T(8,128)} %param.13) | copy-start | bytes 6291460
  1.5 4.6 %copy-start.2 = (f32[1,2,64,4096]{3,2,1,0:T(8,128)S(1)}, f32[1,2,64,4096]{3,2,1,0:T(8,128)}, u32[]{:S(2)}) copy-start(f32[1,2,64,4096]{3,2,1,0:T(8,128)} %param.11) | copy-start | bytes 6291460
  1.5 4.6 %copy-start.8 = (s32[8,8]{1,0:T(8,128)S(1)}, s32[8,8]{1,0:T(8,128)}, u32[]{:S(2)}) copy-start(s32[8,8]{1,0:T(8,128)} %peer_ref.1) | copy-start | bytes 772
  1.5 4.6 %copy-start.9 = (s32[8,8]{1,0:T(8,128)S(1)}, s32[8,8]{1,0:T(8,128)}, u32[]{:S(2)}) copy-start(s32[8,8]{1,0:T(8,128)} %len_ref.1) | copy-start | bytes 772
  1.5 4.6 %copy-start.10 = (s32[8]{0:T(128)S(1)}, s32[8]{0:T(128)}, u32[]{:S(2)}) copy-start(s32[8]{0:T(128)} %active_ref.1) | copy-start | bytes 100
  1.5 8.4 %slice-start = ((s8[16777216]{0:T(1024)(128)(4,1)}), s8[4194304]{0:T(1024)(128)(4,1)S(1)}, s32[]{:S(2)}) async-start(s8[16777216]{0:T(1024)(128)(4,1)} %bitcast.13), calls=%async_computation | async-start | bytes 8388608
  1.5 8.4 %slice-start.1 = ((s8[16777216]{0:T(1024)(128)(4,1)}), s8[4194304]{0:T(1024)(128)(4,1)S(1)}, s32[]{:S(2)}) async-start(s8[16777216]{0:T(1024)(128)(4,1)} %bitcast.13), calls=%async_computation.1 | async-start | bytes 8388608
  1.6 8.2 %collective-permute-start.2 = (f32[2,8,128]{2,1,0:T(8,128)S(1)}, f32[2,8,128]{2,1,0:T(8,128)S(1)}, u32[]{:S(2)}, u32[]{:S(2)}) collective-permute-start(f32[2,8,128]{2,1,0:T(8,128)S(1)} %get-tuple-element.37._), channel_id=1, source_target_pairs={{0,1},{1,0},{2,3},{3,2},{4,5},{5,4},{6,7},{7,6},{8,9},{9,8},{10,11... | collective-permute-start | bytes 24584 | tf_op jit(solution)/shard_map/ppermute | solution.py:180
  4.6 5.2 %collective-permute-start.3 = (f32[2,8,128]{2,1,0:T(8,128)S(1)}, f32[2,8,128]{2,1,0:T(8,128)S(1)}, u32[]{:S(2)}, u32[]{:S(2)}) collective-permute-start(f32[2,8,128]{2,1,0:T(8,128)S(1)} %get-tuple-element.40), channel_id=1, source_target_pairs={{0,3},{1,2},{2,1},{3,0},{4,7},{5,6},{6,5},{7,4},{8,11},{9,10},{10,... | collective-permute-start | bytes 24584 | tf_op jit(solution)/shard_map/ppermute | solution.py:180
  6.1 3.7 %copy-start.4 = (f32[1,2,64,128]{3,2,1,0:T(8,128)S(1)}, f32[1,2,64,128]{3,2,1,0:T(8,128)}, u32[]{:S(2)}) copy-start(f32[1,2,64,128]{3,2,1,0:T(8,128)} %param.15) | copy-start | bytes 196612
  6.1 3.8 %slice-start.2 = ((s8[16777216]{0:T(1024)(128)(4,1)}), s8[4194304]{0:T(1024)(128)(4,1)S(1)}, s32[]{:S(2)}) async-start(s8[16777216]{0:T(1024)(128)(4,1)} %bitcast.13), calls=%async_computation.2 | async-start | bytes 8388608
  6.1 3.8 %slice-start.3 = ((s8[16777216]{0:T(1024)(128)(4,1)}), s8[4194304]{0:T(1024)(128)(4,1)S(1)}, s32[]{:S(2)}) async-start(s8[16777216]{0:T(1024)(128)(4,1)} %bitcast.13), calls=%async_computation.3 | async-start | bytes 8388608
  7.0 13.9 %collective-permute-start = (f32[2,8,3584]{2,1,0:T(8,128)S(1)}, f32[2,8,3584]{2,1,0:T(8,128)S(1)}, u32[]{:S(2)}, u32[]{:S(2)}) collective-permute-start(f32[2,8,3584]{2,1,0:T(8,128)S(1)} %get-tuple-element.38._), channel_id=1, source_target_pairs={{0,1},{1,0},{2,3},{3,2},{4,5},{5,4},{6,7},{7,6},{8,9},{9,8},{10,11... | collective-permute-start | bytes 688136 | tf_op jit(solution)/shard_map/ppermute | solution.py:180
  8.6 12.3 %collective-permute-start.1 = (f32[2,8,3584]{2,1,0:T(8,128)S(1)}, f32[2,8,3584]{2,1,0:T(8,128)S(1)}, u32[]{:S(2)}, u32[]{:S(2)}) collective-permute-start(f32[2,8,3584]{2,1,0:T(8,128)S(1)} %get-tuple-element.39), channel_id=1, source_target_pairs={{0,3},{1,2},{2,1},{3,0},{4,7},{5,6},{6,5},{7,4},{8,11},{9,10},{10,... | collective-permute-start | bytes 688136 | tf_op jit(solution)/shard_map/ppermute | solution.py:180
  9.8 1.3 %collective-permute-start.4 = (f32[2,72,128]{2,1,0:T(8,128)S(1)}, f32[2,72,128]{2,1,0:T(8,128)S(1)}, u32[]{:S(2)}, u32[]{:S(2)}) collective-permute-start(f32[2,72,128]{2,1,0:T(8,128)S(1)} %shard_map.124.mult_ref.refs_1_.own_ref), channel_id=1, source_target_pairs={{0,4},{4,0},{8,12},{12,8},{16,20},{20,16},{24,28},{28,24},{1,5},{5... | collective-permute-start | bytes 221192 | tf_op jit(solution)/shard_map/ppermute | solution.py:189
  10.0 3.8 %copy-start.5 = (f32[1,2,16]{2,1,0:T(2,128)S(1)}, f32[1,2,16]{2,1,0:T(2,128)}, u32[]{:S(2)}) copy-start(f32[1,2,16]{2,1,0:T(2,128)} %pcur_ref.1) | copy-start | bytes 388
  10.0 3.8 %copy-start.6 = (s32[1,16]{1,0:T(1,128)S(1)}, s32[1,16]{1,0:T(1,128)}, u32[]{:S(2)}) copy-start(s32[1,16]{1,0:T(1,128)} %prow_ref.1) | copy-start | bytes 196
  10.0 3.8 %copy-start.7 = (s32[1,16]{1,0:T(1,128)S(1)}, s32[1,16]{1,0:T(1,128)}, u32[]{:S(2)}) copy-start(s32[1,16]{1,0:T(1,128)} %pcol_ref.1) | copy-start | bytes 196
  11.2 7.1 %collective-permute-start.5 = (f32[2,2,72,128]{3,2,1,0:T(8,128)S(1)}, f32[2,2,72,128]{3,2,1,0:T(8,128)S(1)}, u32[]{:S(2)}, u32[]{:S(2)}) collective-permute-start(f32[2,2,72,128]{3,2,1,0:T(8,128)S(1)} %get-tuple-element.57), channel_id=1, source_target_pairs={{0,8},{4,12},{8,0},{12,4},{16,24},{20,28},{24,16},{28,20},{1,9},{5... | collective-permute-start | bytes 442376 | tf_op jit(solution)/shard_map/ppermute | solution.py:213
  18.3 6.3 %collective-permute-start.6 = (f32[1,2,72,128]{3,2,1,0:T(8,128)S(1)}, f32[1,2,72,128]{3,2,1,0:T(8,128)S(1)}, u32[]{:S(2)}, u32[]{:S(2)}) collective-permute-start(f32[1,2,72,128]{3,2,1,0:T(8,128)S(1)} %get-tuple-element.60), channel_id=1, source_target_pairs={{0,16},{4,20},{8,24},{12,28},{16,0},{20,4},{24,8},{28,12},{1,17},{... | collective-permute-start | bytes 221192 | tf_op jit(solution)/shard_map/ppermute | solution.py:213
  27.1 9.0 %collective-permute-start.7 = (f32[2,64,128]{2,1,0:T(8,128)S(1)}, f32[2,64,128]{2,1,0:T(8,128)S(1)}, u32[]{:S(2)}, u32[]{:S(2)}) collective-permute-start(f32[2,64,128]{2,1,0:T(8,128)S(1)} %get-tuple-element.66.refs_0_), channel_id=1, source_target_pairs={{0,8},{4,12},{8,16},{12,20},{16,24},{20,28},{24,0},{28,4},{1,9},{5... | collective-permute-start | bytes 196616 | tf_op jit(solution)/shard_map/ppermute | solution.py:185
  28.2 7.8 %collective-permute-start.8 = (f32[2,64,128]{2,1,0:T(8,128)S(1)}, f32[2,64,128]{2,1,0:T(8,128)S(1)}, u32[]{:S(2)}, u32[]{:S(2)}) collective-permute-start(f32[2,64,128]{2,1,0:T(8,128)S(1)} %get-tuple-element.66.refs_0_), channel_id=1, source_target_pairs={{0,16},{4,20},{8,24},{12,28},{16,0},{20,4},{24,8},{28,12},{1,17},{... | collective-permute-start | bytes 196616 | tf_op jit(solution)/shard_map/ppermute | solution.py:185
  30.6 5.4 %collective-permute-start.9 = (f32[2,64,128]{2,1,0:T(8,128)S(1)}, f32[2,64,128]{2,1,0:T(8,128)S(1)}, u32[]{:S(2)}, u32[]{:S(2)}) collective-permute-start(f32[2,64,128]{2,1,0:T(8,128)S(1)} %get-tuple-element.66.refs_0_), channel_id=1, source_target_pairs={{0,24},{4,28},{8,0},{12,4},{16,8},{20,12},{24,16},{28,20},{1,25},{... | collective-permute-start | bytes 196616 | tf_op jit(solution)/shard_map/ppermute | solution.py:185
  36.1 1.4 %collective-permute-start.10 = (f32[2,64,128]{2,1,0:T(8,128)S(1)}, f32[2,64,128]{2,1,0:T(8,128)S(1)}, u32[]{:S(2)}, u32[]{:S(2)}) collective-permute-start(f32[2,64,128]{2,1,0:T(8,128)S(1)} %get-tuple-element.69), channel_id=1, source_target_pairs={{0,4},{4,0},{8,12},{12,8},{16,20},{20,16},{24,28},{28,24},{1,5},{5... | collective-permute-start | bytes 196616 | tf_op jit(solution)/shard_map/ppermute | solution.py:189
